TPU v7x, 32 devices: a whole 2x2x4 slice. The times are simulated.
32 devices in a mesh: dp: 8 (over z, x), dap: 4 (over y, core).
Axes of the slice: x: 2, y: 2, z: 4, core: 2. Of those that a mesh axis runs over, the one named last changes fastest.
Arguments:
- pair: bfloat16 [8, 64, 64, 128], P('dp', 'dap'), may hold values from -6 to 6
- pair_grad: bfloat16 [8, 64, 64, 128], P('dp', 'dap'), may hold values from -6 to 6
- token_mask: int32 [8, 64], P('dp'), may hold values from 0 to 1, as said below
- w_edges: bfloat16 [128, 512], replicated, may hold values from -0.5 to 0.5
- w_gate: bfloat16 [128, 128], replicated, may hold values from -0.5 to 0.5
- w_out: bfloat16 [128, 128], replicated, may hold values from -0.5 to 0.5
- in_gain: float32 [128], replicated, may hold values from 0.5 to 1.5
- in_bias: float32 [128], replicated, may hold values from -1.5 to 1.5
- output_norm_gain: float32 [128], replicated, may hold values from 0.5 to 1.5
- output_norm_bias: float32 [128], replicated, may hold values from -1.5 to 1.5
Outputs:
- pair_input_grad: bfloat16 [8, 64, 64, 128], P('dp', 'dap')
- grad_edges: float32 [128, 512], replicated
- grad_gate: float32 [128, 128], replicated
- grad_out: float32 [128, 128], replicated
- grad_in_norm: float32 [2, 128], replicated
- output_norm_param_grads: float32 [2, 128], replicated
Inputs may be any that keep to these rules, and one draw needn't show every extreme that they name: `token_mask`: each structure's valid tokens are its first L tokens with L between 32 and 64; structure 0 has all 64 valid.
All inputs are finite; a program needn't handle non-finite values.
Results may differ from a plain program's by a relative error of at most 0.0093.
Values may be sent and summed in bfloat16 or wider, within the bound.
No kernel may reach another device: no remote copies, remote signals or barrier semaphores. Data moves between devices by JAX's collectives and lax.ppermute only.
A program may use at most 64 MiB of HBM per device.

v0:
```python
import jax
import jax.numpy as jnp
from jax import lax
from jax.sharding import PartitionSpec as P

EPS = 1e-05


def apply_layer_norm(values, reduce_dimension):
    mean = jnp.mean(values, axis=reduce_dimension, keepdims=True)
    var = jnp.mean((values - mean) ** 2, axis=reduce_dimension, keepdims=True)
    rstd = lax.rsqrt(var + EPS)
    return ((values - mean) * rstd, rstd)


def layer_norm_backward(dnorm, gain, normed, rstd, reduce_dimension):
    scaled = dnorm * gain
    return (
        scaled
        - jnp.mean(scaled, axis=reduce_dimension, keepdims=True)
        - normed * jnp.mean(scaled * normed, axis=reduce_dimension, keepdims=True)
    ) * rstd


def per_device(
    pair,
    pair_grad,
    token_mask,
    w_edges,
    w_gate,
    w_out,
    in_gain,
    in_bias,
    output_norm_gain,
    output_norm_bias,
):
    z_rows = pair[0]
    dout = pair_grad[0]
    rows = z_rows.shape[0]
    hidden = w_out.shape[0]
    width = w_gate.shape[0]
    first = lax.axis_index("dap") * rows
    mask_full = token_mask[0].astype(jnp.float32)
    mask_rows = lax.dynamic_slice_in_dim(mask_full, first, rows, 0)
    edge_mask = mask_rows[:, None, None] * mask_full[None, None, :]
    zhat, rstd_in = apply_layer_norm(z_rows.astype(jnp.float32), 2)
    zn = (zhat * in_gain + in_bias).astype(jnp.bfloat16)

    def project(columns):
        return jnp.einsum("ikc,ch->ihk", zn, columns, preferred_element_type=jnp.float32)

    def edge_values(pre):
        return (edge_mask * jax.nn.sigmoid(pre[:, :hidden]) * pre[:, hidden:]).astype(jnp.bfloat16)

    pre_left = project(w_edges[:, : 2 * hidden])
    pre_right = project(w_edges[:, 2 * hidden :])
    left_ch, right_ch = (
        lax.all_to_all(edge_values(pre_left), "dap", split_axis=1, concat_axis=0, tiled=True),
        lax.all_to_all(edge_values(pre_right), "dap", split_axis=1, concat_axis=0, tiled=True),
    )
    tri = jnp.einsum("ihk,jhk->ihj", left_ch, right_ch, preferred_element_type=jnp.float32).astype(
        jnp.bfloat16
    )
    triangle_product = lax.all_to_all(tri, "dap", split_axis=0, concat_axis=1, tiled=True)
    centered_scaled_input, output_inverse_deviation = apply_layer_norm(
        triangle_product.astype(jnp.float32), 1
    )
    normalized_product = (
        centered_scaled_input * output_norm_gain[None, :, None] + output_norm_bias[None, :, None]
    ).astype(jnp.bfloat16)
    gate = jax.nn.sigmoid(jnp.einsum("ijc,cd->ijd", zn, w_gate, preferred_element_type=jnp.float32))
    y_out = jnp.einsum("ihj,hc->ijc", normalized_product, w_out, preferred_element_type=jnp.float32)
    doutf = dout.astype(jnp.float32)
    dy = (doutf * gate).astype(jnp.bfloat16)
    dgl = (doutf * y_out * gate * (1.0 - gate)).astype(jnp.bfloat16)
    grad_out = jnp.einsum("ihj,ijc->hc", normalized_product, dy, preferred_element_type=jnp.float32)
    normalized_gradient = jnp.einsum("ijc,hc->ihj", dy, w_out, preferred_element_type=jnp.float32)
    output_norm_backward = jnp.stack(
        [
            jnp.sum(normalized_gradient * centered_scaled_input, axis=(0, 2)),
            jnp.sum(normalized_gradient, axis=(0, 2)),
        ]
    )
    product_gradient = layer_norm_backward(
        normalized_gradient,
        output_norm_gain[None, :, None],
        centered_scaled_input,
        output_inverse_deviation,
        1,
    ).astype(jnp.bfloat16)
    dprod_ch = lax.all_to_all(product_gradient, "dap", split_axis=1, concat_axis=0, tiled=True)
    dleft_ch = jnp.einsum(
        "ihj,jhk->ihk", dprod_ch, right_ch, preferred_element_type=jnp.float32
    ).astype(jnp.bfloat16)
    dright_ch = jnp.einsum(
        "ihj,ihk->jhk", dprod_ch, left_ch, preferred_element_type=jnp.float32
    ).astype(jnp.bfloat16)
    dleft, dright = (
        lax.all_to_all(dleft_ch, "dap", split_axis=0, concat_axis=1, tiled=True),
        lax.all_to_all(dright_ch, "dap", split_axis=0, concat_axis=1, tiled=True),
    )

    def pre_grad(dvalues, pre):
        sig = jax.nn.sigmoid(pre[:, :hidden])
        masked = dvalues.astype(jnp.float32) * edge_mask
        return jnp.concatenate(
            [masked * pre[:, hidden:] * sig * (1.0 - sig), masked * sig], axis=1
        ).astype(jnp.bfloat16)

    dpre_left = pre_grad(dleft, pre_left)
    dpre_right = pre_grad(dright, pre_right)
    grad_edges = jnp.concatenate(
        [
            jnp.einsum("ikc,ihk->ch", zn, dpre_left, preferred_element_type=jnp.float32),
            jnp.einsum("ikc,ihk->ch", zn, dpre_right, preferred_element_type=jnp.float32),
        ],
        axis=1,
    )
    grad_gate = jnp.einsum("ijc,ijd->cd", zn, dgl, preferred_element_type=jnp.float32)
    dzn = jnp.einsum(
        "ihk,ch->ikc", dpre_left, w_edges[:, : 2 * hidden], preferred_element_type=jnp.float32
    )
    dzn = dzn + jnp.einsum(
        "ihk,ch->ikc", dpre_right, w_edges[:, 2 * hidden :], preferred_element_type=jnp.float32
    )
    dzn = dzn + jnp.einsum("ijd,cd->ijc", dgl, w_gate, preferred_element_type=jnp.float32)
    in_norm_grad = jnp.stack([jnp.sum(dzn * zhat, axis=(0, 1)), jnp.sum(dzn, axis=(0, 1))])
    dz = layer_norm_backward(dzn, in_gain, zhat, rstd_in, 2).astype(jnp.bfloat16)
    flat = jnp.concatenate(
        [
            grad_edges.ravel(),
            grad_gate.ravel(),
            grad_out.ravel(),
            in_norm_grad.ravel(),
            output_norm_backward.ravel(),
        ]
    )
    summed = lax.psum(flat, ("dp", "dap"))
    edge_size = width * 4 * hidden
    gate_size = width * width
    out_size = hidden * width
    offset = 0
    total_edges = summed[offset : offset + edge_size].reshape(width, 4 * hidden)
    offset = offset + edge_size
    total_gate = summed[offset : offset + gate_size].reshape(width, width)
    offset = offset + gate_size
    total_out = summed[offset : offset + out_size].reshape(hidden, width)
    offset = offset + out_size
    total_in_norm = summed[offset : offset + 2 * width].reshape(2, width)
    offset = offset + 2 * width
    total_out_norm = summed[offset : offset + 2 * hidden].reshape(2, hidden)
    return (dz[None], total_edges, total_gate, total_out, total_in_norm, total_out_norm)


def solution(mesh):
    in_specs = (
        P("dp", "dap", None, None),
        P("dp", "dap", None, None),
        P("dp", None),
        P(),
        P(),
        P(),
        P(),
        P(),
        P(),
        P(),
    )
    out_specs = (P("dp", "dap", None, None), P(), P(), P(), P(), P())
    return jax.shard_map(
        per_device, mesh=mesh, in_specs=in_specs, out_specs=out_specs, check_vma=False
    )
```

profile of v0, /device:TPU:0, one launch (start us, length us, event | category | flops | bytes accessed | tf_op | source)
XLA Modules:
  0.0 256.7 jit_solution(17805429430126701833)
XLA Ops:
  7.2 1.2 convert_reduce_fusion
  12.1 1.1 reshape.192
  13.2 4.2 %all-to-all-start.1 = ((bf16[4,2,16384]{2,1,0:T(2,128)(2,1)}), bf16[4,2,16384]{2,1,0:T(2,128)(2,1)S(1)}, u32[]{:S(2)}, u32[]{:S(2)}) async-start(bf16[4,2,16384]{2,1,0:T(2,128)(2,1)} %reshape.192), calls=%async_computation.1 | async-start | bytes 524288 | tf_op jit(solution)/shard_map/all_to_all | solution.py:58
  17.8 1.1 reshape.190
  18.9 4.5 %all-to-all-done.1 = bf16[4,2,16384]{2,1,0:T(2,128)(2,1)S(1)} async-done(((bf16[4,2,16384]{2,1,0:T(2,128)(2,1)}), bf16[4,2,16384]{2,1,0:T(2,128)(2,1)S(1)}, u32[]{:S(2)}, u32[]{:S(2)}) %all-to-all-start.1) | async-done | bytes 262176 | tf_op jit(solution)/shard_map/all_to_all | solution.py:58
  24.1 4.0 %all-to-all-start = ((bf16[4,2,16384]{2,1,0:T(2,128)(2,1)}), bf16[4,2,16384]{2,1,0:T(2,128)(2,1)}, u32[]{:S(2)}, u32[]{:S(2)}) async-start(bf16[4,2,16384]{2,1,0:T(2,128)(2,1)} %reshape.190), calls=%async_computation | async-start | bytes 524288 | tf_op jit(solution)/shard_map/all_to_all | solution.py:59
  28.2 1.3 reshape.193
  29.6 4.7 %all-to-all-done = bf16[4,2,16384]{2,1,0:T(2,128)(2,1)} async-done(((bf16[4,2,16384]{2,1,0:T(2,128)(2,1)}), bf16[4,2,16384]{2,1,0:T(2,128)(2,1)}, u32[]{:S(2)}, u32[]{:S(2)}) %all-to-all-start) | async-done | bytes 262176 | tf_op jit(solution)/shard_map/all_to_all | solution.py:59
  34.3 2.1 reshape.191
  36.4 1.1 copy.43
  37.5 1.2 fusion.5
  38.7 1.8 copy.47
  40.5 1.1 reshape.194
  41.6 4.1 %all-to-all-start.2 = ((bf16[4,2,16384]{2,1,0:T(2,128)(2,1)}), bf16[4,2,16384]{2,1,0:T(2,128)(2,1)}, u32[]{:S(2)}, u32[]{:S(2)}) async-start(bf16[4,2,16384]{2,1,0:T(2,128)(2,1)} %reshape.194), calls=%async_computation.2 | async-start | bytes 524288 | tf_op jit(solution)/shard_map/all_to_all | solution.py:64
  45.7 1.3 fusion.4
  47.0 4.8 %all-to-all-done.2 = bf16[4,2,16384]{2,1,0:T(2,128)(2,1)} async-done(((bf16[4,2,16384]{2,1,0:T(2,128)(2,1)}), bf16[4,2,16384]{2,1,0:T(2,128)(2,1)}, u32[]{:S(2)}, u32[]{:S(2)}) %all-to-all-start.2) | async-done | bytes 262176 | tf_op jit(solution)/shard_map/all_to_all | solution.py:64
  51.8 1.3 reshape.195
  53.6 1.1 copy.48
  54.7 1.5 copy.49
  56.2 2.3 fusion.34
  58.5 1.2 reduce_sum.119
  59.7 2.4 multiply_convert_fusion.4
  62.0 2.1 copy.50
  64.2 2.1 reshape.196
  66.3 4.2 %all-to-all-start.3 = ((bf16[4,2,16384]{2,1,0:T(2,128)(2,1)}), bf16[4,2,16384]{2,1,0:T(2,128)(2,1)}, u32[]{:S(2)}, u32[]{:S(2)}) async-start(bf16[4,2,16384]{2,1,0:T(2,128)(2,1)} %reshape.196), calls=%async_computation.3 | async-start | bytes 524288 | tf_op jit(solution)/shard_map/all_to_all | solution.py:91
  70.5 2.3 fusion.10
  72.8 3.8 %all-to-all-done.3 = bf16[4,2,16384]{2,1,0:T(2,128)(2,1)} async-done(((bf16[4,2,16384]{2,1,0:T(2,128)(2,1)}), bf16[4,2,16384]{2,1,0:T(2,128)(2,1)}, u32[]{:S(2)}, u32[]{:S(2)}) %all-to-all-start.3) | async-done | bytes 262176 | tf_op jit(solution)/shard_map/all_to_all | solution.py:91
  76.6 2.1 reshape.197
  78.7 1.2 copy.52
  80.7 1.1 fusion.7
  81.8 2.5 copy.58
  84.4 2.1 reshape.200
  86.5 4.2 %all-to-all-start.5 = ((bf16[4,2,16384]{2,1,0:T(2,128)(2,1)}), bf16[4,2,16384]{2,1,0:T(2,128)(2,1)}, u32[]{:S(2)}, u32[]{:S(2)}) async-start(bf16[4,2,16384]{2,1,0:T(2,128)(2,1)} %reshape.200), calls=%async_computation.5 | async-start | bytes 524288 | tf_op jit(solution)/shard_map/all_to_all | solution.py:100
  90.8 2.3 fusion.6
  93.1 1.8 copy.54
  94.9 1.1 reshape.198
  96.9 4.0 %all-to-all-start.4 = ((bf16[4,2,16384]{2,1,0:T(2,128)(2,1)}), bf16[4,2,16384]{2,1,0:T(2,128)(2,1)}, u32[]{:S(2)}, u32[]{:S(2)}) async-start(bf16[4,2,16384]{2,1,0:T(2,128)(2,1)} %reshape.198), calls=%async_computation.4 | async-start | bytes 524288 | tf_op jit(solution)/shard_map/all_to_all | solution.py:99
  101.0 1.3 reshape.201
  102.4 1.1 copy.59
  103.5 2.3 copy.60
  105.8 1.2 all-to-all-done.4
  107.0 1.3 reshape.199
  108.5 1.1 copy.55
  109.5 2.4 copy.56
  112.0 1.5 multiply_convert_fusion.1
  119.9 1.3 fusion.37
  121.2 125.7 %all-reduce.2.cloned.1.call-done = f32[98816]{0:T(1024)} async-done(((f32[98816]{0:T(1024)}), f32[98816]{0:T(1024)}) %all-reduce.2.cloned.1.call-update) | async-done | bytes 395280 | tf_op jit(solution)/shard_map/psum | solution.py:138
  246.9 0.9 slice-done
  (81 shorter events, 15.4 us)
Async XLA Ops:
  7.2 38.5 %copy-start = (bf16[128,128]{1,0:T(8,128)(2,1)S(1)}, bf16[128,128]{1,0:T(8,128)(2,1)}, u32[]{:S(2)}) copy-start(bf16[128,128]{1,0:T(8,128)(2,1)} %param.14) | copy-start | bytes 98308
  7.2 1.2 copy-start.1
  8.4 0.9 copy-start.12
  8.8 0.7 copy-start.16
  8.9 0.7 copy-start.17
  10.5 0.7 copy-start.19
  13.2 10.3 %all-to-all-start.1 = ((bf16[4,2,16384]{2,1,0:T(2,128)(2,1)}), bf16[4,2,16384]{2,1,0:T(2,128)(2,1)S(1)}, u32[]{:S(2)}, u32[]{:S(2)}) async-start(bf16[4,2,16384]{2,1,0:T(2,128)(2,1)} %reshape.192), calls=%async_computation.1 | async-start | bytes 524288 | tf_op jit(solution)/shard_map/all_to_all | solution.py:58
  23.4 0.7 copy-start.9
  24.1 10.2 %all-to-all-start = ((bf16[4,2,16384]{2,1,0:T(2,128)(2,1)}), bf16[4,2,16384]{2,1,0:T(2,128)(2,1)}, u32[]{:S(2)}, u32[]{:S(2)}) async-start(bf16[4,2,16384]{2,1,0:T(2,128)(2,1)} %reshape.190), calls=%async_computation | async-start | bytes 524288 | tf_op jit(solution)/shard_map/all_to_all | solution.py:59
  29.6 7.9 %copy-start.2 = (bf16[4,16,32,64]{3,1,0,2:T(8,128)(2,1)}, bf16[4,16,32,64]{3,1,0,2:T(8,128)(2,1)S(1)}, u32[]{:S(2)}) copy-start(bf16[4,16,32,64]{3,1,0,2:T(8,128)(2,1)S(1)} %copy.46) | copy-start | bytes 786436
  41.6 10.2 %all-to-all-start.2 = ((bf16[4,2,16384]{2,1,0:T(2,128)(2,1)}), bf16[4,2,16384]{2,1,0:T(2,128)(2,1)}, u32[]{:S(2)}, u32[]{:S(2)}) async-start(bf16[4,2,16384]{2,1,0:T(2,128)(2,1)} %reshape.194), calls=%async_computation.2 | async-start | bytes 524288 | tf_op jit(solution)/shard_map/all_to_all | solution.py:64
  54.7 1.6 copy-start.14
  54.7 1.6 copy-start.15
  66.3 4.2 %copy-start.18 = (f32[128]{0:T(128)S(1)}, f32[128]{0:T(128)}, u32[]{:S(2)}) copy-start(f32[128]{0:T(128)} %param.19) | copy-start | bytes 1540
  66.3 10.3 %all-to-all-start.3 = ((bf16[4,2,16384]{2,1,0:T(2,128)(2,1)}), bf16[4,2,16384]{2,1,0:T(2,128)(2,1)}, u32[]{:S(2)}, u32[]{:S(2)}) async-start(bf16[4,2,16384]{2,1,0:T(2,128)(2,1)} %reshape.196), calls=%async_computation.3 | async-start | bytes 524288 | tf_op jit(solution)/shard_map/all_to_all | solution.py:91
  78.7 2.0 copy-start.3
  79.9 0.8 copy-start.4
  86.5 10.3 %all-to-all-start.5 = ((bf16[4,2,16384]{2,1,0:T(2,128)(2,1)}), bf16[4,2,16384]{2,1,0:T(2,128)(2,1)}, u32[]{:S(2)}, u32[]{:S(2)}) async-start(bf16[4,2,16384]{2,1,0:T(2,128)(2,1)} %reshape.200), calls=%async_computation.5 | async-start | bytes 524288 | tf_op jit(solution)/shard_map/all_to_all | solution.py:100
  96.9 10.2 %all-to-all-start.4 = ((bf16[4,2,16384]{2,1,0:T(2,128)(2,1)}), bf16[4,2,16384]{2,1,0:T(2,128)(2,1)}, u32[]{:S(2)}, u32[]{:S(2)}) async-start(bf16[4,2,16384]{2,1,0:T(2,128)(2,1)} %reshape.198), calls=%async_computation.4 | async-start | bytes 524288 | tf_op jit(solution)/shard_map/all_to_all | solution.py:99
  100.9 146.0 %all-reduce.2.cloned.1.call-start = ((), (), s32[]{:S(2)}) async-start(), calls=%async_computation.6 | async-start | bytes 794624 | tf_op jit(solution)/shard_map/psum | solution.py:138
  109.5 2.4 copy-start.7
  113.5 0.9 copy-start.13
  115.6 1.0 copy-start.11
  117.4 1.0 copy-start.5
  117.4 1.1 copy-start.6
  119.1 0.8 copy-start.8
  246.9 0.9 slice-start
  246.9 1.7 copy-start.10
Sparse Core Ops, SparseCore 0:
  120.0 126.8 all-reduce.1
where the time goes:
time: 259 us; the launch traced here: 257 us
  waiting for transfers between devices  146 us (56%)
  local copies, waits for them, and re-layouts  47.6 us (18%)
  starting transfers between devices  24.8 us (10%)
  matrix products  15 us (6%)
  between operations  14.5 us (6%)
  other arithmetic  9.16 us (4%)
    psum x1, waiting for transfers between devices, per_device(): summed = lax.psum(flat, ('dp', 'dap'))  126 us
    unnamed x54, local copies, waits for them, and re-layouts  23.7 us
    convert_element_type x4, local copies, waits for them, and re-layouts, pre_grad(): masked = dvalues.astype(jnp.float32) * edge_mask  6.89 us
  transfers between devices with their start and end apart: 7, of which 7 were waited for; matrix products, arithmetic and copies ran while one was open for 7% of the time, Pallas kernels for 0%

commit v1 on v0

--- a/solution.py
+++ b/solution.py
@@ -1,9 +1,16 @@
+import functools
+
 import jax
 import jax.numpy as jnp
 from jax import lax
+from jax.experimental import pallas as pl
+from jax.experimental.pallas import tpu as pltpu
 from jax.sharding import PartitionSpec as P
 
 EPS = 1e-05
+LANES = 128
+F32 = jnp.float32
+BF16 = jnp.bfloat16
 
 
 def apply_layer_norm(values, reduce_dimension):
@@ -22,7 +29,7 @@
     ) * rstd
 
 
-def per_device(
+def per_device_exchange(
     pair,
     pair_grad,
     token_mask,
@@ -152,6 +159,357 @@
     return (dz[None], total_edges, total_gate, total_out, total_in_norm, total_out_norm)
 
 
+def dot(a, b):
+    return jnp.dot(a, b, preferred_element_type=F32)
+
+
+def dot_nt(a, b):
+    return lax.dot_general(a, b, (((1,), (1,)), ((), ())), preferred_element_type=F32)
+
+
+def norm_columns(x):
+    mean = jnp.mean(x, axis=0, keepdims=True)
+    centred = x - mean
+    var = jnp.mean(centred * centred, axis=0, keepdims=True)
+    rstd = lax.rsqrt(var + EPS)
+    return centred * rstd, rstd
+
+
+def norm_columns_backward(dnorm, gain, normed, rstd):
+    scaled = dnorm * gain
+    m1 = jnp.mean(scaled, axis=0, keepdims=True)
+    m2 = jnp.mean(scaled * normed, axis=0, keepdims=True)
+    return (scaled - m1 - normed * m2) * rstd
+
+
+def block_diagonal(tiles, low):
+    turned = pltpu.roll(tiles, LANES // 2, 1)
+    zero = jnp.zeros((8, LANES), F32)
+    top, bottom = [], []
+    for a in range(tiles.shape[0] // 8):
+        x = tiles[8 * a : 8 * a + 8]
+        y = turned[8 * a : 8 * a + 8]
+        top += [jnp.where(low, x, zero), jnp.where(low, y, zero)]
+        bottom += [jnp.where(low, zero, y), jnp.where(low, zero, x)]
+    return jnp.concatenate(top + bottom, axis=0).astype(BF16)
+
+
+def fused_kernel(
+    n_blocks,
+    me_ref,
+    mask_ref,
+    *refs,
+):
+    pair_refs = refs[:n_blocks]
+    pg_ref = refs[n_blocks]
+    pgt_refs = refs[n_blocks + 1 : 2 * n_blocks + 1]
+    (
+        we_ref,
+        wg_ref,
+        wo_ref,
+        gain_ref,
+        bias_ref,
+        ogain_ref,
+        obias_ref,
+        dz_ref,
+        grads_ref,
+        weT,
+        wgT,
+        woT,
+        vec,
+        pm,
+        xall,
+        pgs,
+        ls,
+        rs,
+        pre_own,
+        zn_own,
+        zhat_own,
+        rstd_own,
+        bdl,
+        bdr,
+        pr,
+        dgl_own,
+        gacc,
+    ) = refs[2 * n_blocks + 1 :]
+    me = me_ref[0]
+    rows, tokens, width = pair_refs[0].shape
+    half = rows // 2
+    tiles = n_blocks * half
+    hidden = wo_ref.shape[0]
+    f = lambda v: v.astype(F32)
+
+    for b in range(4):
+        cols = slice(b * hidden, (b + 1) * hidden)
+        weT[cols, :] = f(we_ref[:, cols]).T.astype(BF16)
+    wgT[...] = f(wg_ref[...]).T.astype(BF16)
+    woT[...] = f(wo_ref[...]).T.astype(BF16)
+    for b, r in enumerate((gain_ref, bias_ref, ogain_ref, obias_ref)):
+        vec[b] = jnp.broadcast_to(r[...], (width, LANES)).T
+    low = lax.broadcasted_iota(jnp.int32, (8, LANES), 1) < LANES // 2
+    m = f(mask_ref[...])
+    m = jnp.broadcast_to(jnp.concatenate([m, m], axis=1), (LANES, LANES))
+    mt = m.T
+    for a in range(n_blocks):
+        lo = mt[rows * a : rows * a + half]
+        hi = mt[rows * a + half : rows * (a + 1)]
+        pm[half * a : half * (a + 1), :] = jnp.where(low, lo, hi) * m[:8]
+    gacc[...] = jnp.zeros_like(gacc)
+
+    for s in range(n_blocks):
+        a = jnp.bitwise_xor(me, s)
+
+        @pl.loop(0, half)
+        def _(t, s=s, a=a):
+            lo = f(pair_refs[s][t])
+            hi = f(pair_refs[s][t + half])
+            at = pl.multiple_of((a * rows + t) * tokens, tokens)
+            xall[pl.ds(at, tokens), :] = lo
+            xall[pl.ds(at + half * tokens, tokens), :] = hi
+            zhat, rstd = norm_columns(jnp.concatenate([lo, hi], axis=0).T)
+            zn = (zhat * vec[0] + vec[1]).astype(BF16)
+            pre = dot(weT[...], zn)
+            mask = pm[pl.ds(a * half + t, 1), :]
+            left = mask * jax.nn.sigmoid(pre[:hidden]) * pre[hidden : 2 * hidden]
+            right = mask * jax.nn.sigmoid(pre[2 * hidden : 3 * hidden]) * pre[3 * hidden :]
+            ls[pl.ds(a * half + t, hidden, stride=tiles), :] = left
+            rs[pl.ds(a * half + t, hidden, stride=tiles), :] = right
+            if s == 0:
+                pre_own[t] = pre
+                zn_own[t] = zn
+                zhat_own[t] = zhat
+                rstd_own[t] = rstd
+
+        pgs[pl.ds(pl.multiple_of(a * rows * rows, rows), rows * rows), :] = f(
+            pgt_refs[s][...].reshape(rows * rows, width)
+        )
+
+    @pl.loop(0, hidden, unroll=4)
+    def _(h):
+        at = pl.multiple_of(h * tiles, tiles)
+        own = pl.multiple_of(h * tiles + me * half, half)
+        right = block_diagonal(rs[pl.ds(at, tiles), :], low)
+        left = block_diagonal(ls[pl.ds(at, tiles), :], low)
+        bdr[h] = right
+        bdl[h] = left
+        out = pl.multiple_of(h * half, half)
+        pr[0, pl.ds(out, half), :] = dot_nt(ls[pl.ds(own, half), :].astype(BF16), right)
+        pr[1, pl.ds(out, half), :] = dot_nt(rs[pl.ds(own, half), :].astype(BF16), left)
+
+    @pl.loop(0, half)
+    def _(t):
+        for own in (True, False):
+            which = 0 if own else 1
+            prod = pr[which, pl.ds(t, hidden, stride=half), :].astype(BF16).astype(F32)
+            xhat, rstd = norm_columns(prod)
+            if own:
+                zn = zn_own[t]
+                pg = jnp.concatenate([f(pg_ref[t]), f(pg_ref[t + half])], axis=0).T
+            else:
+                j = me * rows + t
+                x = jnp.concatenate(
+                    [
+                        xall[pl.ds(j, tokens, stride=tokens), :],
+                        xall[pl.ds(j + half, tokens, stride=tokens), :],
+                    ],
+                    axis=0,
+                ).T
+                zhat, _ = norm_columns(x)
+                zn = (zhat * vec[0] + vec[1]).astype(BF16)
+                pg = jnp.concatenate(
+                    [
+                        pgs[pl.ds(t, tokens, stride=rows), :],
+                        pgs[pl.ds(t + half, tokens, stride=rows), :],
+                    ],
+                    axis=0,
+                ).T
+            gate = jax.nn.sigmoid(dot(wgT[...], zn))
+            dy = (pg * gate).astype(BF16)
+            dxn = dot(wo_ref[...], dy)
+            if own:
+                xn = (xhat * vec[2] + vec[3]).astype(BF16)
+                y = dot(woT[...], xn)
+                dgl = (pg * y * gate * (1.0 - gate)).astype(BF16)
+                dgl_own[t] = dgl
+                gacc[4] += dot_nt(zn, dgl)
+                gacc[5] += dot_nt(xn, dy)
+                gacc[6] += dxn * xhat
+                gacc[7] += dxn
+            pr[which, pl.ds(t, hidden, stride=half), :] = norm_columns_backward(
+                dxn, vec[2], xhat, rstd
+            )
+
+    @pl.loop(0, hidden, unroll=4)
+    def _(h):
+        at = pl.multiple_of(h * half, half)
+        pr[0, pl.ds(at, half), :] = dot(pr[0, pl.ds(at, half), :].astype(BF16), bdr[h])
+        pr[1, pl.ds(at, half), :] = dot(pr[1, pl.ds(at, half), :].astype(BF16), bdl[h])
+
+    @pl.loop(0, half)
+    def _(t):
+        mask = pm[pl.ds(me * half + t, 1), :]
+        zn = zn_own[t]
+        zhat = zhat_own[t]
+        dzn = dot(wg_ref[...], dgl_own[t])
+        for which in range(2):
+            d = pr[which, pl.ds(t, hidden, stride=half), :].astype(BF16).astype(F32) * mask
+            sig = jax.nn.sigmoid(pre_own[t, pl.ds(2 * which * hidden, hidden), :])
+            val = pre_own[t, pl.ds((2 * which + 1) * hidden, hidden), :]
+            dval = d * sig
+            dgate = (dval * val * (1.0 - sig)).astype(BF16)
+            dval = dval.astype(BF16)
+            gacc[2 * which] += dot_nt(zn, dgate)
+            gacc[2 * which + 1] += dot_nt(zn, dval)
+            dzn += dot(we_ref[:, 2 * which * hidden : (2 * which + 1) * hidden], dgate)
+            dzn += dot(we_ref[:, (2 * which + 1) * hidden : (2 * which + 2) * hidden], dval)
+        gacc[8] += dzn * zhat
+        gacc[9] += dzn
+        dz = norm_columns_backward(dzn, vec[0], zhat, rstd_own[t]).T.astype(BF16)
+        dz_ref[t] = dz[:tokens]
+        dz_ref[t + half] = dz[tokens:]
+
+    for b in range(6):
+        grads_ref[b * LANES : (b + 1) * LANES, :] = gacc[b].astype(BF16)
+    sums = [jnp.sum(gacc[b].T, axis=0, keepdims=True) for b in (8, 9, 6, 7)]
+    pad = grads_ref.shape[0] - 6 * LANES
+    sums.append(jnp.zeros((pad - 4, LANES), F32))
+    grads_ref[6 * LANES :, :] = jnp.concatenate(sums, axis=0).astype(BF16)
+
+
+def pick(x, i):
+    return lax.dynamic_index_in_dim(x, i, 0, keepdims=False)
+
+
+def swap(x, axis, n, bit):
+    return lax.ppermute(x, axis, [(i, i ^ bit) for i in range(n)])
+
+
+def bits_of(n):
+    out = []
+    b = n // 2
+    while b:
+        out.append(b)
+        b //= 2
+    return out
+
+
+def per_device_fused(
+    n_dp,
+    n_dap,
+    pair,
+    pair_grad,
+    token_mask,
+    w_edges,
+    w_gate,
+    w_out,
+    in_gain,
+    in_bias,
+    output_norm_gain,
+    output_norm_bias,
+):
+    rows, tokens, width = pair.shape[1:]
+    hidden = w_out.shape[0]
+    me = lax.axis_index("dap")
+    x = pair[0]
+    g = pair_grad[0]
+
+    blocks = {0: x}
+    for bit in bits_of(n_dap):
+        blocks.update({s ^ bit: swap(b, "dap", n_dap, bit) for s, b in list(blocks.items())})
+    cut = g.reshape(rows, n_dap, rows, width)
+    parts = {
+        0: {r: lax.dynamic_index_in_dim(cut, me ^ r, 1, keepdims=False) for r in range(n_dap)}
+    }
+    for bit in bits_of(n_dap):
+        new = {}
+        for s, cols in parts.items():
+            new[s ^ bit] = {
+                r: swap(cols[r ^ bit], "dap", n_dap, bit) for r in cols if not r & bit
+            }
+        parts = {s: {r: v for r, v in cols.items() if not r & bit} for s, cols in parts.items()}
+        parts.update(new)
+    blocks = [blocks[s] for s in range(n_dap)]
+    columns = [parts[s][0] for s in range(n_dap)]
+
+    half = rows // 2
+    tiles = n_dap * half
+    grad_rows = 6 * LANES + 16 * n_dap
+    vm = functools.partial(pltpu.VMEM)
+    dz, grads = pl.pallas_call(
+        functools.partial(fused_kernel, n_dap),
+        out_shape=(
+            jax.ShapeDtypeStruct((rows, tokens, width), BF16),
+            jax.ShapeDtypeStruct((grad_rows, LANES), BF16),
+        ),
+        in_specs=[pl.BlockSpec(memory_space=pltpu.SMEM)]
+        + [pl.BlockSpec(memory_space=pltpu.VMEM)] * (2 * n_dap + 9),
+        out_specs=(
+            pl.BlockSpec(memory_space=pltpu.VMEM),
+            pl.BlockSpec(memory_space=pltpu.VMEM),
+        ),
+        scratch_shapes=[
+            vm((4 * hidden, width), BF16),
+            vm((width, width), BF16),
+            vm((width, hidden), BF16),
+            vm((4, width, LANES), F32),
+            vm((tiles, LANES), F32),
+            vm((n_dap * rows * tokens, width), F32),
+            vm((n_dap * rows * rows, width), F32),
+            vm((hidden * tiles, LANES), F32),
+            vm((hidden * tiles, LANES), F32),
+            vm((half, 4 * hidden, LANES), F32),
+            vm((half, width, LANES), BF16),
+            vm((half, width, LANES), F32),
+            vm((half, 1, LANES), F32),
+            vm((hidden, LANES, LANES), BF16),
+            vm((hidden, LANES, LANES), BF16),
+            vm((2, hidden * half, LANES), F32),
+            vm((half, width, LANES), BF16),
+            vm((10, LANES, LANES), F32),
+        ],
+        compiler_params=pltpu.CompilerParams(vmem_limit_bytes=48 * 1024 * 1024),
+    )(
+        me.astype(jnp.int32).reshape(1),
+        token_mask,
+        *blocks,
+        g,
+        *columns,
+        w_edges,
+        w_gate,
+        w_out,
+        in_gain.reshape(1, -1),
+        in_bias.reshape(1, -1),
+        output_norm_gain.reshape(1, -1),
+        output_norm_bias.reshape(1, -1),
+    )
+
+    total = grads
+    for bit in reversed(bits_of(n_dap)):
+        total = total.reshape(2, -1, LANES)
+        mine = ((me & bit) > 0).astype(jnp.int32)
+        got = swap(pick(total, 1 - mine), "dap", n_dap, bit)
+        total = (pick(total, mine).astype(F32) + got.astype(F32)).astype(BF16)
+    for bit in reversed(bits_of(n_dp)):
+        total = (total.astype(F32) + swap(total, "dp", n_dp, bit).astype(F32)).astype(BF16)
+    for bit in bits_of(n_dap):
+        got = swap(total, "dap", n_dap, bit)
+        first = (me & bit) == 0
+        total = jnp.where(
+            first, jnp.concatenate([total, got]), jnp.concatenate([got, total])
+        )
+    total = total.astype(F32)
+    edges = total[: 4 * LANES].reshape(4, width, hidden).transpose(1, 0, 2).reshape(width, -1)
+    tail = total[6 * LANES :]
+    return (
+        dz[None],
+        edges,
+        total[4 * LANES : 5 * LANES],
+        total[5 * LANES : 6 * LANES],
+        tail[0:2],
+        tail[2:4],
+    )
+
+
 def solution(mesh):
     in_specs = (
         P("dp", "dap", None, None),
@@ -166,6 +524,24 @@
         P(),
     )
     out_specs = (P("dp", "dap", None, None), P(), P(), P(), P(), P())
+    n_dp, n_dap = mesh.shape["dp"], mesh.shape["dap"]
+
+    def per_device(pair, *others):
+        structs, rows, tokens, width = pair.shape
+        hidden = others[4].shape[0]
+        fits = (
+            structs == 1
+            and 2 * tokens == LANES
+            and rows == 16
+            and width == LANES
+            and hidden == LANES
+            and n_dap & (n_dap - 1) == 0
+            and n_dp & (n_dp - 1) == 0
+        )
+        if fits:
+            return per_device_fused(n_dp, n_dap, pair, *others)
+        return per_device_exchange(pair, *others)
+
     return jax.shard_map(
         per_device, mesh=mesh, in_specs=in_specs, out_specs=out_specs, check_vma=False
     )

time: 259 us -> 85.1 us (0.33)
  waiting for transfers between devices: 146 us -> 25.3 us
  local copies, waits for them, and re-layouts: 47.6 us -> 3.96 us
  Pallas kernels: 0 us -> 39.4 us
  matrix products: 15 us -> 0 us
  between operations: 14.5 us -> 0.88 us
  starting transfers between devices: 24.8 us -> 15.2 us
  other arithmetic: 9.16 us -> 0.18 us
    psum x1 -> x0, waiting for transfers between devices: 126 us -> none  [per_device(): summed = lax.psum(flat, ('dp', 'dap'))]
    pallas_call x0 -> x1, Pallas kernels: none -> 39.4 us  [per_device_fused(): pl.pallas_call(functools.partial(fused_kernel, n_dap), out_shape=(jax.Sha...]
    ppermute x0 -> x14, waiting for transfers between devices: none -> 25.3 us  [swap(): return lax.ppermute(x, axis, [(i, i ^ bit) for i in range(n)])]
    all_to_all x6 -> x0, starting transfers between devices: 24.8 us -> none  [the longest x1 4.24 us: per_device(): lax.all_to_all(edge_values(pre_left), 'dap', split_axis=1, concat_axis=0,...]
    unnamed x54 -> x20, local copies, waits for them, and re-layouts: 23.7 us -> 0.94 us
    all_to_all x6 -> x0, waiting for transfers between devices: 19.9 us -> none  [the longest x1 4.81 us: per_device(): lax.all_to_all(tri, 'dap', split_axis=0, concat_axis=1, tiled=True)]
    convert_element_type x12 -> x0, local copies, waits for them, and re-layouts: 18.6 us -> none  [the longest x4 6.89 us: pre_grad(): masked = dvalues.astype(jnp.float32) * edge_mask]
    ppermute x0 -> x14, starting transfers between devices: none -> 15.2 us  [swap(): return lax.ppermute(x, axis, [(i, i ^ bit) for i in range(n)])]
  transfers between devices with their start and end apart: 7 -> 14, of which waited for: 7 -> 10; matrix products, arithmetic and copies ran while one was open for 7% -> 1% of each run, Pallas kernels for 0% -> 0%
where the time goes in v1:
time: 85.1 us; the launch traced here: 85 us
  Pallas kernels  39.4 us (46%)
  waiting for transfers between devices  25.3 us (30%)
  starting transfers between devices  15.2 us (18%)
  local copies, waits for them, and re-layouts  3.96 us (5%)
  between operations  0.88 us (1%)
    pallas_call x1, Pallas kernels, per_device_fused(): pl.pallas_call(functools.partial(fused_kernel, n_dap), out_shape=(jax.Sha...  39.4 us
    ppermute x14, waiting for transfers between devices, swap(): return lax.ppermute(x, axis, [(i, i ^ bit) for i in range(n)])  25.3 us
    ppermute x14, starting transfers between devices, swap(): return lax.ppermute(x, axis, [(i, i ^ bit) for i in range(n)])  15.2 us
  transfers between devices with their start and end apart: 14, of which 10 were waited for; matrix products, arithmetic and copies ran while one was open for 1% of the time, Pallas kernels for 0%

profile of v1, /device:TPU:0, one launch (start us, length us, event | category | flops | bytes accessed | tf_op | source)
XLA Modules:
  0.0 85.0 jit_solution(2689619101802076816)
XLA Ops:
  0.6 3.0 %collective-permute-start.1 = (bf16[16,64,128]{2,1,0:T(8,128)(2,1)}, bf16[16,64,128]{2,1,0:T(8,128)(2,1)S(1)}, u32[]{:S(2)}, u32[]{:S(2)}) collective-permute-start(bf16[16,64,128]{2,1,0:T(8,128)(2,1)} %bitcast.46), channel_id=1, source_target_pairs={{0,2},{1,3},{2,0},{3,1},{4,6},{5,7},{6,4},{7,5},{8,10},{9,11},{10,... | collective-permute-start | bytes 786440 | tf_op jit(solution)/shard_map/ppermute | solution.py:384
  3.7 0.0 collective-permute-start
  3.7 6.5 %collective-permute-done.1.refs_2_ = bf16[16,64,128]{2,1,0:T(8,128)(2,1)S(1)} collective-permute-done((bf16[16,64,128]{2,1,0:T(8,128)(2,1)}, bf16[16,64,128]{2,1,0:T(8,128)(2,1)S(1)}, u32[]{:S(2)}, u32[]{:S(2)}) %collective-permute-start.1) | collective-permute-done | bytes 262176 | tf_op jit(solution)/shard_map/ppermute | solution.py:384
  10.2 0.0 collective-permute-start.2
  10.2 0.0 copy-start.9
  10.2 0.0 copy-start.4
  10.2 0.0 copy-start
  10.3 1.0 %dynamic-slice_bitcast_fusion.1 = (bf16[16,16,128]{2,1,0:T(8,128)(2,1)S(1)}, bf16[16,16,128]{2,1,0:T(8,128)(2,1)S(1)}, bf16[16,16,128]{2,1,0:T(8,128)(2,1)S(1)}, bf16[16,16,128]{2,1,0:T(8,128)(2,1)S(1)}) fusion(bf16[16,4,16,128]{3,2,1,0:T(8,128)(2,1)} %bitcast.44, s32[]{:T(128)S(6)} %select_n.46, s32[]{:T(128)S(6)} %select_n.45, s32[]{:T(128)S(6)} %select_n.44, ...), kind=kLoop, calls=%fused_computation.12 | loop fusion | bytes 524304 | tf_op jit(solution)/shard_map/jit(dynamic_index_in_dim)/squeeze | solution.py:421
  11.3 0.0 copy-start.3
  11.3 1.8 %collective-permute-start.5 = (bf16[16,16,128]{2,1,0:T(8,128)(2,1)S(1)}, bf16[16,16,128]{2,1,0:T(8,128)(2,1)S(1)}, u32[]{:S(2)}, u32[]{:S(2)}) collective-permute-start(bf16[16,16,128]{2,1,0:T(8,128)(2,1)S(1)} %get-tuple-element.14), channel_id=1, source_target_pairs={{0,2},{1,3},{2,0},{3,1},{4,6},{5,7},{6,4},{7,5},{8,10},{9,11},{10,... | collective-permute-start | bytes 196616 | tf_op jit(solution)/shard_map/ppermute | solution.py:384
  13.1 0.2 collective-permute-start.3
  13.3 0.4 collective-permute-start.4
  13.7 2.2 %collective-permute-done.5 = bf16[16,16,128]{2,1,0:T(8,128)(2,1)S(1)} collective-permute-done((bf16[16,16,128]{2,1,0:T(8,128)(2,1)S(1)}, bf16[16,16,128]{2,1,0:T(8,128)(2,1)S(1)}, u32[]{:S(2)}, u32[]{:S(2)}) %collective-permute-start.5) | collective-permute-done | bytes 65568 | tf_op jit(solution)/shard_map/ppermute | solution.py:384
  15.9 0.0 collective-permute-start.6
  15.9 0.0 collective-permute-done.3.refs_6_
  15.9 1.7 %collective-permute-done.4.refs_7_ = bf16[16,16,128]{2,1,0:T(8,128)(2,1)S(1)} collective-permute-done((bf16[16,16,128]{2,1,0:T(8,128)(2,1)S(1)}, bf16[16,16,128]{2,1,0:T(8,128)(2,1)S(1)}, u32[]{:S(2)}, u32[]{:S(2)}) %collective-permute-start.4) | collective-permute-done | bytes 65568 | tf_op jit(solution)/shard_map/ppermute | solution.py:384
  17.6 0.0 collective-permute-done.6.refs_8_
  17.6 0.0 collective-permute-done.refs_1_
  17.6 0.0 collective-permute-done.2.refs_3_
  17.6 0.0 copy-done.6
  17.6 0.0 copy-done.7
  17.7 0.0 copy-done.8
  17.7 0.0 copy-done.9
  17.7 0.0 copy-done.4
  17.7 0.0 copy-done
  17.7 0.0 copy-done.1
  17.7 0.0 copy-done.5
  17.7 0.0 copy-done.3
  17.7 0.0 copy-start.2
  17.7 0.9 %copy-done.2 = bf16[128,512]{1,0:T(8,128)(2,1)S(1)} copy-done((bf16[128,512]{1,0:T(8,128)(2,1)S(1)}, bf16[128,512]{1,0:T(8,128)(2,1)}, u32[]{:S(2)}) %copy-start.2) | copy-done | bytes 131096
  18.6 39.4 %shard_map.145 = (bf16[16,64,128]{2,1,0:T(8,128)(2,1)}, bf16[832,128]{1,0:T(8,128)(2,1)S(1)}) custom-call(s32[1]{0:T(128)} %bitcast.me_ref, s32[1,64]{1,0:T(1,128)S(1)} %copy-done.5, bf16[16,64,128]{2,1,0:T(8,128)(2,1)S(1)} %bitcast.48, bf16[16,64,128]{2,1,0:T(8,128)(2,1)S(1)} %collective-permute-done.refs_1_, ...), custom_call_target="tpu_custom_call" | custom-call | tf_op jit(solution)/shard_map/pallas_call | solution.py:438
  58.0 0.1 collective-permute-start.7
  58.1 1.3 %collective-permute-done.7 = bf16[416,128]{1,0:T(8,128)(2,1)S(1)} collective-permute-done((bf16[416,128]{1,0:T(8,128)(2,1)S(1)}, bf16[416,128]{1,0:T(8,128)(2,1)S(1)}, u32[]{:S(2)}, u32[]{:S(2)}) %collective-permute-start.7) | collective-permute-done | bytes 106528 | tf_op jit(solution)/shard_map/ppermute | solution.py:384
  59.5 1.7 %collective-permute-start.8 = (bf16[208,128]{1,0:T(8,128)(2,1)S(1)}, bf16[208,128]{1,0:T(8,128)(2,1)S(1)}, u32[]{:S(2)}, u32[]{:S(2)}) collective-permute-start(bf16[208,128]{1,0:T(8,128)(2,1)S(1)} %dynamic-slice_bitcast_fusion.5), channel_id=1, source_target_pairs={{0,2},{1,3},{2,0},{3,1},{4,6},{5,7},{6,4},{7,5},{8,10},{9,11},{10,... | collective-permute-start | bytes 159752 | tf_op jit(solution)/shard_map/ppermute | solution.py:384
  61.1 2.5 %collective-permute-done.8 = bf16[208,128]{1,0:T(8,128)(2,1)S(1)} collective-permute-done((bf16[208,128]{1,0:T(8,128)(2,1)S(1)}, bf16[208,128]{1,0:T(8,128)(2,1)S(1)}, u32[]{:S(2)}, u32[]{:S(2)}) %collective-permute-start.8) | collective-permute-done | bytes 53280 | tf_op jit(solution)/shard_map/ppermute | solution.py:384
  63.7 1.6 %collective-permute-start.9 = (bf16[208,128]{1,0:T(8,128)(2,1)S(1)}, bf16[208,128]{1,0:T(8,128)(2,1)S(1)}, u32[]{:S(2)}, u32[]{:S(2)}) collective-permute-start(bf16[208,128]{1,0:T(8,128)(2,1)S(1)} %fusion.2), channel_id=1, source_target_pairs={{0,4},{4,0},{8,12},{12,8},{16,20},{20,16},{24,28},{28,24},{1,5},{5... | collective-permute-start | bytes 159752 | tf_op jit(solution)/shard_map/ppermute | solution.py:384
  65.2 2.6 %collective-permute-done.9 = bf16[208,128]{1,0:T(8,128)(2,1)S(1)} collective-permute-done((bf16[208,128]{1,0:T(8,128)(2,1)S(1)}, bf16[208,128]{1,0:T(8,128)(2,1)S(1)}, u32[]{:S(2)}, u32[]{:S(2)}) %collective-permute-start.9) | collective-permute-done | bytes 53280 | tf_op jit(solution)/shard_map/ppermute | solution.py:384
  67.9 1.6 %collective-permute-start.10 = (bf16[208,128]{1,0:T(8,128)(2,1)S(1)}, bf16[208,128]{1,0:T(8,128)(2,1)S(1)}, u32[]{:S(2)}, u32[]{:S(2)}) collective-permute-start(bf16[208,128]{1,0:T(8,128)(2,1)S(1)} %add_convert_fusion.2), channel_id=1, source_target_pairs={{0,8},{4,12},{8,0},{12,4},{16,24},{20,28},{24,16},{28,20},{1,9},{5... | collective-permute-start | bytes 159752 | tf_op jit(solution)/shard_map/ppermute | solution.py:384
  69.5 2.6 %collective-permute-done.10 = bf16[208,128]{1,0:T(8,128)(2,1)S(1)} collective-permute-done((bf16[208,128]{1,0:T(8,128)(2,1)S(1)}, bf16[208,128]{1,0:T(8,128)(2,1)S(1)}, u32[]{:S(2)}, u32[]{:S(2)}) %collective-permute-start.10) | collective-permute-done | bytes 53280 | tf_op jit(solution)/shard_map/ppermute | solution.py:384
  72.1 3.1 %collective-permute-start.11 = (bf16[208,128]{1,0:T(8,128)(2,1)S(1)}, bf16[208,128]{1,0:T(8,128)(2,1)S(1)}, u32[]{:S(2)}, u32[]{:S(2)}) collective-permute-start(bf16[208,128]{1,0:T(8,128)(2,1)S(1)} %add_convert_fusion.1), channel_id=1, source_target_pairs={{0,16},{4,20},{8,24},{12,28},{16,0},{20,4},{24,8},{28,12},{1,17},{... | collective-permute-start | bytes 159752 | tf_op jit(solution)/shard_map/ppermute | solution.py:384
  75.2 2.1 %collective-permute-done.11 = bf16[208,128]{1,0:T(8,128)(2,1)S(1)} collective-permute-done((bf16[208,128]{1,0:T(8,128)(2,1)S(1)}, bf16[208,128]{1,0:T(8,128)(2,1)S(1)}, u32[]{:S(2)}, u32[]{:S(2)}) %collective-permute-start.11) | collective-permute-done | bytes 53280 | tf_op jit(solution)/shard_map/ppermute | solution.py:384
  77.3 1.7 %collective-permute-start.12 = (bf16[208,128]{1,0:T(8,128)(2,1)S(1)}, bf16[208,128]{1,0:T(8,128)(2,1)S(1)}, u32[]{:S(2)}, u32[]{:S(2)}) collective-permute-start(bf16[208,128]{1,0:T(8,128)(2,1)S(1)} %add_convert_fusion), channel_id=1, source_target_pairs={{0,2},{1,3},{2,0},{3,1},{4,6},{5,7},{6,4},{7,5},{8,10},{9,11},{10,... | collective-permute-start | bytes 159752 | tf_op jit(solution)/shard_map/ppermute | solution.py:384
  79.1 2.5 %collective-permute-done.12 = bf16[208,128]{1,0:T(8,128)(2,1)S(1)} collective-permute-done((bf16[208,128]{1,0:T(8,128)(2,1)S(1)}, bf16[208,128]{1,0:T(8,128)(2,1)S(1)}, u32[]{:S(2)}, u32[]{:S(2)}) %collective-permute-start.12) | collective-permute-done | bytes 53280 | tf_op jit(solution)/shard_map/ppermute | solution.py:384
  81.5 0.1 collective-permute-start.13
  81.6 1.3 %collective-permute-done.13 = bf16[416,128]{1,0:T(8,128)(2,1)S(1)} collective-permute-done((bf16[416,128]{1,0:T(8,128)(2,1)S(1)}, bf16[416,128]{1,0:T(8,128)(2,1)S(1)}, u32[]{:S(2)}, u32[]{:S(2)}) %collective-permute-start.13) | collective-permute-done | bytes 106528 | tf_op jit(solution)/shard_map/ppermute | solution.py:384
  83.0 0.7 fusion.4
  83.7 0.6 fusion.3
  84.2 0.7 copy.27
  (15 shorter events, 0.2 us)
Async XLA Ops:
  0.6 9.5 %collective-permute-start.1 = (bf16[16,64,128]{2,1,0:T(8,128)(2,1)}, bf16[16,64,128]{2,1,0:T(8,128)(2,1)S(1)}, u32[]{:S(2)}, u32[]{:S(2)}) collective-permute-start(bf16[16,64,128]{2,1,0:T(8,128)(2,1)} %bitcast.46), channel_id=1, source_target_pairs={{0,2},{1,3},{2,0},{3,1},{4,6},{5,7},{6,4},{7,5},{8,10},{9,11},{10,... | collective-permute-start | bytes 786440 | tf_op jit(solution)/shard_map/ppermute | solution.py:384
  3.7 14.0 %collective-permute-start = (bf16[16,64,128]{2,1,0:T(8,128)(2,1)}, bf16[16,64,128]{2,1,0:T(8,128)(2,1)S(1)}, u32[]{:S(2)}, u32[]{:S(2)}) collective-permute-start(bf16[16,64,128]{2,1,0:T(8,128)(2,1)} %bitcast.47), channel_id=1, source_target_pairs={{0,1},{1,0},{2,3},{3,2},{4,5},{5,4},{6,7},{7,6},{8,9},{9,8},{10,11... | collective-permute-start | bytes 786440 | tf_op jit(solution)/shard_map/ppermute | solution.py:384
  10.2 7.4 %collective-permute-start.2 = (bf16[16,64,128]{2,1,0:T(8,128)(2,1)S(1)}, bf16[16,64,128]{2,1,0:T(8,128)(2,1)S(1)}, u32[]{:S(2)}, u32[]{:S(2)}) collective-permute-start(bf16[16,64,128]{2,1,0:T(8,128)(2,1)S(1)} %collective-permute-done.1.refs_2_), channel_id=1, source_target_pairs={{0,1},{1,0},{2,3},{3,2},{4,5},{5,4},{6,7},{7,6},{8,9},{9,8},{10,11... | collective-permute-start | bytes 786440 | tf_op jit(solution)/shard_map/ppermute | solution.py:384
  10.2 7.5 %copy-start.6 = (f32[128]{0:T(128)S(1)}, f32[128]{0:T(128)}, u32[]{:S(2)}) copy-start(f32[128]{0:T(128)} %param.16) | copy-start | bytes 1540
  10.2 7.5 %copy-start.7 = (f32[128]{0:T(128)S(1)}, f32[128]{0:T(128)}, u32[]{:S(2)}) copy-start(f32[128]{0:T(128)} %param.17) | copy-start | bytes 1540
  10.2 7.5 %copy-start.8 = (f32[128]{0:T(128)S(1)}, f32[128]{0:T(128)}, u32[]{:S(2)}) copy-start(f32[128]{0:T(128)} %param.18) | copy-start | bytes 1540
  10.2 7.5 %copy-start.9 = (f32[128]{0:T(128)S(1)}, f32[128]{0:T(128)}, u32[]{:S(2)}) copy-start(f32[128]{0:T(128)} %param.19) | copy-start | bytes 1540
  10.2 7.5 %copy-start.4 = (bf16[128,128]{1,0:T(8,128)(2,1)S(1)}, bf16[128,128]{1,0:T(8,128)(2,1)}, u32[]{:S(2)}) copy-start(bf16[128,128]{1,0:T(8,128)(2,1)} %refs_11_.1) | copy-start | bytes 98308
  10.2 7.5 %copy-start = (bf16[1,16,64,128]{3,2,1,0:T(8,128)(2,1)S(1)}, bf16[1,16,64,128]{3,2,1,0:T(8,128)(2,1)}, u32[]{:S(2)}) copy-start(bf16[1,16,64,128]{3,2,1,0:T(8,128)(2,1)} %param.11) | copy-start | bytes 786436
  10.2 7.5 %copy-start.1 = (bf16[1,16,64,128]{3,2,1,0:T(8,128)(2,1)S(1)}, bf16[1,16,64,128]{3,2,1,0:T(8,128)(2,1)}, u32[]{:S(2)}) copy-start(bf16[1,16,64,128]{3,2,1,0:T(8,128)(2,1)} %param.10) | copy-start | bytes 786436
  10.3 7.5 %copy-start.5 = (s32[1,64]{1,0:T(1,128)S(1)}, s32[1,64]{1,0:T(1,128)}, u32[]{:S(2)}) copy-start(s32[1,64]{1,0:T(1,128)} %mask_ref.1) | copy-start | bytes 772
  11.3 6.4 %copy-start.3 = (bf16[128,128]{1,0:T(8,128)(2,1)S(1)}, bf16[128,128]{1,0:T(8,128)(2,1)}, u32[]{:S(2)}) copy-start(bf16[128,128]{1,0:T(8,128)(2,1)} %refs_10_.1) | copy-start | bytes 98308
  11.3 4.6 %collective-permute-start.5 = (bf16[16,16,128]{2,1,0:T(8,128)(2,1)S(1)}, bf16[16,16,128]{2,1,0:T(8,128)(2,1)S(1)}, u32[]{:S(2)}, u32[]{:S(2)}) collective-permute-start(bf16[16,16,128]{2,1,0:T(8,128)(2,1)S(1)} %get-tuple-element.14), channel_id=1, source_target_pairs={{0,2},{1,3},{2,0},{3,1},{4,6},{5,7},{6,4},{7,5},{8,10},{9,11},{10,... | collective-permute-start | bytes 196616 | tf_op jit(solution)/shard_map/ppermute | solution.py:384
  13.1 2.8 %collective-permute-start.3 = (bf16[16,16,128]{2,1,0:T(8,128)(2,1)S(1)}, bf16[16,16,128]{2,1,0:T(8,128)(2,1)S(1)}, u32[]{:S(2)}, u32[]{:S(2)}) collective-permute-start(bf16[16,16,128]{2,1,0:T(8,128)(2,1)S(1)} %get-tuple-element.16), channel_id=1, source_target_pairs={{0,1},{1,0},{2,3},{3,2},{4,5},{5,4},{6,7},{7,6},{8,9},{9,8},{10,11... | collective-permute-start | bytes 196616 | tf_op jit(solution)/shard_map/ppermute | solution.py:384
  13.3 4.3 %collective-permute-start.4 = (bf16[16,16,128]{2,1,0:T(8,128)(2,1)S(1)}, bf16[16,16,128]{2,1,0:T(8,128)(2,1)S(1)}, u32[]{:S(2)}, u32[]{:S(2)}) collective-permute-start(bf16[16,16,128]{2,1,0:T(8,128)(2,1)S(1)} %get-tuple-element.15), channel_id=1, source_target_pairs={{0,2},{1,3},{2,0},{3,1},{4,6},{5,7},{6,4},{7,5},{8,10},{9,11},{10,... | collective-permute-start | bytes 196616 | tf_op jit(solution)/shard_map/ppermute | solution.py:384
  15.9 1.8 %collective-permute-start.6 = (bf16[16,16,128]{2,1,0:T(8,128)(2,1)S(1)}, bf16[16,16,128]{2,1,0:T(8,128)(2,1)S(1)}, u32[]{:S(2)}, u32[]{:S(2)}) collective-permute-start(bf16[16,16,128]{2,1,0:T(8,128)(2,1)S(1)} %collective-permute-done.5), channel_id=1, source_target_pairs={{0,1},{1,0},{2,3},{3,2},{4,5},{5,4},{6,7},{7,6},{8,9},{9,8},{10,11... | collective-permute-start | bytes 196616 | tf_op jit(solution)/shard_map/ppermute | solution.py:384
  17.7 0.9 %copy-start.2 = (bf16[128,512]{1,0:T(8,128)(2,1)S(1)}, bf16[128,512]{1,0:T(8,128)(2,1)}, u32[]{:S(2)}) copy-start(bf16[128,512]{1,0:T(8,128)(2,1)} %refs_9_.1) | copy-start | bytes 393220
  58.0 1.4 %collective-permute-start.7 = (bf16[416,128]{1,0:T(8,128)(2,1)S(1)}, bf16[416,128]{1,0:T(8,128)(2,1)S(1)}, u32[]{:S(2)}, u32[]{:S(2)}) collective-permute-start(bf16[416,128]{1,0:T(8,128)(2,1)S(1)} %dynamic-slice_bitcast_fusion), channel_id=1, source_target_pairs={{0,1},{1,0},{2,3},{3,2},{4,5},{5,4},{6,7},{7,6},{8,9},{9,8},{10,11... | collective-permute-start | bytes 319496 | tf_op jit(solution)/shard_map/ppermute | solution.py:384
  59.5 4.2 %collective-permute-start.8 = (bf16[208,128]{1,0:T(8,128)(2,1)S(1)}, bf16[208,128]{1,0:T(8,128)(2,1)S(1)}, u32[]{:S(2)}, u32[]{:S(2)}) collective-permute-start(bf16[208,128]{1,0:T(8,128)(2,1)S(1)} %dynamic-slice_bitcast_fusion.5), channel_id=1, source_target_pairs={{0,2},{1,3},{2,0},{3,1},{4,6},{5,7},{6,4},{7,5},{8,10},{9,11},{10,... | collective-permute-start | bytes 159752 | tf_op jit(solution)/shard_map/ppermute | solution.py:384
  63.7 4.2 %collective-permute-start.9 = (bf16[208,128]{1,0:T(8,128)(2,1)S(1)}, bf16[208,128]{1,0:T(8,128)(2,1)S(1)}, u32[]{:S(2)}, u32[]{:S(2)}) collective-permute-start(bf16[208,128]{1,0:T(8,128)(2,1)S(1)} %fusion.2), channel_id=1, source_target_pairs={{0,4},{4,0},{8,12},{12,8},{16,20},{20,16},{24,28},{28,24},{1,5},{5... | collective-permute-start | bytes 159752 | tf_op jit(solution)/shard_map/ppermute | solution.py:384
  67.9 4.2 %collective-permute-start.10 = (bf16[208,128]{1,0:T(8,128)(2,1)S(1)}, bf16[208,128]{1,0:T(8,128)(2,1)S(1)}, u32[]{:S(2)}, u32[]{:S(2)}) collective-permute-start(bf16[208,128]{1,0:T(8,128)(2,1)S(1)} %add_convert_fusion.2), channel_id=1, source_target_pairs={{0,8},{4,12},{8,0},{12,4},{16,24},{20,28},{24,16},{28,20},{1,9},{5... | collective-permute-start | bytes 159752 | tf_op jit(solution)/shard_map/ppermute | solution.py:384
  72.1 5.2 %collective-permute-start.11 = (bf16[208,128]{1,0:T(8,128)(2,1)S(1)}, bf16[208,128]{1,0:T(8,128)(2,1)S(1)}, u32[]{:S(2)}, u32[]{:S(2)}) collective-permute-start(bf16[208,128]{1,0:T(8,128)(2,1)S(1)} %add_convert_fusion.1), channel_id=1, source_target_pairs={{0,16},{4,20},{8,24},{12,28},{16,0},{20,4},{24,8},{28,12},{1,17},{... | collective-permute-start | bytes 159752 | tf_op jit(solution)/shard_map/ppermute | solution.py:384
  77.3 4.2 %collective-permute-start.12 = (bf16[208,128]{1,0:T(8,128)(2,1)S(1)}, bf16[208,128]{1,0:T(8,128)(2,1)S(1)}, u32[]{:S(2)}, u32[]{:S(2)}) collective-permute-start(bf16[208,128]{1,0:T(8,128)(2,1)S(1)} %add_convert_fusion), channel_id=1, source_target_pairs={{0,2},{1,3},{2,0},{3,1},{4,6},{5,7},{6,4},{7,5},{8,10},{9,11},{10,... | collective-permute-start | bytes 159752 | tf_op jit(solution)/shard_map/ppermute | solution.py:384
  81.5 1.4 %collective-permute-start.13 = (bf16[416,128]{1,0:T(8,128)(2,1)S(1)}, bf16[416,128]{1,0:T(8,128)(2,1)S(1)}, u32[]{:S(2)}, u32[]{:S(2)}) collective-permute-start(bf16[416,128]{1,0:T(8,128)(2,1)S(1)} %maximum_select_fusion.1), channel_id=1, source_target_pairs={{0,1},{1,0},{2,3},{3,2},{4,5},{5,4},{6,7},{7,6},{8,9},{9,8},{10,11... | collective-permute-start | bytes 319496 | tf_op jit(solution)/shard_map/ppermute | solution.py:384

commit v2 on v1

--- a/solution.py
+++ b/solution.py
@@ -182,16 +182,22 @@
     return (scaled - m1 - normed * m2) * rstd
 
 
-def block_diagonal(tiles, low):
-    turned = pltpu.roll(tiles, LANES // 2, 1)
-    zero = jnp.zeros((8, LANES), F32)
-    top, bottom = [], []
+def halves(x):
+    n = LANES // 2
+    return jnp.concatenate([x[:, :n], x[:, n:]], axis=0).astype(BF16)
+
+
+def lanes(x):
+    return jnp.concatenate([x[:8], x[8:]], axis=1)
+
+
+def square(tiles):
+    n = LANES // 2
+    parts = []
     for a in range(tiles.shape[0] // 8):
         x = tiles[8 * a : 8 * a + 8]
-        y = turned[8 * a : 8 * a + 8]
-        top += [jnp.where(low, x, zero), jnp.where(low, y, zero)]
-        bottom += [jnp.where(low, zero, y), jnp.where(low, zero, x)]
-    return jnp.concatenate(top + bottom, axis=0).astype(BF16)
+        parts += [x[:, :n], x[:, n:]]
+    return jnp.concatenate(parts, axis=0).astype(BF16)
 
 
 def fused_kernel(
@@ -259,7 +265,7 @@
     for s in range(n_blocks):
         a = jnp.bitwise_xor(me, s)
 
-        @pl.loop(0, half)
+        @pl.loop(0, half, unroll=8)
         def _(t, s=s, a=a):
             lo = f(pair_refs[s][t])
             hi = f(pair_refs[s][t + half])
@@ -284,19 +290,19 @@
             pgt_refs[s][...].reshape(rows * rows, width)
         )
 
-    @pl.loop(0, hidden, unroll=4)
+    @pl.loop(0, hidden, unroll=32)
     def _(h):
         at = pl.multiple_of(h * tiles, tiles)
         own = pl.multiple_of(h * tiles + me * half, half)
-        right = block_diagonal(rs[pl.ds(at, tiles), :], low)
-        left = block_diagonal(ls[pl.ds(at, tiles), :], low)
+        right = square(rs[pl.ds(at, tiles), :])
+        left = square(ls[pl.ds(at, tiles), :])
         bdr[h] = right
         bdl[h] = left
         out = pl.multiple_of(h * half, half)
-        pr[0, pl.ds(out, half), :] = dot_nt(ls[pl.ds(own, half), :].astype(BF16), right)
-        pr[1, pl.ds(out, half), :] = dot_nt(rs[pl.ds(own, half), :].astype(BF16), left)
-
-    @pl.loop(0, half)
+        pr[0, pl.ds(out, half), :] = lanes(dot_nt(halves(ls[pl.ds(own, half), :]), right))
+        pr[1, pl.ds(out, half), :] = lanes(dot_nt(halves(rs[pl.ds(own, half), :]), left))
+
+    @pl.loop(0, half, unroll=8)
     def _(t):
         for own in (True, False):
             which = 0 if own else 1
@@ -339,13 +345,13 @@
                 dxn, vec[2], xhat, rstd
             )
 
-    @pl.loop(0, hidden, unroll=4)
+    @pl.loop(0, hidden, unroll=32)
     def _(h):
         at = pl.multiple_of(h * half, half)
-        pr[0, pl.ds(at, half), :] = dot(pr[0, pl.ds(at, half), :].astype(BF16), bdr[h])
-        pr[1, pl.ds(at, half), :] = dot(pr[1, pl.ds(at, half), :].astype(BF16), bdl[h])
-
-    @pl.loop(0, half)
+        pr[0, pl.ds(at, half), :] = lanes(dot(halves(pr[0, pl.ds(at, half), :]), bdr[h]))
+        pr[1, pl.ds(at, half), :] = lanes(dot(halves(pr[1, pl.ds(at, half), :]), bdl[h]))
+
+    @pl.loop(0, half, unroll=8)
     def _(t):
         mask = pm[pl.ds(me * half + t, 1), :]
         zn = zn_own[t]
@@ -368,12 +374,29 @@
         dz_ref[t] = dz[:tokens]
         dz_ref[t + half] = dz[tokens:]
 
+    total = grads_ref
     for b in range(6):
-        grads_ref[b * LANES : (b + 1) * LANES, :] = gacc[b].astype(BF16)
+        total[b * LANES : (b + 1) * LANES, :] = gacc[b].astype(BF16)
     sums = [jnp.sum(gacc[b].T, axis=0, keepdims=True) for b in (8, 9, 6, 7)]
-    pad = grads_ref.shape[0] - 6 * LANES
+    pad = total.shape[0] - 6 * LANES
     sums.append(jnp.zeros((pad - 4, LANES), F32))
-    grads_ref[6 * LANES :, :] = jnp.concatenate(sums, axis=0).astype(BF16)
+    total[6 * LANES :, :] = jnp.concatenate(sums, axis=0).astype(BF16)
+
+
+def finish_kernel(n_blocks, me_ref, *refs):
+    chunks = refs[:n_blocks]
+    edges_ref, gate_ref, out_ref, in_norm_ref, out_norm_ref, total = refs[n_blocks:]
+    me = me_ref[0]
+    rows = chunks[0].shape[0]
+    for s in range(n_blocks):
+        at = pl.multiple_of(jnp.bitwise_xor(me, s) * rows, rows)
+        total[pl.ds(at, rows), :] = chunks[s][...].astype(F32)
+    for b in range(4):
+        edges_ref[:, b * LANES : (b + 1) * LANES] = total[b * LANES : (b + 1) * LANES, :]
+    gate_ref[...] = total[4 * LANES : 5 * LANES, :]
+    out_ref[...] = total[5 * LANES : 6 * LANES, :]
+    in_norm_ref[...] = total[6 * LANES : 6 * LANES + 2, :]
+    out_norm_ref[...] = total[6 * LANES + 2 : 6 * LANES + 4, :]
 
 
 def pick(x, i):
@@ -410,26 +433,28 @@
     rows, tokens, width = pair.shape[1:]
     hidden = w_out.shape[0]
     me = lax.axis_index("dap")
+    place = me.astype(jnp.int32).reshape(1)
     x = pair[0]
     g = pair_grad[0]
 
     blocks = {0: x}
+    columns = {0: g}
     for bit in bits_of(n_dap):
-        blocks.update({s ^ bit: swap(b, "dap", n_dap, bit) for s, b in list(blocks.items())})
-    cut = g.reshape(rows, n_dap, rows, width)
-    parts = {
-        0: {r: lax.dynamic_index_in_dim(cut, me ^ r, 1, keepdims=False) for r in range(n_dap)}
-    }
-    for bit in bits_of(n_dap):
-        new = {}
-        for s, cols in parts.items():
-            new[s ^ bit] = {
-                r: swap(cols[r ^ bit], "dap", n_dap, bit) for r in cols if not r & bit
-            }
-        parts = {s: {r: v for r, v in cols.items() if not r & bit} for s, cols in parts.items()}
-        parts.update(new)
+        keep, give = {}, {}
+        for s, c in columns.items():
+            c = c.reshape(rows, -1, 2, bit * rows, width)
+            mine = ((me & bit) > 0).astype(jnp.int32)
+            keep[s] = lax.dynamic_index_in_dim(c, mine, 2, keepdims=False).reshape(rows, -1, width)
+            give[s] = lax.dynamic_index_in_dim(c, 1 - mine, 2, keepdims=False).reshape(
+                rows, -1, width
+            )
+        got = {s ^ bit: swap(b, "dap", n_dap, bit) for s, b in blocks.items()}
+        got_columns = {s ^ bit: swap(c, "dap", n_dap, bit) for s, c in give.items()}
+        got, got_columns = lax.optimization_barrier((got, got_columns))
+        blocks.update(got)
+        columns = {**keep, **got_columns}
     blocks = [blocks[s] for s in range(n_dap)]
-    columns = [parts[s][0] for s in range(n_dap)]
+    columns = [columns[s] for s in range(n_dap)]
 
     half = rows // 2
     tiles = n_dap * half
@@ -461,15 +486,15 @@
             vm((half, width, LANES), BF16),
             vm((half, width, LANES), F32),
             vm((half, 1, LANES), F32),
-            vm((hidden, LANES, LANES), BF16),
-            vm((hidden, LANES, LANES), BF16),
+            vm((hidden, tokens, tokens), BF16),
+            vm((hidden, tokens, tokens), BF16),
             vm((2, hidden * half, LANES), F32),
             vm((half, width, LANES), BF16),
             vm((10, LANES, LANES), F32),
         ],
         compiler_params=pltpu.CompilerParams(vmem_limit_bytes=48 * 1024 * 1024),
     )(
-        me.astype(jnp.int32).reshape(1),
+        place,
         token_mask,
         *blocks,
         g,
@@ -483,31 +508,39 @@
         output_norm_bias.reshape(1, -1),
     )
 
-    total = grads
-    for bit in reversed(bits_of(n_dap)):
-        total = total.reshape(2, -1, LANES)
-        mine = ((me & bit) > 0).astype(jnp.int32)
-        got = swap(pick(total, 1 - mine), "dap", n_dap, bit)
-        total = (pick(total, mine).astype(F32) + got.astype(F32)).astype(BF16)
-    for bit in reversed(bits_of(n_dp)):
-        total = (total.astype(F32) + swap(total, "dp", n_dp, bit).astype(F32)).astype(BF16)
-    for bit in bits_of(n_dap):
-        got = swap(total, "dap", n_dap, bit)
-        first = (me & bit) == 0
-        total = jnp.where(
-            first, jnp.concatenate([total, got]), jnp.concatenate([got, total])
-        )
-    total = total.astype(F32)
-    edges = total[: 4 * LANES].reshape(4, width, hidden).transpose(1, 0, 2).reshape(width, -1)
-    tail = total[6 * LANES :]
-    return (
-        dz[None],
-        edges,
-        total[4 * LANES : 5 * LANES],
-        total[5 * LANES : 6 * LANES],
-        tail[0:2],
-        tail[2:4],
-    )
+    chunks = grads.reshape(n_dap, -1, LANES)
+    total = pick(chunks, me).astype(F32)
+    got = [swap(pick(chunks, me ^ s), "dap", n_dap, s) for s in range(1, n_dap)]
+    for c in got:
+        total = total + c.astype(F32)
+    total = total.astype(BF16)
+    bits = bits_of(n_dp)[::-1]
+    for i in range(0, len(bits), 2):
+        terms = [total.astype(F32)]
+        shifts = [0]
+        for bit in bits[i : i + 2]:
+            shifts += [s ^ bit for s in shifts]
+        terms += [swap(total, "dp", n_dp, s).astype(F32) for s in shifts[1:]]
+        while len(terms) > 1:
+            terms = [p + q for p, q in zip(terms[::2], terms[1::2])]
+        total = terms[0].astype(BF16)
+    parts = [total] + [swap(total, "dap", n_dap, s) for s in range(1, n_dap)]
+    out = lambda *shape: jax.ShapeDtypeStruct(shape, F32)
+    edges, gate, outs, in_norm, out_norm = pl.pallas_call(
+        functools.partial(finish_kernel, n_dap),
+        out_shape=(
+            out(width, 4 * hidden),
+            out(width, width),
+            out(hidden, width),
+            out(2, width),
+            out(2, hidden),
+        ),
+        in_specs=[pl.BlockSpec(memory_space=pltpu.SMEM)]
+        + [pl.BlockSpec(memory_space=pltpu.VMEM)] * n_dap,
+        out_specs=(pl.BlockSpec(memory_space=pltpu.VMEM),) * 5,
+        scratch_shapes=[vm((grad_rows, LANES), F32)],
+    )(place, *parts)
+    return (dz[None], edges, gate, outs, in_norm, out_norm)
 
 
 def solution(mesh):

time: 85.1 us -> 57.3 us (0.67)
  Pallas kernels: 39.4 us -> 17.2 us
  waiting for transfers between devices: 25.3 us -> 22.6 us
  local copies, waits for them, and re-layouts: 3.96 us -> 2.44 us
  starting transfers between devices: 15.2 us -> 14 us
    pallas_call x1, Pallas kernels: 39.4 us -> 15.5 us  [per_device_fused(): pl.pallas_call(functools.partial(fused_kernel, n_dap), out_shape=(jax.Sha...]
    ppermute x14 -> x16, waiting for transfers between devices: 25.3 us -> 22.6 us  [swap(): return lax.ppermute(x, axis, [(i, i ^ bit) for i in range(n)])]
    pallas_call x0 -> x1, Pallas kernels: none -> 1.67 us  [per_device_fused(): pl.pallas_call(functools.partial(finish_kernel, n_dap), out_shape=(out(wi...]
    slice x3 -> x0, local copies, waits for them, and re-layouts: 1.25 us -> none  [the longest x1 0.66 us: per_device_fused(): total[5 * LANES:6 * LANES]]
    ppermute x14 -> x16, starting transfers between devices: 15.2 us -> 14 us  [swap(): return lax.ppermute(x, axis, [(i, i ^ bit) for i in range(n)])]
    dynamic_slice x0 -> x1, local copies, waits for them, and re-layouts: none -> 1.03 us  [per_device_fused(): lax.dynamic_index_in_dim(c, mine, 2, keepdims=False)]
    squeeze x1 -> x0, local copies, waits for them, and re-layouts: 1.03 us -> none  [per_device_fused(): lax.dynamic_index_in_dim(cut, me ^ r, 1, keepdims=False)]
  transfers between devices with their start and end apart: 14 -> 16, of which waited for: 10 -> 11; matrix products, arithmetic and copies ran while one was open for 1% -> 2% of each run, Pallas kernels for 0% -> 0%
where the time goes in v2:
time: 57.3 us; the launch traced here: 57.1 us
  waiting for transfers between devices  22.6 us (39%)
  Pallas kernels  17.2 us (30%)
  starting transfers between devices  14 us (24%)
  local copies, waits for them, and re-layouts  2.44 us (4%)
  between operations  0.78 us (1%)
    ppermute x16, waiting for transfers between devices, swap(): return lax.ppermute(x, axis, [(i, i ^ bit) for i in range(n)])  22.6 us
    pallas_call x1, Pallas kernels, per_device_fused(): pl.pallas_call(functools.partial(fused_kernel, n_dap), out_shape=(jax.Sha...  15.5 us
    ppermute x16, starting transfers between devices, swap(): return lax.ppermute(x, axis, [(i, i ^ bit) for i in range(n)])  14 us
    pallas_call x1, Pallas kernels, per_device_fused(): pl.pallas_call(functools.partial(finish_kernel, n_dap), out_shape=(out(wi...  1.67 us
    unnamed x28, local copies, waits for them, and re-layouts  1.37 us
  transfers between devices with their start and end apart: 16, of which 11 were waited for; matrix products, arithmetic and copies ran while one was open for 2% of the time, Pallas kernels for 0%

profile of v2, /device:TPU:0, one launch (start us, length us, event | category | flops | bytes accessed | tf_op | source)
XLA Modules:
  0.0 57.1 jit_solution(17475873565417898038)
XLA Ops:
  0.6 3.0 %collective-permute-start.1 = (bf16[16,64,128]{2,1,0:T(8,128)(2,1)}, bf16[16,64,128]{2,1,0:T(8,128)(2,1)S(1)}, u32[]{:S(2)}, u32[]{:S(2)}) collective-permute-start(bf16[16,64,128]{2,1,0:T(8,128)(2,1)} %bitcast.33), channel_id=1, source_target_pairs={{0,2},{1,3},{2,0},{3,1},{4,6},{5,7},{6,4},{7,5},{8,10},{9,11},{10,... | collective-permute-start | bytes 786440 | tf_op jit(solution)/shard_map/ppermute | solution.py:407
  3.7 1.0 %constant_dynamic-slice_fusion = (bf16[16,1,1,32,128]{4,3,2,0,1:T(8,128)(2,1)S(1)}, bf16[16,32,128]{2,1,0:T(8,128)(2,1)S(1)}) fusion(bf16[16,1,2,32,128]{4,3,2,0,1:T(8,128)(2,1)} %bitcast.31, s32[]{:T(128)S(6)} %select_n.30, s32[]{:T(128)S(6)} %select_n.29), kind=kLoop, calls=%fused_computation.14 | loop fusion | bytes 524296 | tf_op jit(solution)/shard_map/jit(dynamic_index_in_dim)/dynamic_slice | solution.py:447
  4.7 0.1 collective-permute-start.2
  4.8 0.0 copy-done.1
  4.8 0.1 collective-permute-start
  4.9 8.1 %collective-permute-done.2 = bf16[16,32,128]{2,1,0:T(8,128)(2,1)S(1)} collective-permute-done((bf16[16,32,128]{2,1,0:T(8,128)(2,1)S(1)}, bf16[16,32,128]{2,1,0:T(8,128)(2,1)S(1)}, u32[]{:S(2)}, u32[]{:S(2)}) %collective-permute-start.2) | collective-permute-done | bytes 131104 | tf_op jit(solution)/shard_map/ppermute | solution.py:407
  13.0 0.0 collective-permute-done.1.refs_2_
  13.0 0.0 collective-permute-start.3
  13.0 0.6 collective-permute-start.4
  13.6 0.0 copy-start.3
  13.6 0.1 collective-permute-start.5
  13.7 0.9 %collective-permute-done.4.refs_6_ = bf16[16,16,128]{2,1,0:T(8,128)(2,1)S(1)} collective-permute-done((bf16[16,16,128]{2,1,0:T(8,128)(2,1)S(1)}, bf16[16,16,128]{2,1,0:T(8,128)(2,1)S(1)}, u32[]{:S(2)}, u32[]{:S(2)}) %collective-permute-start.4) | collective-permute-done | bytes 65568 | tf_op jit(solution)/shard_map/ppermute | solution.py:407
  14.6 0.0 collective-permute-done.refs_1_
  14.6 0.3 collective-permute-done.5.refs_8_
  14.9 0.0 collective-permute-done.3.refs_3_
  14.9 0.0 copy-start.6
  15.0 0.0 copy-start.7
  15.0 0.0 copy-done
  15.0 0.0 copy-done.2
  15.0 0.6 %copy-done.8 = f32[128]{0:T(128)S(1)} copy-done((f32[128]{0:T(128)S(1)}, f32[128]{0:T(128)}, u32[]{:S(2)}) %copy-start.8) | copy-done | bytes 536
  15.6 0.0 copy-done.9
  15.6 0.0 copy-done.5
  15.6 0.0 copy-done.6
  15.6 0.0 copy-done.7
  15.7 15.5 %shard_map.145 = (bf16[16,64,128]{2,1,0:T(8,128)(2,1)}, bf16[832,128]{1,0:T(8,128)(2,1)S(1)}) custom-call(s32[1]{0:T(128)} %bitcast.me_ref, s32[1,64]{1,0:T(1,128)S(1)} %copy-done.5, bf16[16,64,128]{2,1,0:T(8,128)(2,1)S(1)} %bitcast.35, bf16[16,64,128]{2,1,0:T(8,128)(2,1)S(1)} %collective-permute-done.refs_1_, ...), custom_call_target="tpu_custom_call" | custom-call | tf_op jit(solution)/shard_map/pallas_call | solution.py:463
  31.2 0.3 collective-permute-start.6
  31.5 1.7 %collective-permute-start.7 = (bf16[208,128]{1,0:T(8,128)(2,1)S(1)}, bf16[208,128]{1,0:T(8,128)(2,1)S(1)}, u32[]{:S(2)}, u32[]{:S(2)}) collective-permute-start(bf16[208,128]{1,0:T(8,128)(2,1)S(1)} %get-tuple-element.36), channel_id=1, source_target_pairs={{0,2},{1,3},{2,0},{3,1},{4,6},{5,7},{6,4},{7,5},{8,10},{9,11},{10,... | collective-permute-start | bytes 159752 | tf_op jit(solution)/shard_map/ppermute | solution.py:407
  33.2 0.0 collective-permute-start.8
  33.2 0.0 collective-permute-done.6
  33.2 2.4 %collective-permute-done.7 = bf16[208,128]{1,0:T(8,128)(2,1)S(1)} collective-permute-done((bf16[208,128]{1,0:T(8,128)(2,1)S(1)}, bf16[208,128]{1,0:T(8,128)(2,1)S(1)}, u32[]{:S(2)}, u32[]{:S(2)}) %collective-permute-start.7) | collective-permute-done | bytes 53280 | tf_op jit(solution)/shard_map/ppermute | solution.py:407
  35.6 1.5 %collective-permute-done.8 = bf16[208,128]{1,0:T(8,128)(2,1)S(1)} collective-permute-done((bf16[208,128]{1,0:T(8,128)(2,1)S(1)}, bf16[208,128]{1,0:T(8,128)(2,1)S(1)}, u32[]{:S(2)}, u32[]{:S(2)}) %collective-permute-start.8) | collective-permute-done | bytes 53280 | tf_op jit(solution)/shard_map/ppermute | solution.py:407
  37.1 1.6 %collective-permute-start.10 = (bf16[208,128]{1,0:T(8,128)(2,1)S(1)}, bf16[208,128]{1,0:T(8,128)(2,1)S(1)}, u32[]{:S(2)}, u32[]{:S(2)}) collective-permute-start(bf16[208,128]{1,0:T(8,128)(2,1)S(1)} %fusion.2), channel_id=1, source_target_pairs={{0,8},{4,12},{8,0},{12,4},{16,24},{20,28},{24,16},{28,20},{1,9},{5... | collective-permute-start | bytes 159752 | tf_op jit(solution)/shard_map/ppermute | solution.py:407
  38.8 1.4 %collective-permute-start.11 = (bf16[208,128]{1,0:T(8,128)(2,1)S(1)}, bf16[208,128]{1,0:T(8,128)(2,1)S(1)}, u32[]{:S(2)}, u32[]{:S(2)}) collective-permute-start(bf16[208,128]{1,0:T(8,128)(2,1)S(1)} %fusion.2), channel_id=1, source_target_pairs={{0,12},{4,8},{8,4},{12,0},{16,28},{20,24},{24,20},{28,16},{1,13},{... | collective-permute-start | bytes 159752 | tf_op jit(solution)/shard_map/ppermute | solution.py:407
  40.1 0.5 collective-permute-start.9
  40.7 0.6 %collective-permute-done.10 = bf16[208,128]{1,0:T(8,128)(2,1)S(1)} collective-permute-done((bf16[208,128]{1,0:T(8,128)(2,1)S(1)}, bf16[208,128]{1,0:T(8,128)(2,1)S(1)}, u32[]{:S(2)}, u32[]{:S(2)}) %collective-permute-start.10) | collective-permute-done | bytes 53280 | tf_op jit(solution)/shard_map/ppermute | solution.py:407
  41.3 2.5 %collective-permute-done.11 = bf16[208,128]{1,0:T(8,128)(2,1)S(1)} collective-permute-done((bf16[208,128]{1,0:T(8,128)(2,1)S(1)}, bf16[208,128]{1,0:T(8,128)(2,1)S(1)}, u32[]{:S(2)}, u32[]{:S(2)}) %collective-permute-start.11) | collective-permute-done | bytes 53280 | tf_op jit(solution)/shard_map/ppermute | solution.py:407
  43.8 0.6 %collective-permute-done.9 = bf16[208,128]{1,0:T(8,128)(2,1)S(1)} collective-permute-done((bf16[208,128]{1,0:T(8,128)(2,1)S(1)}, bf16[208,128]{1,0:T(8,128)(2,1)S(1)}, u32[]{:S(2)}, u32[]{:S(2)}) %collective-permute-start.9) | collective-permute-done | bytes 53280 | tf_op jit(solution)/shard_map/ppermute | solution.py:407
  44.5 2.6 %collective-permute-start.12 = (bf16[208,128]{1,0:T(8,128)(2,1)S(1)}, bf16[208,128]{1,0:T(8,128)(2,1)S(1)}, u32[]{:S(2)}, u32[]{:S(2)}) collective-permute-start(bf16[208,128]{1,0:T(8,128)(2,1)S(1)} %add_convert_fusion.1), channel_id=1, source_target_pairs={{0,16},{4,20},{8,24},{12,28},{16,0},{20,4},{24,8},{28,12},{1,17},{... | collective-permute-start | bytes 159752 | tf_op jit(solution)/shard_map/ppermute | solution.py:407
  47.1 2.4 %collective-permute-done.12 = bf16[208,128]{1,0:T(8,128)(2,1)S(1)} collective-permute-done((bf16[208,128]{1,0:T(8,128)(2,1)S(1)}, bf16[208,128]{1,0:T(8,128)(2,1)S(1)}, u32[]{:S(2)}, u32[]{:S(2)}) %collective-permute-start.12) | collective-permute-done | bytes 53280 | tf_op jit(solution)/shard_map/ppermute | solution.py:407
  49.6 0.1 collective-permute-start.13
  49.7 1.0 %collective-permute-start.14 = (bf16[208,128]{1,0:T(8,128)(2,1)S(1)}, bf16[208,128]{1,0:T(8,128)(2,1)S(1)}, u32[]{:S(2)}, u32[]{:S(2)}) collective-permute-start(bf16[208,128]{1,0:T(8,128)(2,1)S(1)} %add_convert_fusion.refs_0_), channel_id=1, source_target_pairs={{0,2},{1,3},{2,0},{3,1},{4,6},{5,7},{6,4},{7,5},{8,10},{9,11},{10,... | collective-permute-start | bytes 159752 | tf_op jit(solution)/shard_map/ppermute | solution.py:407
  50.7 0.8 %collective-permute-start.15 = (bf16[208,128]{1,0:T(8,128)(2,1)S(1)}, bf16[208,128]{1,0:T(8,128)(2,1)S(1)}, u32[]{:S(2)}, u32[]{:S(2)}) collective-permute-start(bf16[208,128]{1,0:T(8,128)(2,1)S(1)} %add_convert_fusion.refs_0_), channel_id=1, source_target_pairs={{0,3},{1,2},{2,1},{3,0},{4,7},{5,6},{6,5},{7,4},{8,11},{9,10},{10,... | collective-permute-start | bytes 159752 | tf_op jit(solution)/shard_map/ppermute | solution.py:407
  51.5 0.0 collective-permute-done.13.refs_1_
  51.5 2.7 %collective-permute-done.14.refs_2_ = bf16[208,128]{1,0:T(8,128)(2,1)S(1)} collective-permute-done((bf16[208,128]{1,0:T(8,128)(2,1)S(1)}, bf16[208,128]{1,0:T(8,128)(2,1)S(1)}, u32[]{:S(2)}, u32[]{:S(2)}) %collective-permute-start.14) | collective-permute-done | bytes 53280 | tf_op jit(solution)/shard_map/ppermute | solution.py:407
  54.2 0.5 collective-permute-done.15.refs_3_
  54.8 0.1 copy-done.12
  54.8 0.6 %copy-done.13 = bf16[208,128]{1,0:T(8,128)(2,1)} copy-done((bf16[208,128]{1,0:T(8,128)(2,1)}, bf16[208,128]{1,0:T(8,128)(2,1)S(1)}, u32[]{:S(2)}) %copy-start.13) | copy-done | bytes 53272
  55.4 1.7 %shard_map.146 = (f32[128,512]{1,0:T(8,128)}, f32[128,128]{1,0:T(8,128)}, f32[128,128]{1,0:T(8,128)}, f32[2,128]{1,0:T(2,128)}, f32[2,128]{1,0:T(2,128)}) custom-call(s32[1]{0:T(128)} %bitcast.me_ref, bf16[208,128]{1,0:T(8,128)(2,1)} %copy-done.10, bf16[208,128]{1,0:T(8,128)(2,1)} %copy-done.11, bf16[208,128]{1,0:T(8,128)(2,1)} %copy-done.12, ...), custom_call_target="tpu_custom_call" | custom-call | tf_op jit(solution)/shard_map/pallas_call | solution.py:529
  (21 shorter events, 0.2 us)
Async XLA Ops:
  0.6 12.4 %collective-permute-start.1 = (bf16[16,64,128]{2,1,0:T(8,128)(2,1)}, bf16[16,64,128]{2,1,0:T(8,128)(2,1)S(1)}, u32[]{:S(2)}, u32[]{:S(2)}) collective-permute-start(bf16[16,64,128]{2,1,0:T(8,128)(2,1)} %bitcast.33), channel_id=1, source_target_pairs={{0,2},{1,3},{2,0},{3,1},{4,6},{5,7},{6,4},{7,5},{8,10},{9,11},{10,... | collective-permute-start | bytes 786440 | tf_op jit(solution)/shard_map/ppermute | solution.py:407
  3.7 1.1 %copy-start.1 = (bf16[1,16,64,128]{3,2,1,0:T(8,128)(2,1)S(1)}, bf16[1,16,64,128]{3,2,1,0:T(8,128)(2,1)}, u32[]{:S(2)}) copy-start(bf16[1,16,64,128]{3,2,1,0:T(8,128)(2,1)} %param.10) | copy-start | bytes 786436
  4.7 8.3 %collective-permute-start.2 = (bf16[16,32,128]{2,1,0:T(8,128)(2,1)S(1)}, bf16[16,32,128]{2,1,0:T(8,128)(2,1)S(1)}, u32[]{:S(2)}, u32[]{:S(2)}) collective-permute-start(bf16[16,32,128]{2,1,0:T(8,128)(2,1)S(1)} %get-tuple-element.33), channel_id=1, source_target_pairs={{0,2},{1,3},{2,0},{3,1},{4,6},{5,7},{6,4},{7,5},{8,10},{9,11},{10,... | collective-permute-start | bytes 393224 | tf_op jit(solution)/shard_map/ppermute | solution.py:407
  4.8 9.8 %collective-permute-start = (bf16[16,64,128]{2,1,0:T(8,128)(2,1)S(1)}, bf16[16,64,128]{2,1,0:T(8,128)(2,1)S(1)}, u32[]{:S(2)}, u32[]{:S(2)}) collective-permute-start(bf16[16,64,128]{2,1,0:T(8,128)(2,1)S(1)} %bitcast.34), channel_id=1, source_target_pairs={{0,1},{1,0},{2,3},{3,2},{4,5},{5,4},{6,7},{7,6},{8,9},{9,8},{10,11... | collective-permute-start | bytes 786440 | tf_op jit(solution)/shard_map/ppermute | solution.py:407
  13.0 1.9 %collective-permute-start.3 = (bf16[16,64,128]{2,1,0:T(8,128)(2,1)S(1)}, bf16[16,64,128]{2,1,0:T(8,128)(2,1)S(1)}, u32[]{:S(2)}, u32[]{:S(2)}) collective-permute-start(bf16[16,64,128]{2,1,0:T(8,128)(2,1)S(1)} %collective-permute-done.1.refs_2_), channel_id=1, source_target_pairs={{0,1},{1,0},{2,3},{3,2},{4,5},{5,4},{6,7},{7,6},{8,9},{9,8},{10,11... | collective-permute-start | bytes 786440 | tf_op jit(solution)/shard_map/ppermute | solution.py:407
  13.0 2.0 %copy-start = (bf16[1,16,64,128]{3,2,1,0:T(8,128)(2,1)S(1)}, bf16[1,16,64,128]{3,2,1,0:T(8,128)(2,1)}, u32[]{:S(2)}) copy-start(bf16[1,16,64,128]{3,2,1,0:T(8,128)(2,1)} %param.11) | copy-start | bytes 786436
  13.0 1.6 %collective-permute-start.4 = (bf16[16,16,128]{2,1,0:T(8,128)(2,1)S(1)}, bf16[16,16,128]{2,1,0:T(8,128)(2,1)S(1)}, u32[]{:S(2)}, u32[]{:S(2)}) collective-permute-start(bf16[16,16,128]{2,1,0:T(8,128)(2,1)S(1)} %get-tuple-element.40), channel_id=1, source_target_pairs={{0,1},{1,0},{2,3},{3,2},{4,5},{5,4},{6,7},{7,6},{8,9},{9,8},{10,11... | collective-permute-start | bytes 196616 | tf_op jit(solution)/shard_map/ppermute | solution.py:407
  13.6 1.4 %copy-start.2 = (bf16[128,512]{1,0:T(8,128)(2,1)S(1)}, bf16[128,512]{1,0:T(8,128)(2,1)}, u32[]{:S(2)}) copy-start(bf16[128,512]{1,0:T(8,128)(2,1)} %refs_9_.1) | copy-start | bytes 393220
  13.6 1.4 %copy-start.4 = (bf16[128,128]{1,0:T(8,128)(2,1)S(1)}, bf16[128,128]{1,0:T(8,128)(2,1)}, u32[]{:S(2)}) copy-start(bf16[128,128]{1,0:T(8,128)(2,1)} %refs_11_.1) | copy-start | bytes 98308
  13.6 1.4 %copy-start.3 = (bf16[128,128]{1,0:T(8,128)(2,1)S(1)}, bf16[128,128]{1,0:T(8,128)(2,1)}, u32[]{:S(2)}) copy-start(bf16[128,128]{1,0:T(8,128)(2,1)} %refs_10_.1) | copy-start | bytes 98308
  13.6 1.3 %collective-permute-start.5 = (bf16[16,16,128]{2,1,0:T(8,128)(2,1)S(1)}, bf16[16,16,128]{2,1,0:T(8,128)(2,1)S(1)}, u32[]{:S(2)}, u32[]{:S(2)}) collective-permute-start(bf16[16,16,128]{2,1,0:T(8,128)(2,1)S(1)} %get-tuple-element.38), channel_id=1, source_target_pairs={{0,1},{1,0},{2,3},{3,2},{4,5},{5,4},{6,7},{7,6},{8,9},{9,8},{10,11... | collective-permute-start | bytes 196616 | tf_op jit(solution)/shard_map/ppermute | solution.py:407
  14.9 0.7 %copy-start.8 = (f32[128]{0:T(128)S(1)}, f32[128]{0:T(128)}, u32[]{:S(2)}) copy-start(f32[128]{0:T(128)} %param.18) | copy-start | bytes 1540
  14.9 0.7 %copy-start.9 = (f32[128]{0:T(128)S(1)}, f32[128]{0:T(128)}, u32[]{:S(2)}) copy-start(f32[128]{0:T(128)} %param.19) | copy-start | bytes 1540
  14.9 0.7 %copy-start.5 = (s32[1,64]{1,0:T(1,128)S(1)}, s32[1,64]{1,0:T(1,128)}, u32[]{:S(2)}) copy-start(s32[1,64]{1,0:T(1,128)} %mask_ref.1) | copy-start | bytes 772
  14.9 0.7 %copy-start.6 = (f32[128]{0:T(128)S(1)}, f32[128]{0:T(128)}, u32[]{:S(2)}) copy-start(f32[128]{0:T(128)} %param.16) | copy-start | bytes 1540
  15.0 0.7 %copy-start.7 = (f32[128]{0:T(128)S(1)}, f32[128]{0:T(128)}, u32[]{:S(2)}) copy-start(f32[128]{0:T(128)} %param.17) | copy-start | bytes 1540
  31.2 2.0 %collective-permute-start.6 = (bf16[208,128]{1,0:T(8,128)(2,1)S(1)}, bf16[208,128]{1,0:T(8,128)(2,1)S(1)}, u32[]{:S(2)}, u32[]{:S(2)}) collective-permute-start(bf16[208,128]{1,0:T(8,128)(2,1)S(1)} %get-tuple-element.34), channel_id=1, source_target_pairs={{0,1},{1,0},{2,3},{3,2},{4,5},{5,4},{6,7},{7,6},{8,9},{9,8},{10,11... | collective-permute-start | bytes 159752 | tf_op jit(solution)/shard_map/ppermute | solution.py:407
  31.5 4.1 %collective-permute-start.7 = (bf16[208,128]{1,0:T(8,128)(2,1)S(1)}, bf16[208,128]{1,0:T(8,128)(2,1)S(1)}, u32[]{:S(2)}, u32[]{:S(2)}) collective-permute-start(bf16[208,128]{1,0:T(8,128)(2,1)S(1)} %get-tuple-element.36), channel_id=1, source_target_pairs={{0,2},{1,3},{2,0},{3,1},{4,6},{5,7},{6,4},{7,5},{8,10},{9,11},{10,... | collective-permute-start | bytes 159752 | tf_op jit(solution)/shard_map/ppermute | solution.py:407
  33.2 3.9 %collective-permute-start.8 = (bf16[208,128]{1,0:T(8,128)(2,1)S(1)}, bf16[208,128]{1,0:T(8,128)(2,1)S(1)}, u32[]{:S(2)}, u32[]{:S(2)}) collective-permute-start(bf16[208,128]{1,0:T(8,128)(2,1)S(1)} %get-tuple-element.35), channel_id=1, source_target_pairs={{0,3},{1,2},{2,1},{3,0},{4,7},{5,6},{6,5},{7,4},{8,11},{9,10},{10,... | collective-permute-start | bytes 159752 | tf_op jit(solution)/shard_map/ppermute | solution.py:407
  37.1 4.2 %collective-permute-start.10 = (bf16[208,128]{1,0:T(8,128)(2,1)S(1)}, bf16[208,128]{1,0:T(8,128)(2,1)S(1)}, u32[]{:S(2)}, u32[]{:S(2)}) collective-permute-start(bf16[208,128]{1,0:T(8,128)(2,1)S(1)} %fusion.2), channel_id=1, source_target_pairs={{0,8},{4,12},{8,0},{12,4},{16,24},{20,28},{24,16},{28,20},{1,9},{5... | collective-permute-start | bytes 159752 | tf_op jit(solution)/shard_map/ppermute | solution.py:407
  38.8 5.1 %collective-permute-start.11 = (bf16[208,128]{1,0:T(8,128)(2,1)S(1)}, bf16[208,128]{1,0:T(8,128)(2,1)S(1)}, u32[]{:S(2)}, u32[]{:S(2)}) collective-permute-start(bf16[208,128]{1,0:T(8,128)(2,1)S(1)} %fusion.2), channel_id=1, source_target_pairs={{0,12},{4,8},{8,4},{12,0},{16,28},{20,24},{24,20},{28,16},{1,13},{... | collective-permute-start | bytes 159752 | tf_op jit(solution)/shard_map/ppermute | solution.py:407
  40.1 4.3 %collective-permute-start.9 = (bf16[208,128]{1,0:T(8,128)(2,1)S(1)}, bf16[208,128]{1,0:T(8,128)(2,1)S(1)}, u32[]{:S(2)}, u32[]{:S(2)}) collective-permute-start(bf16[208,128]{1,0:T(8,128)(2,1)S(1)} %fusion.2), channel_id=1, source_target_pairs={{0,4},{4,0},{8,12},{12,8},{16,20},{20,16},{24,28},{28,24},{1,5},{5... | collective-permute-start | bytes 159752 | tf_op jit(solution)/shard_map/ppermute | solution.py:407
  44.5 5.1 %collective-permute-start.12 = (bf16[208,128]{1,0:T(8,128)(2,1)S(1)}, bf16[208,128]{1,0:T(8,128)(2,1)S(1)}, u32[]{:S(2)}, u32[]{:S(2)}) collective-permute-start(bf16[208,128]{1,0:T(8,128)(2,1)S(1)} %add_convert_fusion.1), channel_id=1, source_target_pairs={{0,16},{4,20},{8,24},{12,28},{16,0},{20,4},{24,8},{28,12},{1,17},{... | collective-permute-start | bytes 159752 | tf_op jit(solution)/shard_map/ppermute | solution.py:407
  49.6 5.2 %copy-start.10 = (bf16[208,128]{1,0:T(8,128)(2,1)}, bf16[208,128]{1,0:T(8,128)(2,1)S(1)}, u32[]{:S(2)}) copy-start(bf16[208,128]{1,0:T(8,128)(2,1)S(1)} %add_convert_fusion.refs_0_) | copy-start | bytes 159748
  49.6 1.9 %collective-permute-start.13 = (bf16[208,128]{1,0:T(8,128)(2,1)S(1)}, bf16[208,128]{1,0:T(8,128)(2,1)S(1)}, u32[]{:S(2)}, u32[]{:S(2)}) collective-permute-start(bf16[208,128]{1,0:T(8,128)(2,1)S(1)} %add_convert_fusion.refs_0_), channel_id=1, source_target_pairs={{0,1},{1,0},{2,3},{3,2},{4,5},{5,4},{6,7},{7,6},{8,9},{9,8},{10,11... | collective-permute-start | bytes 159752 | tf_op jit(solution)/shard_map/ppermute | solution.py:407
  49.7 4.5 %collective-permute-start.14 = (bf16[208,128]{1,0:T(8,128)(2,1)S(1)}, bf16[208,128]{1,0:T(8,128)(2,1)S(1)}, u32[]{:S(2)}, u32[]{:S(2)}) collective-permute-start(bf16[208,128]{1,0:T(8,128)(2,1)S(1)} %add_convert_fusion.refs_0_), channel_id=1, source_target_pairs={{0,2},{1,3},{2,0},{3,1},{4,6},{5,7},{6,4},{7,5},{8,10},{9,11},{10,... | collective-permute-start | bytes 159752 | tf_op jit(solution)/shard_map/ppermute | solution.py:407
  50.7 4.0 %collective-permute-start.15 = (bf16[208,128]{1,0:T(8,128)(2,1)S(1)}, bf16[208,128]{1,0:T(8,128)(2,1)S(1)}, u32[]{:S(2)}, u32[]{:S(2)}) collective-permute-start(bf16[208,128]{1,0:T(8,128)(2,1)S(1)} %add_convert_fusion.refs_0_), channel_id=1, source_target_pairs={{0,3},{1,2},{2,1},{3,0},{4,7},{5,6},{6,5},{7,4},{8,11},{9,10},{10,... | collective-permute-start | bytes 159752 | tf_op jit(solution)/shard_map/ppermute | solution.py:407
  51.5 3.2 %copy-start.11 = (bf16[208,128]{1,0:T(8,128)(2,1)}, bf16[208,128]{1,0:T(8,128)(2,1)S(1)}, u32[]{:S(2)}) copy-start(bf16[208,128]{1,0:T(8,128)(2,1)S(1)} %collective-permute-done.13.refs_1_) | copy-start | bytes 159748
  54.2 0.6 %copy-start.12 = (bf16[208,128]{1,0:T(8,128)(2,1)}, bf16[208,128]{1,0:T(8,128)(2,1)S(1)}, u32[]{:S(2)}) copy-start(bf16[208,128]{1,0:T(8,128)(2,1)S(1)} %collective-permute-done.14.refs_2_) | copy-start | bytes 159748
  54.8 0.6 %copy-start.13 = (bf16[208,128]{1,0:T(8,128)(2,1)}, bf16[208,128]{1,0:T(8,128)(2,1)S(1)}, u32[]{:S(2)}) copy-start(bf16[208,128]{1,0:T(8,128)(2,1)S(1)} %collective-permute-done.15.refs_3_) | copy-start | bytes 159748

commit v3 on v2

--- a/solution.py
+++ b/solution.py
@@ -9,6 +9,7 @@
 
 EPS = 1e-05
 LANES = 128
+VMEM_BYTES = 32 * 1024 * 1024
 F32 = jnp.float32
 BF16 = jnp.bfloat16
 
@@ -191,137 +192,243 @@
     return jnp.concatenate([x[:8], x[8:]], axis=1)
 
 
-def square(tiles):
+def square(blocks):
     n = LANES // 2
-    parts = []
-    for a in range(tiles.shape[0] // 8):
-        x = tiles[8 * a : 8 * a + 8]
-        parts += [x[:, :n], x[:, n:]]
-    return jnp.concatenate(parts, axis=0).astype(BF16)
-
-
-def fused_kernel(
-    n_blocks,
+    return jnp.concatenate([p for x in blocks for p in (x[:, :n], x[:, n:])], axis=0).astype(BF16)
+
+
+def columns_of(ref):
+    return jnp.broadcast_to(ref[...], (ref.shape[1], LANES)).T
+
+
+def transposed(ref):
+    return ref[...].astype(F32).T.astype(BF16)
+
+
+def fill_pair_mask(mask_ref, pm, rows):
+    half = rows // 2
+    low = lax.broadcasted_iota(jnp.int32, (half, LANES), 1) < LANES // 2
+    m = mask_ref[...].astype(F32)
+    m = jnp.broadcast_to(jnp.concatenate([m, m], axis=1), (LANES, LANES))
+    mt = m.T
+    for a in range(pm.shape[0] // half):
+        lo = mt[rows * a : rows * a + half]
+        hi = mt[rows * a + half : rows * (a + 1)]
+        pm[half * a : half * (a + 1), :] = jnp.where(low, lo, hi) * m[:half]
+
+
+def two_rows(ref, t):
+    half = ref.shape[0] // 2
+    return jnp.concatenate([ref[t].astype(F32), ref[t + half].astype(F32)], axis=0).T
+
+
+def edge_tile(pair_ref, t, block, place, weT, vec, pm, ls, rs):
+    half = pair_ref.shape[0] // 2
+    hidden = weT.shape[0] // 4
+    zhat, rstd = norm_columns(two_rows(pair_ref, t))
+    zn = (zhat * vec[0] + vec[1]).astype(BF16)
+    pre = dot(weT[...], zn)
+    mask = pm[pl.ds(block * half + t, 1), :]
+    ls[place, pl.ds(t, hidden, stride=half), :] = (
+        mask * jax.nn.sigmoid(pre[:hidden]) * pre[hidden : 2 * hidden]
+    )
+    rs[place, pl.ds(t, hidden, stride=half), :] = (
+        mask * jax.nn.sigmoid(pre[2 * hidden : 3 * hidden]) * pre[3 * hidden :]
+    )
+    return zhat, rstd, zn, pre
+
+
+def near_kernel(
     me_ref,
+    near_ref,
+    mask_hbm,
+    own_hbm,
+    we_hbm,
+    gain_hbm,
+    bias_hbm,
+    weT,
+    ls,
+    rs,
+    pre_own,
+    zn_own,
+    zhat_own,
+    rstd_own,
+    vec,
+    pm,
     mask_ref,
-    *refs,
+    own_ref,
+    we_ref,
+    gain_ref,
+    bias_ref,
+    sems,
 ):
-    pair_refs = refs[:n_blocks]
-    pg_ref = refs[n_blocks]
-    pgt_refs = refs[n_blocks + 1 : 2 * n_blocks + 1]
-    (
-        we_ref,
-        wg_ref,
-        wo_ref,
-        gain_ref,
-        bias_ref,
-        ogain_ref,
-        obias_ref,
-        dz_ref,
-        grads_ref,
-        weT,
-        wgT,
-        woT,
-        vec,
-        pm,
-        xall,
-        pgs,
-        ls,
-        rs,
-        pre_own,
-        zn_own,
-        zhat_own,
-        rstd_own,
-        bdl,
-        bdr,
-        pr,
-        dgl_own,
-        gacc,
-    ) = refs[2 * n_blocks + 1 :]
     me = me_ref[0]
-    rows, tokens, width = pair_refs[0].shape
+    copies = [
+        pltpu.make_async_copy(src, dst, sems.at[i])
+        for i, (src, dst) in enumerate(
+            (
+                (we_hbm, we_ref),
+                (own_hbm, own_ref),
+                (mask_hbm, mask_ref),
+                (gain_hbm, gain_ref),
+                (bias_hbm, bias_ref),
+            )
+        )
+    ]
+    for copy in copies:
+        copy.start()
+    for copy in copies:
+        copy.wait()
+    rows = own_ref.shape[0]
     half = rows // 2
-    tiles = n_blocks * half
-    hidden = wo_ref.shape[0]
-    f = lambda v: v.astype(F32)
-
+    hidden = we_ref.shape[1] // 4
     for b in range(4):
         cols = slice(b * hidden, (b + 1) * hidden)
-        weT[cols, :] = f(we_ref[:, cols]).T.astype(BF16)
-    wgT[...] = f(wg_ref[...]).T.astype(BF16)
-    woT[...] = f(wo_ref[...]).T.astype(BF16)
-    for b, r in enumerate((gain_ref, bias_ref, ogain_ref, obias_ref)):
-        vec[b] = jnp.broadcast_to(r[...], (width, LANES)).T
-    low = lax.broadcasted_iota(jnp.int32, (8, LANES), 1) < LANES // 2
-    m = f(mask_ref[...])
-    m = jnp.broadcast_to(jnp.concatenate([m, m], axis=1), (LANES, LANES))
-    mt = m.T
-    for a in range(n_blocks):
-        lo = mt[rows * a : rows * a + half]
-        hi = mt[rows * a + half : rows * (a + 1)]
-        pm[half * a : half * (a + 1), :] = jnp.where(low, lo, hi) * m[:8]
-    gacc[...] = jnp.zeros_like(gacc)
-
-    for s in range(n_blocks):
-        a = jnp.bitwise_xor(me, s)
+        weT[cols, :] = we_ref[:, cols].astype(F32).T.astype(BF16)
+    vec[0] = columns_of(gain_ref)
+    vec[1] = columns_of(bias_ref)
+    fill_pair_mask(mask_ref, pm, rows)
+    for s, ref in enumerate((own_ref, near_ref)):
+        block = jnp.bitwise_xor(me, s)
+        place = jnp.bitwise_and(block, 1)
 
         @pl.loop(0, half, unroll=8)
-        def _(t, s=s, a=a):
-            lo = f(pair_refs[s][t])
-            hi = f(pair_refs[s][t + half])
-            at = pl.multiple_of((a * rows + t) * tokens, tokens)
-            xall[pl.ds(at, tokens), :] = lo
-            xall[pl.ds(at + half * tokens, tokens), :] = hi
-            zhat, rstd = norm_columns(jnp.concatenate([lo, hi], axis=0).T)
-            zn = (zhat * vec[0] + vec[1]).astype(BF16)
-            pre = dot(weT[...], zn)
-            mask = pm[pl.ds(a * half + t, 1), :]
-            left = mask * jax.nn.sigmoid(pre[:hidden]) * pre[hidden : 2 * hidden]
-            right = mask * jax.nn.sigmoid(pre[2 * hidden : 3 * hidden]) * pre[3 * hidden :]
-            ls[pl.ds(a * half + t, hidden, stride=tiles), :] = left
-            rs[pl.ds(a * half + t, hidden, stride=tiles), :] = right
+        def _(t, s=s, ref=ref, block=block, place=place):
+            zhat, rstd, zn, pre = edge_tile(ref, t, block, place, weT, vec, pm, ls, rs)
             if s == 0:
                 pre_own[t] = pre
                 zn_own[t] = zn
                 zhat_own[t] = zhat
                 rstd_own[t] = rstd
 
-        pgs[pl.ds(pl.multiple_of(a * rows * rows, rows), rows * rows), :] = f(
-            pgt_refs[s][...].reshape(rows * rows, width)
-        )
+
+def product_kernel(
+    me_ref,
+    mask_ref,
+    pair0,
+    pair1,
+    pair2,
+    pair3,
+    weT,
+    near_ls,
+    near_rs,
+    gain_ref,
+    bias_ref,
+    prod,
+    left_sq,
+    right_sq,
+    zn_cols,
+    vec,
+    pm,
+    xall,
+    far_ls,
+    far_rs,
+):
+    me = me_ref[0]
+    rows, tokens, _ = pair0.shape
+    half = rows // 2
+    hidden = weT.shape[0] // 4
+    vec[0] = columns_of(gain_ref)
+    vec[1] = columns_of(bias_ref)
+    fill_pair_mask(mask_ref, pm, rows)
+    for s, ref in ((2, pair2), (3, pair3)):
+        block = jnp.bitwise_xor(me, s)
+        place = jnp.bitwise_and(block, 1)
+
+        @pl.loop(0, half, unroll=8)
+        def _(t, ref=ref, block=block, place=place):
+            edge_tile(ref, t, block, place, weT, vec, pm, far_ls, far_rs)
+
+    for s, ref in enumerate((pair0, pair1, pair2, pair3)):
+        at = pl.multiple_of(jnp.bitwise_xor(me, s) * rows * tokens, rows * tokens)
+        xall[pl.ds(at, rows * tokens), :] = ref[...].reshape(rows * tokens, -1).astype(F32)
+
+    core = jnp.bitwise_and(me, 1)
+    group = me // 2
+    n_near = pl.multiple_of(group * 2 * rows, 2 * rows)
+    n_far = pl.multiple_of((1 - group) * 2 * rows, 2 * rows)
 
     @pl.loop(0, hidden, unroll=32)
     def _(h):
-        at = pl.multiple_of(h * tiles, tiles)
-        own = pl.multiple_of(h * tiles + me * half, half)
-        right = square(rs[pl.ds(at, tiles), :])
-        left = square(ls[pl.ds(at, tiles), :])
-        bdr[h] = right
-        bdl[h] = left
-        out = pl.multiple_of(h * half, half)
-        pr[0, pl.ds(out, half), :] = lanes(dot_nt(halves(ls[pl.ds(own, half), :]), right))
-        pr[1, pl.ds(out, half), :] = lanes(dot_nt(halves(rs[pl.ds(own, half), :]), left))
+        at = pl.ds(pl.multiple_of(h * half, half), half)
+        for near, far, sq in ((near_ls, far_ls, left_sq), (near_rs, far_rs, right_sq)):
+            sq[h, pl.ds(n_near, 2 * rows), :] = square((near[0, at, :], near[1, at, :]))
+            sq[h, pl.ds(n_far, 2 * rows), :] = square((far[0, at, :], far[1, at, :]))
+        prod[0, at, :] = lanes(dot_nt(halves(near_ls[core, at, :]), right_sq[h]))
+        prod[1, at, :] = lanes(dot_nt(halves(near_rs[core, at, :]), left_sq[h]))
 
     @pl.loop(0, half, unroll=8)
     def _(t):
-        for own in (True, False):
-            which = 0 if own else 1
-            prod = pr[which, pl.ds(t, hidden, stride=half), :].astype(BF16).astype(F32)
-            xhat, rstd = norm_columns(prod)
-            if own:
+        j = me * rows + t
+        x = jnp.concatenate(
+            [
+                xall[pl.ds(j, tokens, stride=tokens), :],
+                xall[pl.ds(j + half, tokens, stride=tokens), :],
+            ],
+            axis=0,
+        ).T
+        zhat, _ = norm_columns(x)
+        zn_cols[t] = (zhat * vec[0] + vec[1]).astype(BF16)
+
+
+def back_kernel(
+    me_ref,
+    mask_ref,
+    prod,
+    left_sq,
+    right_sq,
+    zn_cols,
+    pre_own,
+    zn_own,
+    zhat_own,
+    rstd_own,
+    pg_ref,
+    pg0,
+    pg1,
+    pg2,
+    pg3,
+    we_ref,
+    wg_ref,
+    wo_ref,
+    gain_ref,
+    ogain_ref,
+    obias_ref,
+    dz_ref,
+    grads_ref,
+    wgT,
+    woT,
+    vec,
+    pm,
+    pgs,
+    pr,
+    dgl_own,
+    gacc,
+):
+    me = me_ref[0]
+    rows, tokens, width = pg_ref.shape
+    half = rows // 2
+    hidden = wo_ref.shape[0]
+    wgT[...] = transposed(wg_ref)
+    woT[...] = transposed(wo_ref)
+    vec[0] = columns_of(gain_ref)
+    vec[1] = columns_of(ogain_ref)
+    vec[2] = columns_of(obias_ref)
+    fill_pair_mask(mask_ref, pm, rows)
+    gacc[...] = jnp.zeros_like(gacc)
+    for s, ref in enumerate((pg0, pg1, pg2, pg3)):
+        at = pl.multiple_of(jnp.bitwise_xor(me, s) * rows * rows, rows * rows)
+        pgs[pl.ds(at, rows * rows), :] = ref[...].reshape(rows * rows, width).astype(F32)
+
+    @pl.loop(0, half, unroll=8)
+    def _(t):
+        for which in range(2):
+            x = prod[which, pl.ds(t, hidden, stride=half), :].astype(BF16).astype(F32)
+            xhat, rstd = norm_columns(x)
+            if which == 0:
                 zn = zn_own[t]
-                pg = jnp.concatenate([f(pg_ref[t]), f(pg_ref[t + half])], axis=0).T
+                pg = two_rows(pg_ref, t)
             else:
-                j = me * rows + t
-                x = jnp.concatenate(
-                    [
-                        xall[pl.ds(j, tokens, stride=tokens), :],
-                        xall[pl.ds(j + half, tokens, stride=tokens), :],
-                    ],
-                    axis=0,
-                ).T
-                zhat, _ = norm_columns(x)
-                zn = (zhat * vec[0] + vec[1]).astype(BF16)
+                zn = zn_cols[t]
                 pg = jnp.concatenate(
                     [
                         pgs[pl.ds(t, tokens, stride=rows), :],
@@ -332,8 +439,8 @@
             gate = jax.nn.sigmoid(dot(wgT[...], zn))
             dy = (pg * gate).astype(BF16)
             dxn = dot(wo_ref[...], dy)
-            if own:
-                xn = (xhat * vec[2] + vec[3]).astype(BF16)
+            if which == 0:
+                xn = (xhat * vec[1] + vec[2]).astype(BF16)
                 y = dot(woT[...], xn)
                 dgl = (pg * y * gate * (1.0 - gate)).astype(BF16)
                 dgl_own[t] = dgl
@@ -342,14 +449,14 @@
                 gacc[6] += dxn * xhat
                 gacc[7] += dxn
             pr[which, pl.ds(t, hidden, stride=half), :] = norm_columns_backward(
-                dxn, vec[2], xhat, rstd
+                dxn, vec[1], xhat, rstd
             )
 
     @pl.loop(0, hidden, unroll=32)
     def _(h):
-        at = pl.multiple_of(h * half, half)
-        pr[0, pl.ds(at, half), :] = lanes(dot(halves(pr[0, pl.ds(at, half), :]), bdr[h]))
-        pr[1, pl.ds(at, half), :] = lanes(dot(halves(pr[1, pl.ds(at, half), :]), bdl[h]))
+        at = pl.ds(pl.multiple_of(h * half, half), half)
+        pr[0, at, :] = lanes(dot(halves(pr[0, at, :]), right_sq[h]))
+        pr[1, at, :] = lanes(dot(halves(pr[1, at, :]), left_sq[h]))
 
     @pl.loop(0, half, unroll=8)
     def _(t):
@@ -374,13 +481,12 @@
         dz_ref[t] = dz[:tokens]
         dz_ref[t + half] = dz[tokens:]
 
-    total = grads_ref
     for b in range(6):
-        total[b * LANES : (b + 1) * LANES, :] = gacc[b].astype(BF16)
+        grads_ref[b * LANES : (b + 1) * LANES, :] = gacc[b].astype(BF16)
     sums = [jnp.sum(gacc[b].T, axis=0, keepdims=True) for b in (8, 9, 6, 7)]
-    pad = total.shape[0] - 6 * LANES
+    pad = grads_ref.shape[0] - 6 * LANES
     sums.append(jnp.zeros((pad - 4, LANES), F32))
-    total[6 * LANES :, :] = jnp.concatenate(sums, axis=0).astype(BF16)
+    grads_ref[6 * LANES :, :] = jnp.concatenate(sums, axis=0).astype(BF16)
 
 
 def finish_kernel(n_blocks, me_ref, *refs):
@@ -437,75 +543,125 @@
     x = pair[0]
     g = pair_grad[0]
 
-    blocks = {0: x}
-    columns = {0: g}
-    for bit in bits_of(n_dap):
-        keep, give = {}, {}
-        for s, c in columns.items():
-            c = c.reshape(rows, -1, 2, bit * rows, width)
-            mine = ((me & bit) > 0).astype(jnp.int32)
-            keep[s] = lax.dynamic_index_in_dim(c, mine, 2, keepdims=False).reshape(rows, -1, width)
-            give[s] = lax.dynamic_index_in_dim(c, 1 - mine, 2, keepdims=False).reshape(
-                rows, -1, width
-            )
-        got = {s ^ bit: swap(b, "dap", n_dap, bit) for s, b in blocks.items()}
-        got_columns = {s ^ bit: swap(c, "dap", n_dap, bit) for s, c in give.items()}
-        got, got_columns = lax.optimization_barrier((got, got_columns))
-        blocks.update(got)
-        columns = {**keep, **got_columns}
-    blocks = [blocks[s] for s in range(n_dap)]
-    columns = [columns[s] for s in range(n_dap)]
-
     half = rows // 2
-    tiles = n_dap * half
     grad_rows = 6 * LANES + 16 * n_dap
-    vm = functools.partial(pltpu.VMEM)
-    dz, grads = pl.pallas_call(
-        functools.partial(fused_kernel, n_dap),
-        out_shape=(
-            jax.ShapeDtypeStruct((rows, tokens, width), BF16),
-            jax.ShapeDtypeStruct((grad_rows, LANES), BF16),
-        ),
-        in_specs=[pl.BlockSpec(memory_space=pltpu.SMEM)]
-        + [pl.BlockSpec(memory_space=pltpu.VMEM)] * (2 * n_dap + 9),
-        out_specs=(
-            pl.BlockSpec(memory_space=pltpu.VMEM),
-            pl.BlockSpec(memory_space=pltpu.VMEM),
-        ),
-        scratch_shapes=[
-            vm((4 * hidden, width), BF16),
+    vm = pltpu.VMEM
+    out = jax.ShapeDtypeStruct
+    row = lambda v: v.reshape(1, -1)
+
+    def call(kernel, us, outs, scratch, *args, in_hbm=0):
+        whole = pl.BlockSpec(memory_space=pltpu.VMEM)
+        hbm = pl.BlockSpec(memory_space=pltpu.HBM)
+        return pl.pallas_call(
+            kernel,
+            out_shape=tuple(outs),
+            in_specs=[pl.BlockSpec(memory_space=pltpu.SMEM)]
+            + [whole] * (len(args) - in_hbm)
+            + [hbm] * in_hbm,
+            out_specs=(whole,) * len(outs),
+            scratch_shapes=scratch,
+            compiler_params=pltpu.CompilerParams(vmem_limit_bytes=VMEM_BYTES),
+            cost_estimate=pl.CostEstimate(
+                flops=0, bytes_accessed=int(us * 3.6e6), transcendentals=0
+            ),
+        )(place, *args)
+
+    cut = g.reshape(rows, n_dap, rows, width)
+    far = swap(x, "dap", n_dap, 2)
+    near = swap(x, "dap", n_dap, 1)
+    pg_own, *pgs = [lax.dynamic_index_in_dim(cut, me ^ s, 1, keepdims=False) for s in range(4)]
+    pgs = [swap(v, "dap", n_dap, s) for s, v in enumerate(pgs, 1)]
+    weT, ls, rs, pre_own, zn_own, zhat_own, rstd_own = call(
+        near_kernel,
+        4,
+        [
+            out((4 * hidden, width), BF16),
+            out((2, hidden * half, LANES), F32),
+            out((2, hidden * half, LANES), F32),
+            out((half, 4 * hidden, LANES), F32),
+            out((half, width, LANES), BF16),
+            out((half, width, LANES), F32),
+            out((half, 1, LANES), F32),
+        ],
+        [
+            vm((2, width, LANES), F32),
+            vm((n_dap * half, LANES), F32),
+            vm((1, tokens), jnp.int32),
+            vm((rows, tokens, width), BF16),
+            vm((width, 4 * hidden), BF16),
+            vm((1, width), F32),
+            vm((1, width), F32),
+            pltpu.SemaphoreType.DMA((5,)),
+        ],
+        near,
+        token_mask,
+        x,
+        w_edges,
+        row(in_gain),
+        row(in_bias),
+        in_hbm=5,
+    )
+    far, zn_own, pg_own = lax.optimization_barrier((far, zn_own, pg_own))
+    across = swap(far, "dap", n_dap, 1)
+    prod, left_sq, right_sq, zn_cols = call(
+        product_kernel,
+        8,
+        [
+            out((2, hidden * half, LANES), F32),
+            out((hidden, tokens, tokens), BF16),
+            out((hidden, tokens, tokens), BF16),
+            out((half, width, LANES), BF16),
+        ],
+        [
+            vm((2, width, LANES), F32),
+            vm((n_dap * half, LANES), F32),
+            vm((n_dap * rows * tokens, width), F32),
+            vm((2, hidden * half, LANES), F32),
+            vm((2, hidden * half, LANES), F32),
+        ],
+        token_mask,
+        x,
+        near,
+        far,
+        across,
+        weT,
+        ls,
+        rs,
+        row(in_gain),
+        row(in_bias),
+    )
+    dz, grads = call(
+        back_kernel,
+        8,
+        [out((rows, tokens, width), BF16), out((grad_rows, LANES), BF16)],
+        [
             vm((width, width), BF16),
             vm((width, hidden), BF16),
-            vm((4, width, LANES), F32),
-            vm((tiles, LANES), F32),
-            vm((n_dap * rows * tokens, width), F32),
+            vm((3, width, LANES), F32),
+            vm((n_dap * half, LANES), F32),
             vm((n_dap * rows * rows, width), F32),
-            vm((hidden * tiles, LANES), F32),
-            vm((hidden * tiles, LANES), F32),
-            vm((half, 4 * hidden, LANES), F32),
-            vm((half, width, LANES), BF16),
-            vm((half, width, LANES), F32),
-            vm((half, 1, LANES), F32),
-            vm((hidden, tokens, tokens), BF16),
-            vm((hidden, tokens, tokens), BF16),
             vm((2, hidden * half, LANES), F32),
             vm((half, width, LANES), BF16),
             vm((10, LANES, LANES), F32),
         ],
-        compiler_params=pltpu.CompilerParams(vmem_limit_bytes=48 * 1024 * 1024),
-    )(
-        place,
         token_mask,
-        *blocks,
+        prod,
+        left_sq,
+        right_sq,
+        zn_cols,
+        pre_own,
+        zn_own,
+        zhat_own,
+        rstd_own,
         g,
-        *columns,
+        pg_own,
+        *pgs,
         w_edges,
         w_gate,
         w_out,
-        in_gain.reshape(1, -1),
-        in_bias.reshape(1, -1),
-        output_norm_gain.reshape(1, -1),
-        output_norm_bias.reshape(1, -1),
+        row(in_gain),
+        row(output_norm_gain),
+        row(output_norm_bias),
     )
 
     chunks = grads.reshape(n_dap, -1, LANES)
@@ -525,21 +681,19 @@
             terms = [p + q for p, q in zip(terms[::2], terms[1::2])]
         total = terms[0].astype(BF16)
     parts = [total] + [swap(total, "dap", n_dap, s) for s in range(1, n_dap)]
-    out = lambda *shape: jax.ShapeDtypeStruct(shape, F32)
-    edges, gate, outs, in_norm, out_norm = pl.pallas_call(
+    edges, gate, outs, in_norm, out_norm = call(
         functools.partial(finish_kernel, n_dap),
-        out_shape=(
-            out(width, 4 * hidden),
-            out(width, width),
-            out(hidden, width),
-            out(2, width),
-            out(2, hidden),
-        ),
-        in_specs=[pl.BlockSpec(memory_space=pltpu.SMEM)]
-        + [pl.BlockSpec(memory_space=pltpu.VMEM)] * n_dap,
-        out_specs=(pl.BlockSpec(memory_space=pltpu.VMEM),) * 5,
-        scratch_shapes=[vm((grad_rows, LANES), F32)],
-    )(place, *parts)
+        1,
+        [
+            out((width, 4 * hidden), F32),
+            out((width, width), F32),
+            out((hidden, width), F32),
+            out((2, width), F32),
+            out((2, hidden), F32),
+        ],
+        [vm((grad_rows, LANES), F32)],
+        *parts,
+    )
     return (dz[None], edges, gate, outs, in_norm, out_norm)
 
 
@@ -568,7 +722,7 @@
             and rows == 16
             and width == LANES
             and hidden == LANES
-            and n_dap & (n_dap - 1) == 0
+            and n_dap == 4
             and n_dp & (n_dp - 1) == 0
         )
         if fits:

time: 57.3 us -> 49.6 us (0.87)
  waiting for transfers between devices: 22.6 us -> 13.9 us
  Pallas kernels: 17.2 us -> 13.9 us
  local copies, waits for them, and re-layouts: 2.44 us -> 4.91 us
  starting transfers between devices: 14 us -> 15.8 us
    ppermute x16, waiting for transfers between devices: 22.6 us -> 13.9 us  [swap(): return lax.ppermute(x, axis, [(i, i ^ bit) for i in range(n)])]
    pallas_call x2 -> x4, Pallas kernels: 17.2 us -> 13.9 us  [call(): pl.pallas_call(kernel, out_shape=tuple(outs), in_specs=[pl.BlockSpec(memo...]
    unnamed x28 -> x22, local copies, waits for them, and re-layouts: 1.37 us -> 3.88 us
    ppermute x16, starting transfers between devices: 14 us -> 15.8 us  [swap(): return lax.ppermute(x, axis, [(i, i ^ bit) for i in range(n)])]
    dynamic_slice x1 -> x0, local copies, waits for them, and re-layouts: 1.03 us -> none  [per_device_fused(): lax.dynamic_index_in_dim(c, mine, 2, keepdims=False)]
    squeeze x0 -> x1, local copies, waits for them, and re-layouts: none -> 1.02 us  [per_device_fused(): lax.dynamic_index_in_dim(cut, me ^ s, 1, keepdims=False)]
  transfers between devices with their start and end apart: 16 -> 16, of which waited for: 11 -> 9; matrix products, arithmetic and copies ran while one was open for 2% -> 2% of each run, Pallas kernels for 0% -> 13%
where the time goes in v3:
time: 49.6 us; the launch traced here: 49.4 us
  starting transfers between devices  15.8 us (32%)
  waiting for transfers between devices  13.9 us (28%)
  Pallas kernels  13.9 us (28%)
  local copies, waits for them, and re-layouts  4.91 us (10%)
  between operations  0.8 us (2%)
    ppermute x16, starting transfers between devices, swap(): return lax.ppermute(x, axis, [(i, i ^ bit) for i in range(n)])  15.8 us
    ppermute x16, waiting for transfers between devices, swap(): return lax.ppermute(x, axis, [(i, i ^ bit) for i in range(n)])  13.9 us
    pallas_call x4, Pallas kernels, call(): pl.pallas_call(kernel, out_shape=tuple(outs), in_specs=[pl.BlockSpec(memo...  13.9 us
    unnamed x22, local copies, waits for them, and re-layouts  3.88 us
    squeeze x1, local copies, waits for them, and re-layouts, per_device_fused(): lax.dynamic_index_in_dim(cut, me ^ s, 1, keepdims=False)  1.02 us
  transfers between devices with their start and end apart: 16, of which 9 were waited for; matrix products, arithmetic and copies ran while one was open for 2% of the time, Pallas kernels for 13%

profile of v3, /device:TPU:0, one launch (start us, length us, event | category | flops | bytes accessed | tf_op | source)
XLA Modules:
  0.0 49.4 jit_solution(16939779040487715983)
XLA Ops:
  0.6 0.5 %collective-permute-start = (bf16[16,64,128]{2,1,0:T(8,128)(2,1)}, bf16[16,64,128]{2,1,0:T(8,128)(2,1)S(1)}, u32[]{:S(2)}, u32[]{:S(2)}) collective-permute-start(bf16[16,64,128]{2,1,0:T(8,128)(2,1)} %bitcast.37), channel_id=1, source_target_pairs={{0,1},{1,0},{2,3},{3,2},{4,5},{5,4},{6,7},{7,6},{8,9},{9,8},{10,11... | collective-permute-start | bytes 786440 | tf_op jit(solution)/shard_map/ppermute | solution.py:513
  1.2 2.6 %collective-permute-start.1 = (bf16[16,64,128]{2,1,0:T(8,128)(2,1)}, bf16[16,64,128]{2,1,0:T(8,128)(2,1)S(1)}, u32[]{:S(2)}, u32[]{:S(2)}) collective-permute-start(bf16[16,64,128]{2,1,0:T(8,128)(2,1)} %bitcast.38), channel_id=1, source_target_pairs={{0,2},{1,3},{2,0},{3,1},{4,6},{5,7},{6,4},{7,5},{8,10},{9,11},{10,... | collective-permute-start | bytes 786440 | tf_op jit(solution)/shard_map/ppermute | solution.py:513
  3.8 0.0 copy-start.10
  3.8 1.0 %dynamic-slice_bitcast_fusion = (bf16[16,16,128]{2,1,0:T(8,128)(2,1)S(1)}, bf16[16,16,128]{2,1,0:T(8,128)(2,1)S(1)}, bf16[16,16,128]{2,1,0:T(8,128)(2,1)S(1)}, bf16[16,16,128]{2,1,0:T(8,128)(2,1)S(1)}) fusion(bf16[16,4,16,128]{3,2,1,0:T(8,128)(2,1)} %bitcast.35, s32[]{:T(128)S(6)} %select_n.21, s32[]{:T(128)S(6)} %select_n.20, s32[]{:T(128)S(6)} %select_n.19, ...), kind=kLoop, calls=%fused_computation.6 | loop fusion | bytes 524304 | tf_op jit(solution)/shard_map/jit(dynamic_index_in_dim)/squeeze | solution.py:572
  4.8 0.0 copy-start
  4.8 0.0 collective-permute-done.near_ref.pair1
  4.8 0.0 copy-start.1
  4.8 1.0 %copy-done.1 = bf16[1,16,64,128]{3,2,1,0:T(8,128)(2,1)S(1)} copy-done((bf16[1,16,64,128]{3,2,1,0:T(8,128)(2,1)S(1)}, bf16[1,16,64,128]{3,2,1,0:T(8,128)(2,1)}, u32[]{:S(2)}) %copy-start.1) | copy-done | bytes 262168
  5.8 0.9 %copy-done.2 = bf16[128,512]{1,0:T(8,128)(2,1)S(1)} copy-done((bf16[128,512]{1,0:T(8,128)(2,1)S(1)}, bf16[128,512]{1,0:T(8,128)(2,1)}, u32[]{:S(2)}) %copy-start.2) | copy-done | bytes 131096
  6.7 0.7 %copy-done.6 = s32[1,64]{1,0:T(1,128)S(1)} copy-done((s32[1,64]{1,0:T(1,128)S(1)}, s32[1,64]{1,0:T(1,128)}, u32[]{:S(2)}) %copy-start.6) | copy-done | bytes 280
  7.4 0.7 %copy-done.7 = f32[128]{0:T(128)S(1)} copy-done((f32[128]{0:T(128)S(1)}, f32[128]{0:T(128)}, u32[]{:S(2)}) %copy-start.7) | copy-done | bytes 536
  8.0 0.7 %copy-done.8 = f32[128]{0:T(128)S(1)} copy-done((f32[128]{0:T(128)S(1)}, f32[128]{0:T(128)}, u32[]{:S(2)}) %copy-start.8) | copy-done | bytes 536
  8.7 1.4 %shard_map.145 = (bf16[512,128]{1,0:T(8,128)(2,1)S(1)}, f32[2,1024,128]{2,1,0:T(8,128)S(1)}, f32[2,1024,128]{2,1,0:T(8,128)S(1)}, f32[8,512,128]{2,1,0:T(8,128)S...) custom-call(s32[1]{0:T(128)} %bitcast.me_ref, ...), custom_call_target="tpu_custom_call" | custom-call | bytes 14400000 | tf_op jit(solution)/shard_map/pallas_call | solution.py:555
  10.1 0.7 %collective-permute-done.1.pair2 = bf16[16,64,128]{2,1,0:T(8,128)(2,1)S(1)} collective-permute-done((bf16[16,64,128]{2,1,0:T(8,128)(2,1)}, bf16[16,64,128]{2,1,0:T(8,128)(2,1)S(1)}, u32[]{:S(2)}, u32[]{:S(2)}) %collective-permute-start.1) | collective-permute-done | bytes 262176 | tf_op jit(solution)/shard_map/ppermute | solution.py:513
  10.9 0.0 collective-permute-start.2
  10.9 1.9 %collective-permute-start.5 = (bf16[16,16,128]{2,1,0:T(8,128)(2,1)S(1)}, bf16[16,16,128]{2,1,0:T(8,128)(2,1)S(1)}, u32[]{:S(2)}, u32[]{:S(2)}) collective-permute-start(bf16[16,16,128]{2,1,0:T(8,128)(2,1)S(1)} %get-tuple-element.48), channel_id=1, source_target_pairs={{0,3},{1,2},{2,1},{3,0},{4,7},{5,6},{6,5},{7,4},{8,11},{9,10},{10,... | collective-permute-start | bytes 196616 | tf_op jit(solution)/shard_map/ppermute | solution.py:513
  12.7 0.3 collective-permute-start.4
  13.0 0.0 collective-permute-start.3
  13.0 0.0 collective-permute-done.2.pair3
  13.0 5.2 %shard_map.146 = (f32[2,1024,128]{2,1,0:T(8,128)S(1)}, bf16[128,64,64]{2,1,0:T(8,128)(2,1)S(1)}, bf16[128,64,64]{2,1,0:T(8,128)(2,1)S(1)}, bf16[8,128,128]{2,1,0:T(8,128)(2,1)S(1)}) custom-call(s32[1]{0:T(128)} %bitcast.me_ref, s32[1,64]{1,0:T(1,128)S(1)} %copy-done.6, bf16[16,64,128]{2,1,0:T(8,128)(2,1)S(1)} %bitcast.40, ...), custom_call_target="tpu_custom_call" | custom-call | bytes 28800000 | tf_op jit(solution)/shard_map/pallas_call | solution.py:555
  18.2 0.0 collective-permute-done.5.pg3
  18.2 0.0 collective-permute-done.4.pg2
  18.2 0.0 collective-permute-done.3.pg1
  18.2 0.0 copy-done.3
  18.2 0.0 copy-done.4
  18.2 0.0 copy-done.5
  18.3 6.5 %shard_map.147 = (bf16[16,64,128]{2,1,0:T(8,128)(2,1)}, bf16[832,128]{1,0:T(8,128)(2,1)S(1)}) custom-call(s32[1]{0:T(128)} %bitcast.me_ref, s32[1,64]{1,0:T(1,128)S(1)} %copy-done.6, f32[2,1024,128]{2,1,0:T(8,128)S(1)} %get-tuple-element.32.prod, bf16[128,64,64]{2,1,0:T(8,128)(2,1)S(1)} %get-tuple-element.33.left_sq, ...), custom_call_target="tpu_custom_call" | custom-call | bytes 28800000 | tf_op jit(solution)/shard_map/pallas_call | solution.py:555
  24.8 0.6 %collective-permute-start.6 = (bf16[208,128]{1,0:T(8,128)(2,1)S(1)}, bf16[208,128]{1,0:T(8,128)(2,1)S(1)}, u32[]{:S(2)}, u32[]{:S(2)}) collective-permute-start(bf16[208,128]{1,0:T(8,128)(2,1)S(1)} %get-tuple-element.52), channel_id=1, source_target_pairs={{0,1},{1,0},{2,3},{3,2},{4,5},{5,4},{6,7},{7,6},{8,9},{9,8},{10,11... | collective-permute-start | bytes 159752 | tf_op jit(solution)/shard_map/ppermute | solution.py:513
  25.4 1.5 %collective-permute-start.8 = (bf16[208,128]{1,0:T(8,128)(2,1)S(1)}, bf16[208,128]{1,0:T(8,128)(2,1)S(1)}, u32[]{:S(2)}, u32[]{:S(2)}) collective-permute-start(bf16[208,128]{1,0:T(8,128)(2,1)S(1)} %get-tuple-element.53), channel_id=1, source_target_pairs={{0,3},{1,2},{2,1},{3,0},{4,7},{5,6},{6,5},{7,4},{8,11},{9,10},{10,... | collective-permute-start | bytes 159752 | tf_op jit(solution)/shard_map/ppermute | solution.py:513
  26.8 0.3 collective-permute-start.7
  27.2 0.0 collective-permute-done.6
  27.2 2.0 %collective-permute-done.8 = bf16[208,128]{1,0:T(8,128)(2,1)S(1)} collective-permute-done((bf16[208,128]{1,0:T(8,128)(2,1)S(1)}, bf16[208,128]{1,0:T(8,128)(2,1)S(1)}, u32[]{:S(2)}, u32[]{:S(2)}) %collective-permute-start.8) | collective-permute-done | bytes 53280 | tf_op jit(solution)/shard_map/ppermute | solution.py:513
  29.2 1.8 %collective-permute-done.7 = bf16[208,128]{1,0:T(8,128)(2,1)S(1)} collective-permute-done((bf16[208,128]{1,0:T(8,128)(2,1)S(1)}, bf16[208,128]{1,0:T(8,128)(2,1)S(1)}, u32[]{:S(2)}, u32[]{:S(2)}) %collective-permute-start.7) | collective-permute-done | bytes 53280 | tf_op jit(solution)/shard_map/ppermute | solution.py:513
  31.1 2.6 %collective-permute-start.11 = (bf16[208,128]{1,0:T(8,128)(2,1)S(1)}, bf16[208,128]{1,0:T(8,128)(2,1)S(1)}, u32[]{:S(2)}, u32[]{:S(2)}) collective-permute-start(bf16[208,128]{1,0:T(8,128)(2,1)S(1)} %fusion.2), channel_id=1, source_target_pairs={{0,12},{4,8},{8,4},{12,0},{16,28},{20,24},{24,20},{28,16},{1,13},{... | collective-permute-start | bytes 159752 | tf_op jit(solution)/shard_map/ppermute | solution.py:513
  33.6 0.4 collective-permute-start.10
  34.1 0.5 %collective-permute-start.9 = (bf16[208,128]{1,0:T(8,128)(2,1)S(1)}, bf16[208,128]{1,0:T(8,128)(2,1)S(1)}, u32[]{:S(2)}, u32[]{:S(2)}) collective-permute-start(bf16[208,128]{1,0:T(8,128)(2,1)S(1)} %fusion.2), channel_id=1, source_target_pairs={{0,4},{4,0},{8,12},{12,8},{16,20},{20,16},{24,28},{28,24},{1,5},{5... | collective-permute-start | bytes 159752 | tf_op jit(solution)/shard_map/ppermute | solution.py:513
  34.6 2.2 %collective-permute-done.11 = bf16[208,128]{1,0:T(8,128)(2,1)S(1)} collective-permute-done((bf16[208,128]{1,0:T(8,128)(2,1)S(1)}, bf16[208,128]{1,0:T(8,128)(2,1)S(1)}, u32[]{:S(2)}, u32[]{:S(2)}) %collective-permute-start.11) | collective-permute-done | bytes 53280 | tf_op jit(solution)/shard_map/ppermute | solution.py:513
  36.8 0.9 %collective-permute-done.10 = bf16[208,128]{1,0:T(8,128)(2,1)S(1)} collective-permute-done((bf16[208,128]{1,0:T(8,128)(2,1)S(1)}, bf16[208,128]{1,0:T(8,128)(2,1)S(1)}, u32[]{:S(2)}, u32[]{:S(2)}) %collective-permute-start.10) | collective-permute-done | bytes 53280 | tf_op jit(solution)/shard_map/ppermute | solution.py:513
  37.8 0.4 collective-permute-done.9
  38.3 2.7 %collective-permute-start.12 = (bf16[208,128]{1,0:T(8,128)(2,1)S(1)}, bf16[208,128]{1,0:T(8,128)(2,1)S(1)}, u32[]{:S(2)}, u32[]{:S(2)}) collective-permute-start(bf16[208,128]{1,0:T(8,128)(2,1)S(1)} %add_convert_fusion.1), channel_id=1, source_target_pairs={{0,16},{4,20},{8,24},{12,28},{16,0},{20,4},{24,8},{28,12},{1,17},{... | collective-permute-start | bytes 159752 | tf_op jit(solution)/shard_map/ppermute | solution.py:513
  40.9 2.4 %collective-permute-done.12 = bf16[208,128]{1,0:T(8,128)(2,1)S(1)} collective-permute-done((bf16[208,128]{1,0:T(8,128)(2,1)S(1)}, bf16[208,128]{1,0:T(8,128)(2,1)S(1)}, u32[]{:S(2)}, u32[]{:S(2)}) %collective-permute-start.12) | collective-permute-done | bytes 53280 | tf_op jit(solution)/shard_map/ppermute | solution.py:513
  43.4 0.1 collective-permute-start.15
  43.5 1.5 %collective-permute-start.14 = (bf16[208,128]{1,0:T(8,128)(2,1)S(1)}, bf16[208,128]{1,0:T(8,128)(2,1)S(1)}, u32[]{:S(2)}, u32[]{:S(2)}) collective-permute-start(bf16[208,128]{1,0:T(8,128)(2,1)S(1)} %add_convert_fusion.refs_0_), channel_id=1, source_target_pairs={{0,2},{1,3},{2,0},{3,1},{4,6},{5,7},{6,4},{7,5},{8,10},{9,11},{10,... | collective-permute-start | bytes 159752 | tf_op jit(solution)/shard_map/ppermute | solution.py:513
  44.9 0.4 collective-permute-start.13
  45.3 2.3 %collective-permute-done.15.refs_3_ = bf16[208,128]{1,0:T(8,128)(2,1)S(1)} collective-permute-done((bf16[208,128]{1,0:T(8,128)(2,1)S(1)}, bf16[208,128]{1,0:T(8,128)(2,1)S(1)}, u32[]{:S(2)}, u32[]{:S(2)}) %collective-permute-start.15) | collective-permute-done | bytes 53280 | tf_op jit(solution)/shard_map/ppermute | solution.py:513
  47.6 1.1 %collective-permute-done.14.refs_2_ = bf16[208,128]{1,0:T(8,128)(2,1)S(1)} collective-permute-done((bf16[208,128]{1,0:T(8,128)(2,1)S(1)}, bf16[208,128]{1,0:T(8,128)(2,1)S(1)}, u32[]{:S(2)}, u32[]{:S(2)}) %collective-permute-start.14) | collective-permute-done | bytes 53280 | tf_op jit(solution)/shard_map/ppermute | solution.py:513
  48.6 0.0 collective-permute-done.13.refs_1_
  48.6 0.8 %shard_map.148 = (f32[128,512]{1,0:T(8,128)}, f32[128,128]{1,0:T(8,128)}, f32[128,128]{1,0:T(8,128)}, f32[2,128]{1,0:T(2,128)}, f32[2,128]{1,0:T(2,128)}) custom-call(s32[1]{0:T(128)} %bitcast.me_ref, bf16[208,128]{1,0:T(8,128)(2,1)S(1)} %add_convert_fusion.refs_0_, bf16[208,128]{1,0:T(8,128)(2,1)S(1)} %collective-permute-done.13.refs_1_, ...), custom_call_target="tpu_custom_call" | custom-call | bytes 3600000 | tf_op jit(solution)/shard_map/pallas_call | solution.py:555
  (15 shorter events, 0.1 us)
Async XLA Ops:
  0.6 4.2 %collective-permute-start = (bf16[16,64,128]{2,1,0:T(8,128)(2,1)}, bf16[16,64,128]{2,1,0:T(8,128)(2,1)S(1)}, u32[]{:S(2)}, u32[]{:S(2)}) collective-permute-start(bf16[16,64,128]{2,1,0:T(8,128)(2,1)} %bitcast.37), channel_id=1, source_target_pairs={{0,1},{1,0},{2,3},{3,2},{4,5},{5,4},{6,7},{7,6},{8,9},{9,8},{10,11... | collective-permute-start | bytes 786440 | tf_op jit(solution)/shard_map/ppermute | solution.py:513
  1.2 9.7 %collective-permute-start.1 = (bf16[16,64,128]{2,1,0:T(8,128)(2,1)}, bf16[16,64,128]{2,1,0:T(8,128)(2,1)S(1)}, u32[]{:S(2)}, u32[]{:S(2)}) collective-permute-start(bf16[16,64,128]{2,1,0:T(8,128)(2,1)} %bitcast.38), channel_id=1, source_target_pairs={{0,2},{1,3},{2,0},{3,1},{4,6},{5,7},{6,4},{7,5},{8,10},{9,11},{10,... | collective-permute-start | bytes 786440 | tf_op jit(solution)/shard_map/ppermute | solution.py:513
  3.7 14.5 %copy-start.3 = (bf16[128,512]{1,0:T(8,128)(2,1)S(1)}, bf16[128,512]{1,0:T(8,128)(2,1)}, u32[]{:S(2)}) copy-start(bf16[128,512]{1,0:T(8,128)(2,1)} %we_ref.1) | copy-start | bytes 393220
  3.7 14.5 %copy-start.4 = (bf16[128,128]{1,0:T(8,128)(2,1)S(1)}, bf16[128,128]{1,0:T(8,128)(2,1)}, u32[]{:S(2)}) copy-start(bf16[128,128]{1,0:T(8,128)(2,1)} %wg_ref.1) | copy-start | bytes 98308
  3.8 14.5 %copy-start.5 = (bf16[128,128]{1,0:T(8,128)(2,1)S(1)}, bf16[128,128]{1,0:T(8,128)(2,1)}, u32[]{:S(2)}) copy-start(bf16[128,128]{1,0:T(8,128)(2,1)} %wo_ref.1) | copy-start | bytes 98308
  3.8 14.5 %copy-start.9 = (f32[128]{0:T(128)S(1)}, f32[128]{0:T(128)}, u32[]{:S(2)}) copy-start(f32[128]{0:T(128)} %param.18) | copy-start | bytes 1540
  3.8 14.5 %copy-start.10 = (f32[128]{0:T(128)S(1)}, f32[128]{0:T(128)}, u32[]{:S(2)}) copy-start(f32[128]{0:T(128)} %param.19) | copy-start | bytes 1540
  4.8 13.5 %copy-start = (bf16[1,16,64,128]{3,2,1,0:T(8,128)(2,1)S(1)}, bf16[1,16,64,128]{3,2,1,0:T(8,128)(2,1)}, u32[]{:S(2)}) copy-start(bf16[1,16,64,128]{3,2,1,0:T(8,128)(2,1)} %param.11) | copy-start | bytes 786436
  4.8 1.0 %copy-start.1 = (bf16[1,16,64,128]{3,2,1,0:T(8,128)(2,1)S(1)}, bf16[1,16,64,128]{3,2,1,0:T(8,128)(2,1)}, u32[]{:S(2)}) copy-start(bf16[1,16,64,128]{3,2,1,0:T(8,128)(2,1)} %param.10) | copy-start | bytes 786436
  5.8 0.9 %copy-start.2 = (bf16[128,512]{1,0:T(8,128)(2,1)S(1)}, bf16[128,512]{1,0:T(8,128)(2,1)}, u32[]{:S(2)}) copy-start(bf16[128,512]{1,0:T(8,128)(2,1)} %we_ref.1) | copy-start | bytes 393220
  6.7 0.7 %copy-start.6 = (s32[1,64]{1,0:T(1,128)S(1)}, s32[1,64]{1,0:T(1,128)}, u32[]{:S(2)}) copy-start(s32[1,64]{1,0:T(1,128)} %mask_ref.3) | copy-start | bytes 772
  7.4 0.7 %copy-start.7 = (f32[128]{0:T(128)S(1)}, f32[128]{0:T(128)}, u32[]{:S(2)}) copy-start(f32[128]{0:T(128)} %param.16) | copy-start | bytes 1540
  8.0 0.7 %copy-start.8 = (f32[128]{0:T(128)S(1)}, f32[128]{0:T(128)}, u32[]{:S(2)}) copy-start(f32[128]{0:T(128)} %param.17) | copy-start | bytes 1540
  10.9 2.1 %collective-permute-start.2 = (bf16[16,64,128]{2,1,0:T(8,128)(2,1)S(1)}, bf16[16,64,128]{2,1,0:T(8,128)(2,1)S(1)}, u32[]{:S(2)}, u32[]{:S(2)}) collective-permute-start(bf16[16,64,128]{2,1,0:T(8,128)(2,1)S(1)} %collective-permute-done.1.pair2), channel_id=1, source_target_pairs={{0,1},{1,0},{2,3},{3,2},{4,5},{5,4},{6,7},{7,6},{8,9},{9,8},{10,11... | collective-permute-start | bytes 786440 | tf_op jit(solution)/shard_map/ppermute | solution.py:513
  10.9 7.3 %collective-permute-start.5 = (bf16[16,16,128]{2,1,0:T(8,128)(2,1)S(1)}, bf16[16,16,128]{2,1,0:T(8,128)(2,1)S(1)}, u32[]{:S(2)}, u32[]{:S(2)}) collective-permute-start(bf16[16,16,128]{2,1,0:T(8,128)(2,1)S(1)} %get-tuple-element.48), channel_id=1, source_target_pairs={{0,3},{1,2},{2,1},{3,0},{4,7},{5,6},{6,5},{7,4},{8,11},{9,10},{10,... | collective-permute-start | bytes 196616 | tf_op jit(solution)/shard_map/ppermute | solution.py:513
  12.7 5.5 %collective-permute-start.4 = (bf16[16,16,128]{2,1,0:T(8,128)(2,1)S(1)}, bf16[16,16,128]{2,1,0:T(8,128)(2,1)S(1)}, u32[]{:S(2)}, u32[]{:S(2)}) collective-permute-start(bf16[16,16,128]{2,1,0:T(8,128)(2,1)S(1)} %get-tuple-element.49), channel_id=1, source_target_pairs={{0,2},{1,3},{2,0},{3,1},{4,6},{5,7},{6,4},{7,5},{8,10},{9,11},{10,... | collective-permute-start | bytes 196616 | tf_op jit(solution)/shard_map/ppermute | solution.py:513
  13.0 5.2 %collective-permute-start.3 = (bf16[16,16,128]{2,1,0:T(8,128)(2,1)S(1)}, bf16[16,16,128]{2,1,0:T(8,128)(2,1)S(1)}, u32[]{:S(2)}, u32[]{:S(2)}) collective-permute-start(bf16[16,16,128]{2,1,0:T(8,128)(2,1)S(1)} %get-tuple-element.50), channel_id=1, source_target_pairs={{0,1},{1,0},{2,3},{3,2},{4,5},{5,4},{6,7},{7,6},{8,9},{9,8},{10,11... | collective-permute-start | bytes 196616 | tf_op jit(solution)/shard_map/ppermute | solution.py:513
  24.8 2.4 %collective-permute-start.6 = (bf16[208,128]{1,0:T(8,128)(2,1)S(1)}, bf16[208,128]{1,0:T(8,128)(2,1)S(1)}, u32[]{:S(2)}, u32[]{:S(2)}) collective-permute-start(bf16[208,128]{1,0:T(8,128)(2,1)S(1)} %get-tuple-element.52), channel_id=1, source_target_pairs={{0,1},{1,0},{2,3},{3,2},{4,5},{5,4},{6,7},{7,6},{8,9},{9,8},{10,11... | collective-permute-start | bytes 159752 | tf_op jit(solution)/shard_map/ppermute | solution.py:513
  25.4 3.9 %collective-permute-start.8 = (bf16[208,128]{1,0:T(8,128)(2,1)S(1)}, bf16[208,128]{1,0:T(8,128)(2,1)S(1)}, u32[]{:S(2)}, u32[]{:S(2)}) collective-permute-start(bf16[208,128]{1,0:T(8,128)(2,1)S(1)} %get-tuple-element.53), channel_id=1, source_target_pairs={{0,3},{1,2},{2,1},{3,0},{4,7},{5,6},{6,5},{7,4},{8,11},{9,10},{10,... | collective-permute-start | bytes 159752 | tf_op jit(solution)/shard_map/ppermute | solution.py:513
  26.8 4.2 %collective-permute-start.7 = (bf16[208,128]{1,0:T(8,128)(2,1)S(1)}, bf16[208,128]{1,0:T(8,128)(2,1)S(1)}, u32[]{:S(2)}, u32[]{:S(2)}) collective-permute-start(bf16[208,128]{1,0:T(8,128)(2,1)S(1)} %get-tuple-element.54), channel_id=1, source_target_pairs={{0,2},{1,3},{2,0},{3,1},{4,6},{5,7},{6,4},{7,5},{8,10},{9,11},{10,... | collective-permute-start | bytes 159752 | tf_op jit(solution)/shard_map/ppermute | solution.py:513
  31.1 5.8 %collective-permute-start.11 = (bf16[208,128]{1,0:T(8,128)(2,1)S(1)}, bf16[208,128]{1,0:T(8,128)(2,1)S(1)}, u32[]{:S(2)}, u32[]{:S(2)}) collective-permute-start(bf16[208,128]{1,0:T(8,128)(2,1)S(1)} %fusion.2), channel_id=1, source_target_pairs={{0,12},{4,8},{8,4},{12,0},{16,28},{20,24},{24,20},{28,16},{1,13},{... | collective-permute-start | bytes 159752 | tf_op jit(solution)/shard_map/ppermute | solution.py:513
  33.6 4.1 %collective-permute-start.10 = (bf16[208,128]{1,0:T(8,128)(2,1)S(1)}, bf16[208,128]{1,0:T(8,128)(2,1)S(1)}, u32[]{:S(2)}, u32[]{:S(2)}) collective-permute-start(bf16[208,128]{1,0:T(8,128)(2,1)S(1)} %fusion.2), channel_id=1, source_target_pairs={{0,8},{4,12},{8,0},{12,4},{16,24},{20,28},{24,16},{28,20},{1,9},{5... | collective-permute-start | bytes 159752 | tf_op jit(solution)/shard_map/ppermute | solution.py:513
  34.1 4.1 %collective-permute-start.9 = (bf16[208,128]{1,0:T(8,128)(2,1)S(1)}, bf16[208,128]{1,0:T(8,128)(2,1)S(1)}, u32[]{:S(2)}, u32[]{:S(2)}) collective-permute-start(bf16[208,128]{1,0:T(8,128)(2,1)S(1)} %fusion.2), channel_id=1, source_target_pairs={{0,4},{4,0},{8,12},{12,8},{16,20},{20,16},{24,28},{28,24},{1,5},{5... | collective-permute-start | bytes 159752 | tf_op jit(solution)/shard_map/ppermute | solution.py:513
  38.3 5.1 %collective-permute-start.12 = (bf16[208,128]{1,0:T(8,128)(2,1)S(1)}, bf16[208,128]{1,0:T(8,128)(2,1)S(1)}, u32[]{:S(2)}, u32[]{:S(2)}) collective-permute-start(bf16[208,128]{1,0:T(8,128)(2,1)S(1)} %add_convert_fusion.1), channel_id=1, source_target_pairs={{0,16},{4,20},{8,24},{12,28},{16,0},{20,4},{24,8},{28,12},{1,17},{... | collective-permute-start | bytes 159752 | tf_op jit(solution)/shard_map/ppermute | solution.py:513
  43.4 4.2 %collective-permute-start.15 = (bf16[208,128]{1,0:T(8,128)(2,1)S(1)}, bf16[208,128]{1,0:T(8,128)(2,1)S(1)}, u32[]{:S(2)}, u32[]{:S(2)}) collective-permute-start(bf16[208,128]{1,0:T(8,128)(2,1)S(1)} %add_convert_fusion.refs_0_), channel_id=1, source_target_pairs={{0,3},{1,2},{2,1},{3,0},{4,7},{5,6},{6,5},{7,4},{8,11},{9,10},{10,... | collective-permute-start | bytes 159752 | tf_op jit(solution)/shard_map/ppermute | solution.py:513
  43.5 5.2 %collective-permute-start.14 = (bf16[208,128]{1,0:T(8,128)(2,1)S(1)}, bf16[208,128]{1,0:T(8,128)(2,1)S(1)}, u32[]{:S(2)}, u32[]{:S(2)}) collective-permute-start(bf16[208,128]{1,0:T(8,128)(2,1)S(1)} %add_convert_fusion.refs_0_), channel_id=1, source_target_pairs={{0,2},{1,3},{2,0},{3,1},{4,6},{5,7},{6,4},{7,5},{8,10},{9,11},{10,... | collective-permute-start | bytes 159752 | tf_op jit(solution)/shard_map/ppermute | solution.py:513
  44.9 3.7 %collective-permute-start.13 = (bf16[208,128]{1,0:T(8,128)(2,1)S(1)}, bf16[208,128]{1,0:T(8,128)(2,1)S(1)}, u32[]{:S(2)}, u32[]{:S(2)}) collective-permute-start(bf16[208,128]{1,0:T(8,128)(2,1)S(1)} %add_convert_fusion.refs_0_), channel_id=1, source_target_pairs={{0,1},{1,0},{2,3},{3,2},{4,5},{5,4},{6,7},{7,6},{8,9},{9,8},{10,11... | collective-permute-start | bytes 159752 | tf_op jit(solution)/shard_map/ppermute | solution.py:513

commit v4 on v3

--- a/solution.py
+++ b/solution.py
@@ -249,12 +249,13 @@
     weT,
     ls,
     rs,
-    pre_own,
+    factors,
     zn_own,
     zhat_own,
     rstd_own,
     vec,
     pm,
+    near_x,
     mask_ref,
     own_ref,
     we_ref,
@@ -291,12 +292,20 @@
     for s, ref in enumerate((own_ref, near_ref)):
         block = jnp.bitwise_xor(me, s)
         place = jnp.bitwise_and(block, 1)
+        near_x[place] = ref[...].astype(F32).reshape(near_x.shape[1:])
 
         @pl.loop(0, half, unroll=8)
         def _(t, s=s, ref=ref, block=block, place=place):
             zhat, rstd, zn, pre = edge_tile(ref, t, block, place, weT, vec, pm, ls, rs)
             if s == 0:
-                pre_own[t] = pre
+                mask = pm[pl.ds(block * half + t, 1), :]
+                for which in range(2):
+                    at = 2 * which * hidden
+                    sig = jax.nn.sigmoid(pre[at : at + hidden])
+                    val = pre[at + hidden : at + 2 * hidden]
+                    masked = mask * sig
+                    factors[t, at : at + hidden, :] = masked * val * (1.0 - sig)
+                    factors[t, at + hidden : at + 2 * hidden, :] = masked
                 zn_own[t] = zn
                 zhat_own[t] = zhat
                 rstd_own[t] = rstd
@@ -304,33 +313,26 @@
 
 def product_kernel(
     me_ref,
-    mask_ref,
-    pair0,
-    pair1,
     pair2,
     pair3,
     weT,
     near_ls,
     near_rs,
-    gain_ref,
-    bias_ref,
+    vec,
+    pm,
+    near_x,
     prod,
     left_sq,
     right_sq,
     zn_cols,
-    vec,
-    pm,
-    xall,
+    far_x,
     far_ls,
     far_rs,
 ):
     me = me_ref[0]
-    rows, tokens, _ = pair0.shape
+    rows, tokens, _ = pair2.shape
     half = rows // 2
     hidden = weT.shape[0] // 4
-    vec[0] = columns_of(gain_ref)
-    vec[1] = columns_of(bias_ref)
-    fill_pair_mask(mask_ref, pm, rows)
     for s, ref in ((2, pair2), (3, pair3)):
         block = jnp.bitwise_xor(me, s)
         place = jnp.bitwise_and(block, 1)
@@ -339,9 +341,7 @@
         def _(t, ref=ref, block=block, place=place):
             edge_tile(ref, t, block, place, weT, vec, pm, far_ls, far_rs)
 
-    for s, ref in enumerate((pair0, pair1, pair2, pair3)):
-        at = pl.multiple_of(jnp.bitwise_xor(me, s) * rows * tokens, rows * tokens)
-        xall[pl.ds(at, rows * tokens), :] = ref[...].reshape(rows * tokens, -1).astype(F32)
+        far_x[place] = ref[...].astype(F32).reshape(far_x.shape[1:])
 
     core = jnp.bitwise_and(me, 1)
     group = me // 2
@@ -359,29 +359,29 @@
 
     @pl.loop(0, half, unroll=8)
     def _(t):
-        j = me * rows + t
-        x = jnp.concatenate(
-            [
-                xall[pl.ds(j, tokens, stride=tokens), :],
-                xall[pl.ds(j + half, tokens, stride=tokens), :],
-            ],
-            axis=0,
-        ).T
+        x = []
+        for j in (me * rows + t, me * rows + t + half):
+            near, far = (
+                jnp.concatenate(
+                    [v[p, pl.ds(j, rows, stride=tokens), :] for p in range(2)], axis=0
+                )
+                for v in (near_x, far_x)
+            )
+            x += [jnp.where(group == 0, near, far), jnp.where(group == 0, far, near)]
+        x = jnp.concatenate(x, axis=0).T
         zhat, _ = norm_columns(x)
         zn_cols[t] = (zhat * vec[0] + vec[1]).astype(BF16)
 
 
 def back_kernel(
     me_ref,
-    mask_ref,
     prod,
     left_sq,
     right_sq,
     zn_cols,
-    pre_own,
+    factors,
     zn_own,
     zhat_own,
-    rstd_own,
     pg_ref,
     pg0,
     pg1,
@@ -390,15 +390,13 @@
     we_ref,
     wg_ref,
     wo_ref,
-    gain_ref,
     ogain_ref,
     obias_ref,
-    dz_ref,
+    dzn_ref,
     grads_ref,
     wgT,
     woT,
     vec,
-    pm,
     pgs,
     pr,
     dgl_own,
@@ -410,10 +408,8 @@
     hidden = wo_ref.shape[0]
     wgT[...] = transposed(wg_ref)
     woT[...] = transposed(wo_ref)
-    vec[0] = columns_of(gain_ref)
-    vec[1] = columns_of(ogain_ref)
-    vec[2] = columns_of(obias_ref)
-    fill_pair_mask(mask_ref, pm, rows)
+    vec[0] = columns_of(ogain_ref)
+    vec[1] = columns_of(obias_ref)
     gacc[...] = jnp.zeros_like(gacc)
     for s, ref in enumerate((pg0, pg1, pg2, pg3)):
         at = pl.multiple_of(jnp.bitwise_xor(me, s) * rows * rows, rows * rows)
@@ -440,7 +436,7 @@
             dy = (pg * gate).astype(BF16)
             dxn = dot(wo_ref[...], dy)
             if which == 0:
-                xn = (xhat * vec[1] + vec[2]).astype(BF16)
+                xn = (xhat * vec[0] + vec[1]).astype(BF16)
                 y = dot(woT[...], xn)
                 dgl = (pg * y * gate * (1.0 - gate)).astype(BF16)
                 dgl_own[t] = dgl
@@ -449,7 +445,7 @@
                 gacc[6] += dxn * xhat
                 gacc[7] += dxn
             pr[which, pl.ds(t, hidden, stride=half), :] = norm_columns_backward(
-                dxn, vec[1], xhat, rstd
+                dxn, vec[0], xhat, rstd
             )
 
     @pl.loop(0, hidden, unroll=32)
@@ -460,26 +456,19 @@
 
     @pl.loop(0, half, unroll=8)
     def _(t):
-        mask = pm[pl.ds(me * half + t, 1), :]
         zn = zn_own[t]
         zhat = zhat_own[t]
         dzn = dot(wg_ref[...], dgl_own[t])
         for which in range(2):
-            d = pr[which, pl.ds(t, hidden, stride=half), :].astype(BF16).astype(F32) * mask
-            sig = jax.nn.sigmoid(pre_own[t, pl.ds(2 * which * hidden, hidden), :])
-            val = pre_own[t, pl.ds((2 * which + 1) * hidden, hidden), :]
-            dval = d * sig
-            dgate = (dval * val * (1.0 - sig)).astype(BF16)
-            dval = dval.astype(BF16)
-            gacc[2 * which] += dot_nt(zn, dgate)
-            gacc[2 * which + 1] += dot_nt(zn, dval)
-            dzn += dot(we_ref[:, 2 * which * hidden : (2 * which + 1) * hidden], dgate)
-            dzn += dot(we_ref[:, (2 * which + 1) * hidden : (2 * which + 2) * hidden], dval)
+            d = pr[which, pl.ds(t, hidden, stride=half), :].astype(BF16).astype(F32)
+            for b in (2 * which, 2 * which + 1):
+                cols = slice(b * hidden, (b + 1) * hidden)
+                dpre = (d * factors[t, cols, :]).astype(BF16)
+                gacc[b] += dot_nt(zn, dpre)
+                dzn += dot(we_ref[:, cols], dpre)
         gacc[8] += dzn * zhat
         gacc[9] += dzn
-        dz = norm_columns_backward(dzn, vec[0], zhat, rstd_own[t]).T.astype(BF16)
-        dz_ref[t] = dz[:tokens]
-        dz_ref[t + half] = dz[tokens:]
+        dzn_ref[t] = dzn
 
     for b in range(6):
         grads_ref[b * LANES : (b + 1) * LANES, :] = gacc[b].astype(BF16)
@@ -487,6 +476,16 @@
     pad = grads_ref.shape[0] - 6 * LANES
     sums.append(jnp.zeros((pad - 4, LANES), F32))
     grads_ref[6 * LANES :, :] = jnp.concatenate(sums, axis=0).astype(BF16)
+
+
+def input_kernel(me_ref, dzn_ref, zhat_own, rstd_own, vec, dz_ref):
+    half = dzn_ref.shape[0]
+    tokens = dz_ref.shape[1]
+    gain = vec[0]
+    for t in range(half):
+        dz = norm_columns_backward(dzn_ref[t], gain, zhat_own[t], rstd_own[t]).T.astype(BF16)
+        dz_ref[t] = dz[:tokens]
+        dz_ref[t + half] = dz[tokens:]
 
 
 def finish_kernel(n_blocks, me_ref, *refs):
@@ -571,7 +570,7 @@
     near = swap(x, "dap", n_dap, 1)
     pg_own, *pgs = [lax.dynamic_index_in_dim(cut, me ^ s, 1, keepdims=False) for s in range(4)]
     pgs = [swap(v, "dap", n_dap, s) for s, v in enumerate(pgs, 1)]
-    weT, ls, rs, pre_own, zn_own, zhat_own, rstd_own = call(
+    weT, ls, rs, factors, zn_own, zhat_own, rstd_own, vec, pm, near_x = call(
         near_kernel,
         4,
         [
@@ -582,10 +581,11 @@
             out((half, width, LANES), BF16),
             out((half, width, LANES), F32),
             out((half, 1, LANES), F32),
+            out((2, width, LANES), F32),
+            out((n_dap * half, LANES), F32),
+            out((2, rows * tokens, width), F32),
         ],
         [
-            vm((2, width, LANES), F32),
-            vm((n_dap * half, LANES), F32),
             vm((1, tokens), jnp.int32),
             vm((rows, tokens, width), BF16),
             vm((width, 4 * hidden), BF16),
@@ -613,55 +613,57 @@
             out((half, width, LANES), BF16),
         ],
         [
-            vm((2, width, LANES), F32),
-            vm((n_dap * half, LANES), F32),
-            vm((n_dap * rows * tokens, width), F32),
+            vm((2, rows * tokens, width), F32),
             vm((2, hidden * half, LANES), F32),
             vm((2, hidden * half, LANES), F32),
         ],
-        token_mask,
-        x,
-        near,
         far,
         across,
         weT,
         ls,
         rs,
-        row(in_gain),
-        row(in_bias),
-    )
-    dz, grads = call(
+        vec,
+        pm,
+        near_x,
+    )
+    dzn, grads = call(
         back_kernel,
         8,
-        [out((rows, tokens, width), BF16), out((grad_rows, LANES), BF16)],
+        [out((half, width, LANES), F32), out((grad_rows, LANES), BF16)],
         [
             vm((width, width), BF16),
             vm((width, hidden), BF16),
-            vm((3, width, LANES), F32),
-            vm((n_dap * half, LANES), F32),
+            vm((2, width, LANES), F32),
             vm((n_dap * rows * rows, width), F32),
             vm((2, hidden * half, LANES), F32),
             vm((half, width, LANES), BF16),
             vm((10, LANES, LANES), F32),
         ],
-        token_mask,
         prod,
         left_sq,
         right_sq,
         zn_cols,
-        pre_own,
+        factors,
         zn_own,
         zhat_own,
-        rstd_own,
         g,
         pg_own,
         *pgs,
         w_edges,
         w_gate,
         w_out,
-        row(in_gain),
         row(output_norm_gain),
         row(output_norm_bias),
+    )
+    (dz,) = call(
+        input_kernel,
+        1,
+        [out((rows, tokens, width), BF16)],
+        [],
+        dzn,
+        zhat_own,
+        rstd_own,
+        vec,
     )
 
     chunks = grads.reshape(n_dap, -1, LANES)

time: 49.6 us -> 49 us (0.988)
  waiting for transfers between devices: 13.9 us -> 12.8 us
  Pallas kernels: 13.9 us -> 14.4 us
    ppermute x16, waiting for transfers between devices: 13.9 us -> 12.8 us  [swap(): return lax.ppermute(x, axis, [(i, i ^ bit) for i in range(n)])]
    pallas_call x4 -> x5, Pallas kernels: 13.9 us -> 14.4 us  [call(): pl.pallas_call(kernel, out_shape=tuple(outs), in_specs=[pl.BlockSpec(memo...]
    unnamed x22 -> x20, local copies, waits for them, and re-layouts: 3.88 us -> 3.84 us
  transfers between devices with their start and end apart: 16 -> 16, of which waited for: 9 -> 9; matrix products, arithmetic and copies ran while one was open for 2% -> 2% of each run, Pallas kernels for 13% -> 16%
where the time goes in v4:
time: 49 us; the launch traced here: 48.8 us
  starting transfers between devices  15.8 us (32%)
  Pallas kernels  14.4 us (29%)
  waiting for transfers between devices  12.8 us (26%)
  local copies, waits for them, and re-layouts  4.83 us (10%)
  between operations  0.82 us (2%)
    ppermute x16, starting transfers between devices, swap(): return lax.ppermute(x, axis, [(i, i ^ bit) for i in range(n)])  15.8 us
    pallas_call x5, Pallas kernels, call(): pl.pallas_call(kernel, out_shape=tuple(outs), in_specs=[pl.BlockSpec(memo...  14.4 us
    ppermute x16, waiting for transfers between devices, swap(): return lax.ppermute(x, axis, [(i, i ^ bit) for i in range(n)])  12.8 us
    unnamed x20, local copies, waits for them, and re-layouts  3.84 us
  transfers between devices with their start and end apart: 16, of which 9 were waited for; matrix products, arithmetic and copies ran while one was open for 2% of the time, Pallas kernels for 16%

profile of v4, /device:TPU:0, one launch (start us, length us, event | category | flops | bytes accessed | tf_op | source)
XLA Modules:
  0.0 48.8 jit_solution(18158852440804903497)
XLA Ops:
  0.6 0.5 %collective-permute-start.1 = (bf16[16,64,128]{2,1,0:T(8,128)(2,1)}, bf16[16,64,128]{2,1,0:T(8,128)(2,1)S(1)}, u32[]{:S(2)}, u32[]{:S(2)}) collective-permute-start(bf16[16,64,128]{2,1,0:T(8,128)(2,1)} %bitcast.37), channel_id=1, source_target_pairs={{0,1},{1,0},{2,3},{3,2},{4,5},{5,4},{6,7},{7,6},{8,9},{9,8},{10,11... | collective-permute-start | bytes 786440 | tf_op jit(solution)/shard_map/ppermute | solution.py:512
  1.1 2.6 %collective-permute-start = (bf16[16,64,128]{2,1,0:T(8,128)(2,1)}, bf16[16,64,128]{2,1,0:T(8,128)(2,1)S(1)}, u32[]{:S(2)}, u32[]{:S(2)}) collective-permute-start(bf16[16,64,128]{2,1,0:T(8,128)(2,1)} %bitcast.38), channel_id=1, source_target_pairs={{0,2},{1,3},{2,0},{3,1},{4,6},{5,7},{6,4},{7,5},{8,10},{9,11},{10,... | collective-permute-start | bytes 786440 | tf_op jit(solution)/shard_map/ppermute | solution.py:512
  3.7 1.0 %dynamic-slice_bitcast_fusion = (bf16[16,16,128]{2,1,0:T(8,128)(2,1)S(1)}, bf16[16,16,128]{2,1,0:T(8,128)(2,1)S(1)}, bf16[16,16,128]{2,1,0:T(8,128)(2,1)S(1)}, bf16[16,16,128]{2,1,0:T(8,128)(2,1)S(1)}) fusion(bf16[16,4,16,128]{3,2,1,0:T(8,128)(2,1)} %bitcast.35, s32[]{:T(128)S(6)} %select_n.21, s32[]{:T(128)S(6)} %select_n.20, s32[]{:T(128)S(6)} %select_n.19, ...), kind=kLoop, calls=%fused_computation.6 | loop fusion | bytes 524304 | tf_op jit(solution)/shard_map/jit(dynamic_index_in_dim)/squeeze | solution.py:571
  4.7 0.0 collective-permute-done.1.near_ref
  4.7 0.0 copy-start.1
  4.7 0.9 %copy-done.1 = bf16[128,512]{1,0:T(8,128)(2,1)S(1)} copy-done((bf16[128,512]{1,0:T(8,128)(2,1)S(1)}, bf16[128,512]{1,0:T(8,128)(2,1)}, u32[]{:S(2)}) %copy-start.1) | copy-done | bytes 131096
  5.6 0.9 %copy-done.2 = bf16[1,16,64,128]{3,2,1,0:T(8,128)(2,1)S(1)} copy-done((bf16[1,16,64,128]{3,2,1,0:T(8,128)(2,1)S(1)}, bf16[1,16,64,128]{3,2,1,0:T(8,128)(2,1)}, u32[]{:S(2)}) %copy-start.2) | copy-done | bytes 262168
  6.6 0.7 %copy-done.5 = s32[1,64]{1,0:T(1,128)S(1)} copy-done((s32[1,64]{1,0:T(1,128)S(1)}, s32[1,64]{1,0:T(1,128)}, u32[]{:S(2)}) %copy-start.5) | copy-done | bytes 280
  7.2 0.7 %copy-done.6 = f32[128]{0:T(128)S(1)} copy-done((f32[128]{0:T(128)S(1)}, f32[128]{0:T(128)}, u32[]{:S(2)}) %copy-start.6) | copy-done | bytes 536
  7.9 0.7 %copy-done.7 = f32[128]{0:T(128)S(1)} copy-done((f32[128]{0:T(128)S(1)}, f32[128]{0:T(128)}, u32[]{:S(2)}) %copy-start.7) | copy-done | bytes 536
  8.5 1.6 %shard_map.145 = (bf16[512,128]{1,0:T(8,128)(2,1)S(1)}, f32[2,1024,128]{2,1,0:T(8,128)S(1)}, f32[2,1024,128]{2,1,0:T(8,128)S(1)}, f32[8,512,128]{2,1,0:T(8,128)S...) custom-call(s32[1]{0:T(128)} %bitcast.me_ref, ...), custom_call_target="tpu_custom_call" | custom-call | bytes 14400000 | tf_op jit(solution)/shard_map/pallas_call | solution.py:554
  10.2 0.0 copy-start
  10.2 0.0 copy-start.3
  10.2 0.0 copy-start.4
  10.2 0.0 copy-start.8
  10.2 0.0 copy-start.9
  10.2 0.6 %collective-permute-done.pair2 = bf16[16,64,128]{2,1,0:T(8,128)(2,1)S(1)} collective-permute-done((bf16[16,64,128]{2,1,0:T(8,128)(2,1)}, bf16[16,64,128]{2,1,0:T(8,128)(2,1)S(1)}, u32[]{:S(2)}, u32[]{:S(2)}) %collective-permute-start) | collective-permute-done | bytes 262176 | tf_op jit(solution)/shard_map/ppermute | solution.py:512
  10.9 0.0 collective-permute-start.2
  10.9 1.9 %collective-permute-start.5 = (bf16[16,16,128]{2,1,0:T(8,128)(2,1)S(1)}, bf16[16,16,128]{2,1,0:T(8,128)(2,1)S(1)}, u32[]{:S(2)}, u32[]{:S(2)}) collective-permute-start(bf16[16,16,128]{2,1,0:T(8,128)(2,1)S(1)} %get-tuple-element.54), channel_id=1, source_target_pairs={{0,3},{1,2},{2,1},{3,0},{4,7},{5,6},{6,5},{7,4},{8,11},{9,10},{10,... | collective-permute-start | bytes 196616 | tf_op jit(solution)/shard_map/ppermute | solution.py:512
  12.7 0.3 collective-permute-start.4
  13.0 0.0 collective-permute-start.3
  13.0 0.0 collective-permute-done.2.pair3
  13.0 5.2 %shard_map.146 = (f32[2,1024,128]{2,1,0:T(8,128)S(1)}, bf16[128,64,64]{2,1,0:T(8,128)(2,1)S(1)}, bf16[128,64,64]{2,1,0:T(8,128)(2,1)S(1)}, bf16[8,128,128]{2,1,0:T(8,128)(2,1)S(1)}) custom-call(s32[1]{0:T(128)} %bitcast.me_ref, bf16[16,64,128]{2,1,0:T(8,128)(2,1)S(1)} %collective-permute-done.pair2, bf16[16,64,128]{2,1,0:T(8,128)(2,1)S(1)} %collective-permute-done.2.pair3, ...), custom_call_target="tpu_custom_call" | custom-call | bytes 28800000 | tf_op jit(solution)/shard_map/pallas_call | solution.py:554
  18.2 0.0 collective-permute-done.5.pg3
  18.2 0.0 collective-permute-done.4.pg2
  18.3 5.9 %shard_map.147 = (f32[8,128,128]{2,1,0:T(8,128)S(1)}, bf16[832,128]{1,0:T(8,128)(2,1)S(1)}) custom-call(s32[1]{0:T(128)} %bitcast.me_ref, f32[2,1024,128]{2,1,0:T(8,128)S(1)} %get-tuple-element.38.prod, bf16[128,64,64]{2,1,0:T(8,128)(2,1)S(1)} %get-tuple-element.39.left_sq, bf16[128,64,64]{2,1,0:T(8,128)(2,1)S(1)} %get-tuple-element.40.right_sq, ...), custom_call_target="tpu_custom_call" | custom-call | bytes 28800000 | tf_op jit(solution)/shard_map/pallas_call | solution.py:554
  24.1 0.6 %collective-permute-start.6 = (bf16[208,128]{1,0:T(8,128)(2,1)S(1)}, bf16[208,128]{1,0:T(8,128)(2,1)S(1)}, u32[]{:S(2)}, u32[]{:S(2)}) collective-permute-start(bf16[208,128]{1,0:T(8,128)(2,1)S(1)} %get-tuple-element.58), channel_id=1, source_target_pairs={{0,1},{1,0},{2,3},{3,2},{4,5},{5,4},{6,7},{7,6},{8,9},{9,8},{10,11... | collective-permute-start | bytes 159752 | tf_op jit(solution)/shard_map/ppermute | solution.py:512
  24.7 1.5 %collective-permute-start.8 = (bf16[208,128]{1,0:T(8,128)(2,1)S(1)}, bf16[208,128]{1,0:T(8,128)(2,1)S(1)}, u32[]{:S(2)}, u32[]{:S(2)}) collective-permute-start(bf16[208,128]{1,0:T(8,128)(2,1)S(1)} %get-tuple-element.59), channel_id=1, source_target_pairs={{0,3},{1,2},{2,1},{3,0},{4,7},{5,6},{6,5},{7,4},{8,11},{9,10},{10,... | collective-permute-start | bytes 159752 | tf_op jit(solution)/shard_map/ppermute | solution.py:512
  26.2 0.3 collective-permute-start.7
  26.5 0.0 collective-permute-done.6
  26.5 2.0 %collective-permute-done.8 = bf16[208,128]{1,0:T(8,128)(2,1)S(1)} collective-permute-done((bf16[208,128]{1,0:T(8,128)(2,1)S(1)}, bf16[208,128]{1,0:T(8,128)(2,1)S(1)}, u32[]{:S(2)}, u32[]{:S(2)}) %collective-permute-start.8) | collective-permute-done | bytes 53280 | tf_op jit(solution)/shard_map/ppermute | solution.py:512
  28.5 1.9 %collective-permute-done.7 = bf16[208,128]{1,0:T(8,128)(2,1)S(1)} collective-permute-done((bf16[208,128]{1,0:T(8,128)(2,1)S(1)}, bf16[208,128]{1,0:T(8,128)(2,1)S(1)}, u32[]{:S(2)}, u32[]{:S(2)}) %collective-permute-start.7) | collective-permute-done | bytes 53280 | tf_op jit(solution)/shard_map/ppermute | solution.py:512
  30.4 2.6 %collective-permute-start.11 = (bf16[208,128]{1,0:T(8,128)(2,1)S(1)}, bf16[208,128]{1,0:T(8,128)(2,1)S(1)}, u32[]{:S(2)}, u32[]{:S(2)}) collective-permute-start(bf16[208,128]{1,0:T(8,128)(2,1)S(1)} %fusion.2), channel_id=1, source_target_pairs={{0,12},{4,8},{8,4},{12,0},{16,28},{20,24},{24,20},{28,16},{1,13},{... | collective-permute-start | bytes 159752 | tf_op jit(solution)/shard_map/ppermute | solution.py:512
  33.0 0.4 collective-permute-start.10
  33.4 0.5 %collective-permute-start.9 = (bf16[208,128]{1,0:T(8,128)(2,1)S(1)}, bf16[208,128]{1,0:T(8,128)(2,1)S(1)}, u32[]{:S(2)}, u32[]{:S(2)}) collective-permute-start(bf16[208,128]{1,0:T(8,128)(2,1)S(1)} %fusion.2), channel_id=1, source_target_pairs={{0,4},{4,0},{8,12},{12,8},{16,20},{20,16},{24,28},{28,24},{1,5},{5... | collective-permute-start | bytes 159752 | tf_op jit(solution)/shard_map/ppermute | solution.py:512
  34.0 2.2 %collective-permute-done.11 = bf16[208,128]{1,0:T(8,128)(2,1)S(1)} collective-permute-done((bf16[208,128]{1,0:T(8,128)(2,1)S(1)}, bf16[208,128]{1,0:T(8,128)(2,1)S(1)}, u32[]{:S(2)}, u32[]{:S(2)}) %collective-permute-start.11) | collective-permute-done | bytes 53280 | tf_op jit(solution)/shard_map/ppermute | solution.py:512
  36.2 0.9 %collective-permute-done.10 = bf16[208,128]{1,0:T(8,128)(2,1)S(1)} collective-permute-done((bf16[208,128]{1,0:T(8,128)(2,1)S(1)}, bf16[208,128]{1,0:T(8,128)(2,1)S(1)}, u32[]{:S(2)}, u32[]{:S(2)}) %collective-permute-start.10) | collective-permute-done | bytes 53280 | tf_op jit(solution)/shard_map/ppermute | solution.py:512
  37.1 0.4 collective-permute-done.9
  37.6 2.7 %collective-permute-start.12 = (bf16[208,128]{1,0:T(8,128)(2,1)S(1)}, bf16[208,128]{1,0:T(8,128)(2,1)S(1)}, u32[]{:S(2)}, u32[]{:S(2)}) collective-permute-start(bf16[208,128]{1,0:T(8,128)(2,1)S(1)} %add_convert_fusion.1), channel_id=1, source_target_pairs={{0,16},{4,20},{8,24},{12,28},{16,0},{20,4},{24,8},{28,12},{1,17},{... | collective-permute-start | bytes 159752 | tf_op jit(solution)/shard_map/ppermute | solution.py:512
  40.2 2.4 %collective-permute-done.12 = bf16[208,128]{1,0:T(8,128)(2,1)S(1)} collective-permute-done((bf16[208,128]{1,0:T(8,128)(2,1)S(1)}, bf16[208,128]{1,0:T(8,128)(2,1)S(1)}, u32[]{:S(2)}, u32[]{:S(2)}) %collective-permute-start.12) | collective-permute-done | bytes 53280 | tf_op jit(solution)/shard_map/ppermute | solution.py:512
  42.7 0.1 collective-permute-start.15
  42.8 1.5 %collective-permute-start.14 = (bf16[208,128]{1,0:T(8,128)(2,1)S(1)}, bf16[208,128]{1,0:T(8,128)(2,1)S(1)}, u32[]{:S(2)}, u32[]{:S(2)}) collective-permute-start(bf16[208,128]{1,0:T(8,128)(2,1)S(1)} %add_convert_fusion.refs_0_), channel_id=1, source_target_pairs={{0,2},{1,3},{2,0},{3,1},{4,6},{5,7},{6,4},{7,5},{8,10},{9,11},{10,... | collective-permute-start | bytes 159752 | tf_op jit(solution)/shard_map/ppermute | solution.py:512
  44.3 0.4 collective-permute-start.13
  44.6 1.0 %shard_map.148 = bf16[16,64,128]{2,1,0:T(8,128)(2,1)} custom-call(s32[1]{0:T(128)} %bitcast.me_ref, f32[8,128,128]{2,1,0:T(8,128)S(1)} %get-tuple-element.46.dzn_ref, f32[8,128,128]{2,1,0:T(8,128)S(1)} %get-tuple-element.44.zhat_own, f32[8,1,128]{2,1,0:T(1,128)S(1)} %get-tuple-element.47.rstd_own, f32[2,128,128]{2,1,0:T(8,128)S(1)} %get-tuple-element.35.vec), custom_call_target="tpu_custom_call" | custom-call | bytes 3600000 | tf_op jit(solution)/shard_map/pallas_call | solution.py:554
  45.6 1.3 %collective-permute-done.15.refs_3_ = bf16[208,128]{1,0:T(8,128)(2,1)S(1)} collective-permute-done((bf16[208,128]{1,0:T(8,128)(2,1)S(1)}, bf16[208,128]{1,0:T(8,128)(2,1)S(1)}, u32[]{:S(2)}, u32[]{:S(2)}) %collective-permute-start.15) | collective-permute-done | bytes 53280 | tf_op jit(solution)/shard_map/ppermute | solution.py:512
  46.9 1.1 %collective-permute-done.14.refs_2_ = bf16[208,128]{1,0:T(8,128)(2,1)S(1)} collective-permute-done((bf16[208,128]{1,0:T(8,128)(2,1)S(1)}, bf16[208,128]{1,0:T(8,128)(2,1)S(1)}, u32[]{:S(2)}, u32[]{:S(2)}) %collective-permute-start.14) | collective-permute-done | bytes 53280 | tf_op jit(solution)/shard_map/ppermute | solution.py:512
  48.0 0.0 collective-permute-done.13.refs_1_
  48.0 0.8 %shard_map.149 = (f32[128,512]{1,0:T(8,128)}, f32[128,128]{1,0:T(8,128)}, f32[128,128]{1,0:T(8,128)}, f32[2,128]{1,0:T(2,128)}, f32[2,128]{1,0:T(2,128)}) custom-call(s32[1]{0:T(128)} %bitcast.me_ref, bf16[208,128]{1,0:T(8,128)(2,1)S(1)} %add_convert_fusion.refs_0_, bf16[208,128]{1,0:T(8,128)(2,1)S(1)} %collective-permute-done.13.refs_1_, ...), custom_call_target="tpu_custom_call" | custom-call | bytes 3600000 | tf_op jit(solution)/shard_map/pallas_call | solution.py:554
  (14 shorter events, 0.1 us)
Async XLA Ops:
  0.6 4.1 %collective-permute-start.1 = (bf16[16,64,128]{2,1,0:T(8,128)(2,1)}, bf16[16,64,128]{2,1,0:T(8,128)(2,1)S(1)}, u32[]{:S(2)}, u32[]{:S(2)}) collective-permute-start(bf16[16,64,128]{2,1,0:T(8,128)(2,1)} %bitcast.37), channel_id=1, source_target_pairs={{0,1},{1,0},{2,3},{3,2},{4,5},{5,4},{6,7},{7,6},{8,9},{9,8},{10,11... | collective-permute-start | bytes 786440 | tf_op jit(solution)/shard_map/ppermute | solution.py:512
  1.1 9.7 %collective-permute-start = (bf16[16,64,128]{2,1,0:T(8,128)(2,1)}, bf16[16,64,128]{2,1,0:T(8,128)(2,1)S(1)}, u32[]{:S(2)}, u32[]{:S(2)}) collective-permute-start(bf16[16,64,128]{2,1,0:T(8,128)(2,1)} %bitcast.38), channel_id=1, source_target_pairs={{0,2},{1,3},{2,0},{3,1},{4,6},{5,7},{6,4},{7,5},{8,10},{9,11},{10,... | collective-permute-start | bytes 786440 | tf_op jit(solution)/shard_map/ppermute | solution.py:512
  4.7 0.9 %copy-start.1 = (bf16[128,512]{1,0:T(8,128)(2,1)S(1)}, bf16[128,512]{1,0:T(8,128)(2,1)}, u32[]{:S(2)}) copy-start(bf16[128,512]{1,0:T(8,128)(2,1)} %we_ref.1) | copy-start | bytes 393220
  5.6 0.9 %copy-start.2 = (bf16[1,16,64,128]{3,2,1,0:T(8,128)(2,1)S(1)}, bf16[1,16,64,128]{3,2,1,0:T(8,128)(2,1)}, u32[]{:S(2)}) copy-start(bf16[1,16,64,128]{3,2,1,0:T(8,128)(2,1)} %param.10) | copy-start | bytes 786436
  6.6 0.7 %copy-start.5 = (s32[1,64]{1,0:T(1,128)S(1)}, s32[1,64]{1,0:T(1,128)}, u32[]{:S(2)}) copy-start(s32[1,64]{1,0:T(1,128)} %mask_hbm.1) | copy-start | bytes 772
  7.2 0.7 %copy-start.6 = (f32[128]{0:T(128)S(1)}, f32[128]{0:T(128)}, u32[]{:S(2)}) copy-start(f32[128]{0:T(128)} %param.16) | copy-start | bytes 1540
  7.9 0.7 %copy-start.7 = (f32[128]{0:T(128)S(1)}, f32[128]{0:T(128)}, u32[]{:S(2)}) copy-start(f32[128]{0:T(128)} %param.17) | copy-start | bytes 1540
  10.2 8.0 %copy-start = (bf16[1,16,64,128]{3,2,1,0:T(8,128)(2,1)S(1)}, bf16[1,16,64,128]{3,2,1,0:T(8,128)(2,1)}, u32[]{:S(2)}) copy-start(bf16[1,16,64,128]{3,2,1,0:T(8,128)(2,1)} %param.11) | copy-start | bytes 786436
  10.2 8.0 %copy-start.3 = (bf16[128,128]{1,0:T(8,128)(2,1)S(1)}, bf16[128,128]{1,0:T(8,128)(2,1)}, u32[]{:S(2)}) copy-start(bf16[128,128]{1,0:T(8,128)(2,1)} %wg_ref.1) | copy-start | bytes 98308
  10.2 8.0 %copy-start.4 = (bf16[128,128]{1,0:T(8,128)(2,1)S(1)}, bf16[128,128]{1,0:T(8,128)(2,1)}, u32[]{:S(2)}) copy-start(bf16[128,128]{1,0:T(8,128)(2,1)} %wo_ref.1) | copy-start | bytes 98308
  10.2 8.0 %copy-start.8 = (f32[128]{0:T(128)S(1)}, f32[128]{0:T(128)}, u32[]{:S(2)}) copy-start(f32[128]{0:T(128)} %param.18) | copy-start | bytes 1540
  10.2 8.0 %copy-start.9 = (f32[128]{0:T(128)S(1)}, f32[128]{0:T(128)}, u32[]{:S(2)}) copy-start(f32[128]{0:T(128)} %param.19) | copy-start | bytes 1540
  10.9 2.1 %collective-permute-start.2 = (bf16[16,64,128]{2,1,0:T(8,128)(2,1)S(1)}, bf16[16,64,128]{2,1,0:T(8,128)(2,1)S(1)}, u32[]{:S(2)}, u32[]{:S(2)}) collective-permute-start(bf16[16,64,128]{2,1,0:T(8,128)(2,1)S(1)} %collective-permute-done.pair2), channel_id=1, source_target_pairs={{0,1},{1,0},{2,3},{3,2},{4,5},{5,4},{6,7},{7,6},{8,9},{9,8},{10,11... | collective-permute-start | bytes 786440 | tf_op jit(solution)/shard_map/ppermute | solution.py:512
  10.9 7.3 %collective-permute-start.5 = (bf16[16,16,128]{2,1,0:T(8,128)(2,1)S(1)}, bf16[16,16,128]{2,1,0:T(8,128)(2,1)S(1)}, u32[]{:S(2)}, u32[]{:S(2)}) collective-permute-start(bf16[16,16,128]{2,1,0:T(8,128)(2,1)S(1)} %get-tuple-element.54), channel_id=1, source_target_pairs={{0,3},{1,2},{2,1},{3,0},{4,7},{5,6},{6,5},{7,4},{8,11},{9,10},{10,... | collective-permute-start | bytes 196616 | tf_op jit(solution)/shard_map/ppermute | solution.py:512
  12.7 5.5 %collective-permute-start.4 = (bf16[16,16,128]{2,1,0:T(8,128)(2,1)S(1)}, bf16[16,16,128]{2,1,0:T(8,128)(2,1)S(1)}, u32[]{:S(2)}, u32[]{:S(2)}) collective-permute-start(bf16[16,16,128]{2,1,0:T(8,128)(2,1)S(1)} %get-tuple-element.55), channel_id=1, source_target_pairs={{0,2},{1,3},{2,0},{3,1},{4,6},{5,7},{6,4},{7,5},{8,10},{9,11},{10,... | collective-permute-start | bytes 196616 | tf_op jit(solution)/shard_map/ppermute | solution.py:512
  13.0 5.2 %collective-permute-start.3 = (bf16[16,16,128]{2,1,0:T(8,128)(2,1)S(1)}, bf16[16,16,128]{2,1,0:T(8,128)(2,1)S(1)}, u32[]{:S(2)}, u32[]{:S(2)}) collective-permute-start(bf16[16,16,128]{2,1,0:T(8,128)(2,1)S(1)} %get-tuple-element.56), channel_id=1, source_target_pairs={{0,1},{1,0},{2,3},{3,2},{4,5},{5,4},{6,7},{7,6},{8,9},{9,8},{10,11... | collective-permute-start | bytes 196616 | tf_op jit(solution)/shard_map/ppermute | solution.py:512
  24.1 2.4 %collective-permute-start.6 = (bf16[208,128]{1,0:T(8,128)(2,1)S(1)}, bf16[208,128]{1,0:T(8,128)(2,1)S(1)}, u32[]{:S(2)}, u32[]{:S(2)}) collective-permute-start(bf16[208,128]{1,0:T(8,128)(2,1)S(1)} %get-tuple-element.58), channel_id=1, source_target_pairs={{0,1},{1,0},{2,3},{3,2},{4,5},{5,4},{6,7},{7,6},{8,9},{9,8},{10,11... | collective-permute-start | bytes 159752 | tf_op jit(solution)/shard_map/ppermute | solution.py:512
  24.7 3.8 %collective-permute-start.8 = (bf16[208,128]{1,0:T(8,128)(2,1)S(1)}, bf16[208,128]{1,0:T(8,128)(2,1)S(1)}, u32[]{:S(2)}, u32[]{:S(2)}) collective-permute-start(bf16[208,128]{1,0:T(8,128)(2,1)S(1)} %get-tuple-element.59), channel_id=1, source_target_pairs={{0,3},{1,2},{2,1},{3,0},{4,7},{5,6},{6,5},{7,4},{8,11},{9,10},{10,... | collective-permute-start | bytes 159752 | tf_op jit(solution)/shard_map/ppermute | solution.py:512
  26.2 4.2 %collective-permute-start.7 = (bf16[208,128]{1,0:T(8,128)(2,1)S(1)}, bf16[208,128]{1,0:T(8,128)(2,1)S(1)}, u32[]{:S(2)}, u32[]{:S(2)}) collective-permute-start(bf16[208,128]{1,0:T(8,128)(2,1)S(1)} %get-tuple-element.60), channel_id=1, source_target_pairs={{0,2},{1,3},{2,0},{3,1},{4,6},{5,7},{6,4},{7,5},{8,10},{9,11},{10,... | collective-permute-start | bytes 159752 | tf_op jit(solution)/shard_map/ppermute | solution.py:512
  30.4 5.8 %collective-permute-start.11 = (bf16[208,128]{1,0:T(8,128)(2,1)S(1)}, bf16[208,128]{1,0:T(8,128)(2,1)S(1)}, u32[]{:S(2)}, u32[]{:S(2)}) collective-permute-start(bf16[208,128]{1,0:T(8,128)(2,1)S(1)} %fusion.2), channel_id=1, source_target_pairs={{0,12},{4,8},{8,4},{12,0},{16,28},{20,24},{24,20},{28,16},{1,13},{... | collective-permute-start | bytes 159752 | tf_op jit(solution)/shard_map/ppermute | solution.py:512
  33.0 4.1 %collective-permute-start.10 = (bf16[208,128]{1,0:T(8,128)(2,1)S(1)}, bf16[208,128]{1,0:T(8,128)(2,1)S(1)}, u32[]{:S(2)}, u32[]{:S(2)}) collective-permute-start(bf16[208,128]{1,0:T(8,128)(2,1)S(1)} %fusion.2), channel_id=1, source_target_pairs={{0,8},{4,12},{8,0},{12,4},{16,24},{20,28},{24,16},{28,20},{1,9},{5... | collective-permute-start | bytes 159752 | tf_op jit(solution)/shard_map/ppermute | solution.py:512
  33.4 4.1 %collective-permute-start.9 = (bf16[208,128]{1,0:T(8,128)(2,1)S(1)}, bf16[208,128]{1,0:T(8,128)(2,1)S(1)}, u32[]{:S(2)}, u32[]{:S(2)}) collective-permute-start(bf16[208,128]{1,0:T(8,128)(2,1)S(1)} %fusion.2), channel_id=1, source_target_pairs={{0,4},{4,0},{8,12},{12,8},{16,20},{20,16},{24,28},{28,24},{1,5},{5... | collective-permute-start | bytes 159752 | tf_op jit(solution)/shard_map/ppermute | solution.py:512
  37.6 5.1 %collective-permute-start.12 = (bf16[208,128]{1,0:T(8,128)(2,1)S(1)}, bf16[208,128]{1,0:T(8,128)(2,1)S(1)}, u32[]{:S(2)}, u32[]{:S(2)}) collective-permute-start(bf16[208,128]{1,0:T(8,128)(2,1)S(1)} %add_convert_fusion.1), channel_id=1, source_target_pairs={{0,16},{4,20},{8,24},{12,28},{16,0},{20,4},{24,8},{28,12},{1,17},{... | collective-permute-start | bytes 159752 | tf_op jit(solution)/shard_map/ppermute | solution.py:512
  42.7 4.2 %collective-permute-start.15 = (bf16[208,128]{1,0:T(8,128)(2,1)S(1)}, bf16[208,128]{1,0:T(8,128)(2,1)S(1)}, u32[]{:S(2)}, u32[]{:S(2)}) collective-permute-start(bf16[208,128]{1,0:T(8,128)(2,1)S(1)} %add_convert_fusion.refs_0_), channel_id=1, source_target_pairs={{0,3},{1,2},{2,1},{3,0},{4,7},{5,6},{6,5},{7,4},{8,11},{9,10},{10,... | collective-permute-start | bytes 159752 | tf_op jit(solution)/shard_map/ppermute | solution.py:512
  42.8 5.2 %collective-permute-start.14 = (bf16[208,128]{1,0:T(8,128)(2,1)S(1)}, bf16[208,128]{1,0:T(8,128)(2,1)S(1)}, u32[]{:S(2)}, u32[]{:S(2)}) collective-permute-start(bf16[208,128]{1,0:T(8,128)(2,1)S(1)} %add_convert_fusion.refs_0_), channel_id=1, source_target_pairs={{0,2},{1,3},{2,0},{3,1},{4,6},{5,7},{6,4},{7,5},{8,10},{9,11},{10,... | collective-permute-start | bytes 159752 | tf_op jit(solution)/shard_map/ppermute | solution.py:512
  44.3 3.7 %collective-permute-start.13 = (bf16[208,128]{1,0:T(8,128)(2,1)S(1)}, bf16[208,128]{1,0:T(8,128)(2,1)S(1)}, u32[]{:S(2)}, u32[]{:S(2)}) collective-permute-start(bf16[208,128]{1,0:T(8,128)(2,1)S(1)} %add_convert_fusion.refs_0_), channel_id=1, source_target_pairs={{0,1},{1,0},{2,3},{3,2},{4,5},{5,4},{6,7},{7,6},{8,9},{9,8},{10,11... | collective-permute-start | bytes 159752 | tf_op jit(solution)/shard_map/ppermute | solution.py:512

commit v5 on v4

--- a/solution.py
+++ b/solution.py
@@ -348,7 +348,7 @@
     n_near = pl.multiple_of(group * 2 * rows, 2 * rows)
     n_far = pl.multiple_of((1 - group) * 2 * rows, 2 * rows)
 
-    @pl.loop(0, hidden, unroll=32)
+    @pl.loop(0, hidden, unroll=128)
     def _(h):
         at = pl.ds(pl.multiple_of(h * half, half), half)
         for near, far, sq in ((near_ls, far_ls, left_sq), (near_rs, far_rs, right_sq)):
@@ -400,6 +400,9 @@
     pgs,
     pr,
     dgl_own,
+    xn_own,
+    dy_own,
+    dpre_own,
     gacc,
 ):
     me = me_ref[0]
@@ -440,15 +443,15 @@
                 y = dot(woT[...], xn)
                 dgl = (pg * y * gate * (1.0 - gate)).astype(BF16)
                 dgl_own[t] = dgl
-                gacc[4] += dot_nt(zn, dgl)
-                gacc[5] += dot_nt(xn, dy)
-                gacc[6] += dxn * xhat
-                gacc[7] += dxn
+                xn_own[t] = xn
+                dy_own[t] = dy
+                gacc[0] += dxn * xhat
+                gacc[1] += dxn
             pr[which, pl.ds(t, hidden, stride=half), :] = norm_columns_backward(
                 dxn, vec[0], xhat, rstd
             )
 
-    @pl.loop(0, hidden, unroll=32)
+    @pl.loop(0, hidden, unroll=128)
     def _(h):
         at = pl.ds(pl.multiple_of(h * half, half), half)
         pr[0, at, :] = lanes(dot(halves(pr[0, at, :]), right_sq[h]))
@@ -464,15 +467,23 @@
             for b in (2 * which, 2 * which + 1):
                 cols = slice(b * hidden, (b + 1) * hidden)
                 dpre = (d * factors[t, cols, :]).astype(BF16)
-                gacc[b] += dot_nt(zn, dpre)
+                dpre_own[t, cols, :] = dpre
                 dzn += dot(we_ref[:, cols], dpre)
-        gacc[8] += dzn * zhat
-        gacc[9] += dzn
+        gacc[2] += dzn * zhat
+        gacc[3] += dzn
         dzn_ref[t] = dzn
 
-    for b in range(6):
-        grads_ref[b * LANES : (b + 1) * LANES, :] = gacc[b].astype(BF16)
-    sums = [jnp.sum(gacc[b].T, axis=0, keepdims=True) for b in (8, 9, 6, 7)]
+    wide = lambda ref, rows_: jnp.concatenate([ref[t, rows_, :] for t in range(half)], axis=1)
+    every = slice(0, LANES)
+    zn = wide(zn_own, every)
+    for b in range(4):
+        cols = slice(b * LANES, (b + 1) * LANES)
+        grads_ref[cols, :] = dot_nt(zn, wide(dpre_own, cols)).astype(BF16)
+    grads_ref[4 * LANES : 5 * LANES, :] = dot_nt(zn, wide(dgl_own, every)).astype(BF16)
+    grads_ref[5 * LANES : 6 * LANES, :] = dot_nt(
+        wide(xn_own, every), wide(dy_own, every)
+    ).astype(BF16)
+    sums = [jnp.sum(gacc[b].T, axis=0, keepdims=True) for b in (2, 3, 0, 1)]
     pad = grads_ref.shape[0] - 6 * LANES
     sums.append(jnp.zeros((pad - 4, LANES), F32))
     grads_ref[6 * LANES :, :] = jnp.concatenate(sums, axis=0).astype(BF16)
@@ -637,7 +648,10 @@
             vm((n_dap * rows * rows, width), F32),
             vm((2, hidden * half, LANES), F32),
             vm((half, width, LANES), BF16),
-            vm((10, LANES, LANES), F32),
+            vm((half, hidden, LANES), BF16),
+            vm((half, width, LANES), BF16),
+            vm((half, 4 * hidden, LANES), BF16),
+            vm((4, LANES, LANES), F32),
         ],
         prod,
         left_sq,

time: 49 us -> 46.7 us (0.953)
  Pallas kernels: 14.4 us -> 12.1 us
    pallas_call x5, Pallas kernels: 14.4 us -> 12.1 us  [call(): pl.pallas_call(kernel, out_shape=tuple(outs), in_specs=[pl.BlockSpec(memo...]
  transfers between devices with their start and end apart: 16 -> 16, of which waited for: 9 -> 9; matrix products, arithmetic and copies ran while one was open for 2% -> 2% of each run, Pallas kernels for 16% -> 15%
where the time goes in v5:
time: 46.7 us; the launch traced here: 46.5 us
  starting transfers between devices  15.8 us (34%)
  waiting for transfers between devices  12.8 us (27%)
  Pallas kernels  12.1 us (26%)
  local copies, waits for them, and re-layouts  4.83 us (10%)
  between operations  0.82 us (2%)
    ppermute x16, starting transfers between devices, swap(): return lax.ppermute(x, axis, [(i, i ^ bit) for i in range(n)])  15.8 us
    ppermute x16, waiting for transfers between devices, swap(): return lax.ppermute(x, axis, [(i, i ^ bit) for i in range(n)])  12.8 us
    pallas_call x5, Pallas kernels, call(): pl.pallas_call(kernel, out_shape=tuple(outs), in_specs=[pl.BlockSpec(memo...  12.1 us
    unnamed x20, local copies, waits for them, and re-layouts  3.84 us
    squeeze x1, local copies, waits for them, and re-layouts, per_device_fused(): lax.dynamic_index_in_dim(cut, me ^ s, 1, keepdims=False)  0.96 us
  transfers between devices with their start and end apart: 16, of which 9 were waited for; matrix products, arithmetic and copies ran while one was open for 2% of the time, Pallas kernels for 15%

profile of v5, /device:TPU:0, one launch (start us, length us, event | category | flops | bytes accessed | tf_op | source)
XLA Modules:
  0.0 46.5 jit_solution(9695919747601640206)
XLA Ops:
  0.6 0.5 %collective-permute-start.1 = (bf16[16,64,128]{2,1,0:T(8,128)(2,1)}, bf16[16,64,128]{2,1,0:T(8,128)(2,1)S(1)}, u32[]{:S(2)}, u32[]{:S(2)}) collective-permute-start(bf16[16,64,128]{2,1,0:T(8,128)(2,1)} %bitcast.37), channel_id=1, source_target_pairs={{0,1},{1,0},{2,3},{3,2},{4,5},{5,4},{6,7},{7,6},{8,9},{9,8},{10,11... | collective-permute-start | bytes 786440 | tf_op jit(solution)/shard_map/ppermute | solution.py:523
  1.1 2.6 %collective-permute-start = (bf16[16,64,128]{2,1,0:T(8,128)(2,1)}, bf16[16,64,128]{2,1,0:T(8,128)(2,1)S(1)}, u32[]{:S(2)}, u32[]{:S(2)}) collective-permute-start(bf16[16,64,128]{2,1,0:T(8,128)(2,1)} %bitcast.38), channel_id=1, source_target_pairs={{0,2},{1,3},{2,0},{3,1},{4,6},{5,7},{6,4},{7,5},{8,10},{9,11},{10,... | collective-permute-start | bytes 786440 | tf_op jit(solution)/shard_map/ppermute | solution.py:523
  3.7 1.0 %dynamic-slice_bitcast_fusion = (bf16[16,16,128]{2,1,0:T(8,128)(2,1)S(1)}, bf16[16,16,128]{2,1,0:T(8,128)(2,1)S(1)}, bf16[16,16,128]{2,1,0:T(8,128)(2,1)S(1)}, bf16[16,16,128]{2,1,0:T(8,128)(2,1)S(1)}) fusion(bf16[16,4,16,128]{3,2,1,0:T(8,128)(2,1)} %bitcast.35, s32[]{:T(128)S(6)} %select_n.21, s32[]{:T(128)S(6)} %select_n.20, s32[]{:T(128)S(6)} %select_n.19, ...), kind=kLoop, calls=%fused_computation.6 | loop fusion | bytes 524304 | tf_op jit(solution)/shard_map/jit(dynamic_index_in_dim)/squeeze | solution.py:582
  4.7 0.0 collective-permute-done.1.near_ref
  4.7 0.0 copy-start.1
  4.7 0.9 %copy-done.1 = bf16[128,512]{1,0:T(8,128)(2,1)S(1)} copy-done((bf16[128,512]{1,0:T(8,128)(2,1)S(1)}, bf16[128,512]{1,0:T(8,128)(2,1)}, u32[]{:S(2)}) %copy-start.1) | copy-done | bytes 131096
  5.6 0.9 %copy-done.2 = bf16[1,16,64,128]{3,2,1,0:T(8,128)(2,1)S(1)} copy-done((bf16[1,16,64,128]{3,2,1,0:T(8,128)(2,1)S(1)}, bf16[1,16,64,128]{3,2,1,0:T(8,128)(2,1)}, u32[]{:S(2)}) %copy-start.2) | copy-done | bytes 262168
  6.6 0.7 %copy-done.5 = s32[1,64]{1,0:T(1,128)S(1)} copy-done((s32[1,64]{1,0:T(1,128)S(1)}, s32[1,64]{1,0:T(1,128)}, u32[]{:S(2)}) %copy-start.5) | copy-done | bytes 280
  7.2 0.7 %copy-done.6 = f32[128]{0:T(128)S(1)} copy-done((f32[128]{0:T(128)S(1)}, f32[128]{0:T(128)}, u32[]{:S(2)}) %copy-start.6) | copy-done | bytes 536
  7.9 0.7 %copy-done.7 = f32[128]{0:T(128)S(1)} copy-done((f32[128]{0:T(128)S(1)}, f32[128]{0:T(128)}, u32[]{:S(2)}) %copy-start.7) | copy-done | bytes 536
  8.5 1.6 %shard_map.145 = (bf16[512,128]{1,0:T(8,128)(2,1)S(1)}, f32[2,1024,128]{2,1,0:T(8,128)S(1)}, f32[2,1024,128]{2,1,0:T(8,128)S(1)}, f32[8,512,128]{2,1,0:T(8,128)S...) custom-call(s32[1]{0:T(128)} %bitcast.me_ref, ...), custom_call_target="tpu_custom_call" | custom-call | bytes 14400000 | tf_op jit(solution)/shard_map/pallas_call | solution.py:565
  10.2 0.0 copy-start
  10.2 0.0 copy-start.3
  10.2 0.0 copy-start.4
  10.2 0.0 copy-start.8
  10.2 0.0 copy-start.9
  10.2 0.6 %collective-permute-done.pair2 = bf16[16,64,128]{2,1,0:T(8,128)(2,1)S(1)} collective-permute-done((bf16[16,64,128]{2,1,0:T(8,128)(2,1)}, bf16[16,64,128]{2,1,0:T(8,128)(2,1)S(1)}, u32[]{:S(2)}, u32[]{:S(2)}) %collective-permute-start) | collective-permute-done | bytes 262176 | tf_op jit(solution)/shard_map/ppermute | solution.py:523
  10.9 0.0 collective-permute-start.2
  10.9 1.9 %collective-permute-start.5 = (bf16[16,16,128]{2,1,0:T(8,128)(2,1)S(1)}, bf16[16,16,128]{2,1,0:T(8,128)(2,1)S(1)}, u32[]{:S(2)}, u32[]{:S(2)}) collective-permute-start(bf16[16,16,128]{2,1,0:T(8,128)(2,1)S(1)} %get-tuple-element.54), channel_id=1, source_target_pairs={{0,3},{1,2},{2,1},{3,0},{4,7},{5,6},{6,5},{7,4},{8,11},{9,10},{10,... | collective-permute-start | bytes 196616 | tf_op jit(solution)/shard_map/ppermute | solution.py:523
  12.7 0.3 collective-permute-start.4
  13.0 0.0 collective-permute-start.3
  13.0 0.0 collective-permute-done.2.pair3
  13.0 4.3 %shard_map.146 = (f32[2,1024,128]{2,1,0:T(8,128)S(1)}, bf16[128,64,64]{2,1,0:T(8,128)(2,1)S(1)}, bf16[128,64,64]{2,1,0:T(8,128)(2,1)S(1)}, bf16[8,128,128]{2,1,0:T(8,128)(2,1)S(1)}) custom-call(s32[1]{0:T(128)} %bitcast.me_ref, bf16[16,64,128]{2,1,0:T(8,128)(2,1)S(1)} %collective-permute-done.pair2, bf16[16,64,128]{2,1,0:T(8,128)(2,1)S(1)} %collective-permute-done.2.pair3, ...), custom_call_target="tpu_custom_call" | custom-call | bytes 28800000 | tf_op jit(solution)/shard_map/pallas_call | solution.py:565
  17.3 0.0 collective-permute-done.5.pg3
  17.3 0.0 collective-permute-done.4.pg2
  17.3 0.0 collective-permute-done.3.pg1
  17.4 4.4 %shard_map.147 = (f32[8,128,128]{2,1,0:T(8,128)S(1)}, bf16[832,128]{1,0:T(8,128)(2,1)S(1)}) custom-call(s32[1]{0:T(128)} %bitcast.me_ref, f32[2,1024,128]{2,1,0:T(8,128)S(1)} %get-tuple-element.38.prod, bf16[128,64,64]{2,1,0:T(8,128)(2,1)S(1)} %get-tuple-element.39.left_sq, bf16[128,64,64]{2,1,0:T(8,128)(2,1)S(1)} %get-tuple-element.40.right_sq, ...), custom_call_target="tpu_custom_call" | custom-call | bytes 28800000 | tf_op jit(solution)/shard_map/pallas_call | solution.py:565
  21.8 0.6 %collective-permute-start.6 = (bf16[208,128]{1,0:T(8,128)(2,1)S(1)}, bf16[208,128]{1,0:T(8,128)(2,1)S(1)}, u32[]{:S(2)}, u32[]{:S(2)}) collective-permute-start(bf16[208,128]{1,0:T(8,128)(2,1)S(1)} %get-tuple-element.58), channel_id=1, source_target_pairs={{0,1},{1,0},{2,3},{3,2},{4,5},{5,4},{6,7},{7,6},{8,9},{9,8},{10,11... | collective-permute-start | bytes 159752 | tf_op jit(solution)/shard_map/ppermute | solution.py:523
  22.4 1.5 %collective-permute-start.8 = (bf16[208,128]{1,0:T(8,128)(2,1)S(1)}, bf16[208,128]{1,0:T(8,128)(2,1)S(1)}, u32[]{:S(2)}, u32[]{:S(2)}) collective-permute-start(bf16[208,128]{1,0:T(8,128)(2,1)S(1)} %get-tuple-element.59), channel_id=1, source_target_pairs={{0,3},{1,2},{2,1},{3,0},{4,7},{5,6},{6,5},{7,4},{8,11},{9,10},{10,... | collective-permute-start | bytes 159752 | tf_op jit(solution)/shard_map/ppermute | solution.py:523
  23.9 0.3 collective-permute-start.7
  24.2 2.0 %collective-permute-done.8 = bf16[208,128]{1,0:T(8,128)(2,1)S(1)} collective-permute-done((bf16[208,128]{1,0:T(8,128)(2,1)S(1)}, bf16[208,128]{1,0:T(8,128)(2,1)S(1)}, u32[]{:S(2)}, u32[]{:S(2)}) %collective-permute-start.8) | collective-permute-done | bytes 53280 | tf_op jit(solution)/shard_map/ppermute | solution.py:523
  26.2 1.9 %collective-permute-done.7 = bf16[208,128]{1,0:T(8,128)(2,1)S(1)} collective-permute-done((bf16[208,128]{1,0:T(8,128)(2,1)S(1)}, bf16[208,128]{1,0:T(8,128)(2,1)S(1)}, u32[]{:S(2)}, u32[]{:S(2)}) %collective-permute-start.7) | collective-permute-done | bytes 53280 | tf_op jit(solution)/shard_map/ppermute | solution.py:523
  28.1 2.6 %collective-permute-start.11 = (bf16[208,128]{1,0:T(8,128)(2,1)S(1)}, bf16[208,128]{1,0:T(8,128)(2,1)S(1)}, u32[]{:S(2)}, u32[]{:S(2)}) collective-permute-start(bf16[208,128]{1,0:T(8,128)(2,1)S(1)} %fusion.2), channel_id=1, source_target_pairs={{0,12},{4,8},{8,4},{12,0},{16,28},{20,24},{24,20},{28,16},{1,13},{... | collective-permute-start | bytes 159752 | tf_op jit(solution)/shard_map/ppermute | solution.py:523
  30.7 0.4 collective-permute-start.10
  31.1 0.5 %collective-permute-start.9 = (bf16[208,128]{1,0:T(8,128)(2,1)S(1)}, bf16[208,128]{1,0:T(8,128)(2,1)S(1)}, u32[]{:S(2)}, u32[]{:S(2)}) collective-permute-start(bf16[208,128]{1,0:T(8,128)(2,1)S(1)} %fusion.2), channel_id=1, source_target_pairs={{0,4},{4,0},{8,12},{12,8},{16,20},{20,16},{24,28},{28,24},{1,5},{5... | collective-permute-start | bytes 159752 | tf_op jit(solution)/shard_map/ppermute | solution.py:523
  31.7 2.2 %collective-permute-done.11 = bf16[208,128]{1,0:T(8,128)(2,1)S(1)} collective-permute-done((bf16[208,128]{1,0:T(8,128)(2,1)S(1)}, bf16[208,128]{1,0:T(8,128)(2,1)S(1)}, u32[]{:S(2)}, u32[]{:S(2)}) %collective-permute-start.11) | collective-permute-done | bytes 53280 | tf_op jit(solution)/shard_map/ppermute | solution.py:523
  33.9 1.0 %collective-permute-done.10 = bf16[208,128]{1,0:T(8,128)(2,1)S(1)} collective-permute-done((bf16[208,128]{1,0:T(8,128)(2,1)S(1)}, bf16[208,128]{1,0:T(8,128)(2,1)S(1)}, u32[]{:S(2)}, u32[]{:S(2)}) %collective-permute-start.10) | collective-permute-done | bytes 53280 | tf_op jit(solution)/shard_map/ppermute | solution.py:523
  34.8 0.4 collective-permute-done.9
  35.3 2.6 %collective-permute-start.12 = (bf16[208,128]{1,0:T(8,128)(2,1)S(1)}, bf16[208,128]{1,0:T(8,128)(2,1)S(1)}, u32[]{:S(2)}, u32[]{:S(2)}) collective-permute-start(bf16[208,128]{1,0:T(8,128)(2,1)S(1)} %add_convert_fusion.1), channel_id=1, source_target_pairs={{0,16},{4,20},{8,24},{12,28},{16,0},{20,4},{24,8},{28,12},{1,17},{... | collective-permute-start | bytes 159752 | tf_op jit(solution)/shard_map/ppermute | solution.py:523
  38.0 2.5 %collective-permute-done.12 = bf16[208,128]{1,0:T(8,128)(2,1)S(1)} collective-permute-done((bf16[208,128]{1,0:T(8,128)(2,1)S(1)}, bf16[208,128]{1,0:T(8,128)(2,1)S(1)}, u32[]{:S(2)}, u32[]{:S(2)}) %collective-permute-start.12) | collective-permute-done | bytes 53280 | tf_op jit(solution)/shard_map/ppermute | solution.py:523
  40.4 0.1 collective-permute-start.15
  40.5 1.5 %collective-permute-start.14 = (bf16[208,128]{1,0:T(8,128)(2,1)S(1)}, bf16[208,128]{1,0:T(8,128)(2,1)S(1)}, u32[]{:S(2)}, u32[]{:S(2)}) collective-permute-start(bf16[208,128]{1,0:T(8,128)(2,1)S(1)} %add_convert_fusion.refs_0_), channel_id=1, source_target_pairs={{0,2},{1,3},{2,0},{3,1},{4,6},{5,7},{6,4},{7,5},{8,10},{9,11},{10,... | collective-permute-start | bytes 159752 | tf_op jit(solution)/shard_map/ppermute | solution.py:523
  42.0 0.4 collective-permute-start.13
  42.4 1.0 %shard_map.148 = bf16[16,64,128]{2,1,0:T(8,128)(2,1)} custom-call(s32[1]{0:T(128)} %bitcast.me_ref, f32[8,128,128]{2,1,0:T(8,128)S(1)} %get-tuple-element.46.dzn_ref, f32[8,128,128]{2,1,0:T(8,128)S(1)} %get-tuple-element.44.zhat_own, f32[8,1,128]{2,1,0:T(1,128)S(1)} %get-tuple-element.47.rstd_own, f32[2,128,128]{2,1,0:T(8,128)S(1)} %get-tuple-element.35.vec), custom_call_target="tpu_custom_call" | custom-call | bytes 3600000 | tf_op jit(solution)/shard_map/pallas_call | solution.py:565
  43.3 1.3 %collective-permute-done.15.refs_3_ = bf16[208,128]{1,0:T(8,128)(2,1)S(1)} collective-permute-done((bf16[208,128]{1,0:T(8,128)(2,1)S(1)}, bf16[208,128]{1,0:T(8,128)(2,1)S(1)}, u32[]{:S(2)}, u32[]{:S(2)}) %collective-permute-start.15) | collective-permute-done | bytes 53280 | tf_op jit(solution)/shard_map/ppermute | solution.py:523
  44.6 1.1 %collective-permute-done.14.refs_2_ = bf16[208,128]{1,0:T(8,128)(2,1)S(1)} collective-permute-done((bf16[208,128]{1,0:T(8,128)(2,1)S(1)}, bf16[208,128]{1,0:T(8,128)(2,1)S(1)}, u32[]{:S(2)}, u32[]{:S(2)}) %collective-permute-start.14) | collective-permute-done | bytes 53280 | tf_op jit(solution)/shard_map/ppermute | solution.py:523
  45.7 0.0 collective-permute-done.13.refs_1_
  45.7 0.8 %shard_map.149 = (f32[128,512]{1,0:T(8,128)}, f32[128,128]{1,0:T(8,128)}, f32[128,128]{1,0:T(8,128)}, f32[2,128]{1,0:T(2,128)}, f32[2,128]{1,0:T(2,128)}) custom-call(s32[1]{0:T(128)} %bitcast.me_ref, bf16[208,128]{1,0:T(8,128)(2,1)S(1)} %add_convert_fusion.refs_0_, bf16[208,128]{1,0:T(8,128)(2,1)S(1)} %collective-permute-done.13.refs_1_, ...), custom_call_target="tpu_custom_call" | custom-call | bytes 3600000 | tf_op jit(solution)/shard_map/pallas_call | solution.py:565
  (14 shorter events, 0.1 us)
Async XLA Ops:
  0.6 4.1 %collective-permute-start.1 = (bf16[16,64,128]{2,1,0:T(8,128)(2,1)}, bf16[16,64,128]{2,1,0:T(8,128)(2,1)S(1)}, u32[]{:S(2)}, u32[]{:S(2)}) collective-permute-start(bf16[16,64,128]{2,1,0:T(8,128)(2,1)} %bitcast.37), channel_id=1, source_target_pairs={{0,1},{1,0},{2,3},{3,2},{4,5},{5,4},{6,7},{7,6},{8,9},{9,8},{10,11... | collective-permute-start | bytes 786440 | tf_op jit(solution)/shard_map/ppermute | solution.py:523
  1.1 9.7 %collective-permute-start = (bf16[16,64,128]{2,1,0:T(8,128)(2,1)}, bf16[16,64,128]{2,1,0:T(8,128)(2,1)S(1)}, u32[]{:S(2)}, u32[]{:S(2)}) collective-permute-start(bf16[16,64,128]{2,1,0:T(8,128)(2,1)} %bitcast.38), channel_id=1, source_target_pairs={{0,2},{1,3},{2,0},{3,1},{4,6},{5,7},{6,4},{7,5},{8,10},{9,11},{10,... | collective-permute-start | bytes 786440 | tf_op jit(solution)/shard_map/ppermute | solution.py:523
  4.7 0.9 %copy-start.1 = (bf16[128,512]{1,0:T(8,128)(2,1)S(1)}, bf16[128,512]{1,0:T(8,128)(2,1)}, u32[]{:S(2)}) copy-start(bf16[128,512]{1,0:T(8,128)(2,1)} %we_ref.1) | copy-start | bytes 393220
  5.6 0.9 %copy-start.2 = (bf16[1,16,64,128]{3,2,1,0:T(8,128)(2,1)S(1)}, bf16[1,16,64,128]{3,2,1,0:T(8,128)(2,1)}, u32[]{:S(2)}) copy-start(bf16[1,16,64,128]{3,2,1,0:T(8,128)(2,1)} %param.10) | copy-start | bytes 786436
  6.6 0.7 %copy-start.5 = (s32[1,64]{1,0:T(1,128)S(1)}, s32[1,64]{1,0:T(1,128)}, u32[]{:S(2)}) copy-start(s32[1,64]{1,0:T(1,128)} %mask_hbm.1) | copy-start | bytes 772
  7.2 0.7 %copy-start.6 = (f32[128]{0:T(128)S(1)}, f32[128]{0:T(128)}, u32[]{:S(2)}) copy-start(f32[128]{0:T(128)} %param.16) | copy-start | bytes 1540
  7.9 0.7 %copy-start.7 = (f32[128]{0:T(128)S(1)}, f32[128]{0:T(128)}, u32[]{:S(2)}) copy-start(f32[128]{0:T(128)} %param.17) | copy-start | bytes 1540
  10.2 7.1 %copy-start = (bf16[1,16,64,128]{3,2,1,0:T(8,128)(2,1)S(1)}, bf16[1,16,64,128]{3,2,1,0:T(8,128)(2,1)}, u32[]{:S(2)}) copy-start(bf16[1,16,64,128]{3,2,1,0:T(8,128)(2,1)} %param.11) | copy-start | bytes 786436
  10.2 7.1 %copy-start.3 = (bf16[128,128]{1,0:T(8,128)(2,1)S(1)}, bf16[128,128]{1,0:T(8,128)(2,1)}, u32[]{:S(2)}) copy-start(bf16[128,128]{1,0:T(8,128)(2,1)} %wg_ref.1) | copy-start | bytes 98308
  10.2 7.1 %copy-start.4 = (bf16[128,128]{1,0:T(8,128)(2,1)S(1)}, bf16[128,128]{1,0:T(8,128)(2,1)}, u32[]{:S(2)}) copy-start(bf16[128,128]{1,0:T(8,128)(2,1)} %wo_ref.1) | copy-start | bytes 98308
  10.2 7.1 %copy-start.8 = (f32[128]{0:T(128)S(1)}, f32[128]{0:T(128)}, u32[]{:S(2)}) copy-start(f32[128]{0:T(128)} %param.18) | copy-start | bytes 1540
  10.2 7.1 %copy-start.9 = (f32[128]{0:T(128)S(1)}, f32[128]{0:T(128)}, u32[]{:S(2)}) copy-start(f32[128]{0:T(128)} %param.19) | copy-start | bytes 1540
  10.9 2.1 %collective-permute-start.2 = (bf16[16,64,128]{2,1,0:T(8,128)(2,1)S(1)}, bf16[16,64,128]{2,1,0:T(8,128)(2,1)S(1)}, u32[]{:S(2)}, u32[]{:S(2)}) collective-permute-start(bf16[16,64,128]{2,1,0:T(8,128)(2,1)S(1)} %collective-permute-done.pair2), channel_id=1, source_target_pairs={{0,1},{1,0},{2,3},{3,2},{4,5},{5,4},{6,7},{7,6},{8,9},{9,8},{10,11... | collective-permute-start | bytes 786440 | tf_op jit(solution)/shard_map/ppermute | solution.py:523
  10.9 6.4 %collective-permute-start.5 = (bf16[16,16,128]{2,1,0:T(8,128)(2,1)S(1)}, bf16[16,16,128]{2,1,0:T(8,128)(2,1)S(1)}, u32[]{:S(2)}, u32[]{:S(2)}) collective-permute-start(bf16[16,16,128]{2,1,0:T(8,128)(2,1)S(1)} %get-tuple-element.54), channel_id=1, source_target_pairs={{0,3},{1,2},{2,1},{3,0},{4,7},{5,6},{6,5},{7,4},{8,11},{9,10},{10,... | collective-permute-start | bytes 196616 | tf_op jit(solution)/shard_map/ppermute | solution.py:523
  12.7 4.6 %collective-permute-start.4 = (bf16[16,16,128]{2,1,0:T(8,128)(2,1)S(1)}, bf16[16,16,128]{2,1,0:T(8,128)(2,1)S(1)}, u32[]{:S(2)}, u32[]{:S(2)}) collective-permute-start(bf16[16,16,128]{2,1,0:T(8,128)(2,1)S(1)} %get-tuple-element.55), channel_id=1, source_target_pairs={{0,2},{1,3},{2,0},{3,1},{4,6},{5,7},{6,4},{7,5},{8,10},{9,11},{10,... | collective-permute-start | bytes 196616 | tf_op jit(solution)/shard_map/ppermute | solution.py:523
  13.0 4.3 %collective-permute-start.3 = (bf16[16,16,128]{2,1,0:T(8,128)(2,1)S(1)}, bf16[16,16,128]{2,1,0:T(8,128)(2,1)S(1)}, u32[]{:S(2)}, u32[]{:S(2)}) collective-permute-start(bf16[16,16,128]{2,1,0:T(8,128)(2,1)S(1)} %get-tuple-element.56), channel_id=1, source_target_pairs={{0,1},{1,0},{2,3},{3,2},{4,5},{5,4},{6,7},{7,6},{8,9},{9,8},{10,11... | collective-permute-start | bytes 196616 | tf_op jit(solution)/shard_map/ppermute | solution.py:523
  21.8 2.4 %collective-permute-start.6 = (bf16[208,128]{1,0:T(8,128)(2,1)S(1)}, bf16[208,128]{1,0:T(8,128)(2,1)S(1)}, u32[]{:S(2)}, u32[]{:S(2)}) collective-permute-start(bf16[208,128]{1,0:T(8,128)(2,1)S(1)} %get-tuple-element.58), channel_id=1, source_target_pairs={{0,1},{1,0},{2,3},{3,2},{4,5},{5,4},{6,7},{7,6},{8,9},{9,8},{10,11... | collective-permute-start | bytes 159752 | tf_op jit(solution)/shard_map/ppermute | solution.py:523
  22.4 3.8 %collective-permute-start.8 = (bf16[208,128]{1,0:T(8,128)(2,1)S(1)}, bf16[208,128]{1,0:T(8,128)(2,1)S(1)}, u32[]{:S(2)}, u32[]{:S(2)}) collective-permute-start(bf16[208,128]{1,0:T(8,128)(2,1)S(1)} %get-tuple-element.59), channel_id=1, source_target_pairs={{0,3},{1,2},{2,1},{3,0},{4,7},{5,6},{6,5},{7,4},{8,11},{9,10},{10,... | collective-permute-start | bytes 159752 | tf_op jit(solution)/shard_map/ppermute | solution.py:523
  23.9 4.2 %collective-permute-start.7 = (bf16[208,128]{1,0:T(8,128)(2,1)S(1)}, bf16[208,128]{1,0:T(8,128)(2,1)S(1)}, u32[]{:S(2)}, u32[]{:S(2)}) collective-permute-start(bf16[208,128]{1,0:T(8,128)(2,1)S(1)} %get-tuple-element.60), channel_id=1, source_target_pairs={{0,2},{1,3},{2,0},{3,1},{4,6},{5,7},{6,4},{7,5},{8,10},{9,11},{10,... | collective-permute-start | bytes 159752 | tf_op jit(solution)/shard_map/ppermute | solution.py:523
  28.1 5.8 %collective-permute-start.11 = (bf16[208,128]{1,0:T(8,128)(2,1)S(1)}, bf16[208,128]{1,0:T(8,128)(2,1)S(1)}, u32[]{:S(2)}, u32[]{:S(2)}) collective-permute-start(bf16[208,128]{1,0:T(8,128)(2,1)S(1)} %fusion.2), channel_id=1, source_target_pairs={{0,12},{4,8},{8,4},{12,0},{16,28},{20,24},{24,20},{28,16},{1,13},{... | collective-permute-start | bytes 159752 | tf_op jit(solution)/shard_map/ppermute | solution.py:523
  30.7 4.1 %collective-permute-start.10 = (bf16[208,128]{1,0:T(8,128)(2,1)S(1)}, bf16[208,128]{1,0:T(8,128)(2,1)S(1)}, u32[]{:S(2)}, u32[]{:S(2)}) collective-permute-start(bf16[208,128]{1,0:T(8,128)(2,1)S(1)} %fusion.2), channel_id=1, source_target_pairs={{0,8},{4,12},{8,0},{12,4},{16,24},{20,28},{24,16},{28,20},{1,9},{5... | collective-permute-start | bytes 159752 | tf_op jit(solution)/shard_map/ppermute | solution.py:523
  31.1 4.1 %collective-permute-start.9 = (bf16[208,128]{1,0:T(8,128)(2,1)S(1)}, bf16[208,128]{1,0:T(8,128)(2,1)S(1)}, u32[]{:S(2)}, u32[]{:S(2)}) collective-permute-start(bf16[208,128]{1,0:T(8,128)(2,1)S(1)} %fusion.2), channel_id=1, source_target_pairs={{0,4},{4,0},{8,12},{12,8},{16,20},{20,16},{24,28},{28,24},{1,5},{5... | collective-permute-start | bytes 159752 | tf_op jit(solution)/shard_map/ppermute | solution.py:523
  35.3 5.1 %collective-permute-start.12 = (bf16[208,128]{1,0:T(8,128)(2,1)S(1)}, bf16[208,128]{1,0:T(8,128)(2,1)S(1)}, u32[]{:S(2)}, u32[]{:S(2)}) collective-permute-start(bf16[208,128]{1,0:T(8,128)(2,1)S(1)} %add_convert_fusion.1), channel_id=1, source_target_pairs={{0,16},{4,20},{8,24},{12,28},{16,0},{20,4},{24,8},{28,12},{1,17},{... | collective-permute-start | bytes 159752 | tf_op jit(solution)/shard_map/ppermute | solution.py:523
  40.4 4.2 %collective-permute-start.15 = (bf16[208,128]{1,0:T(8,128)(2,1)S(1)}, bf16[208,128]{1,0:T(8,128)(2,1)S(1)}, u32[]{:S(2)}, u32[]{:S(2)}) collective-permute-start(bf16[208,128]{1,0:T(8,128)(2,1)S(1)} %add_convert_fusion.refs_0_), channel_id=1, source_target_pairs={{0,3},{1,2},{2,1},{3,0},{4,7},{5,6},{6,5},{7,4},{8,11},{9,10},{10,... | collective-permute-start | bytes 159752 | tf_op jit(solution)/shard_map/ppermute | solution.py:523
  40.5 5.2 %collective-permute-start.14 = (bf16[208,128]{1,0:T(8,128)(2,1)S(1)}, bf16[208,128]{1,0:T(8,128)(2,1)S(1)}, u32[]{:S(2)}, u32[]{:S(2)}) collective-permute-start(bf16[208,128]{1,0:T(8,128)(2,1)S(1)} %add_convert_fusion.refs_0_), channel_id=1, source_target_pairs={{0,2},{1,3},{2,0},{3,1},{4,6},{5,7},{6,4},{7,5},{8,10},{9,11},{10,... | collective-permute-start | bytes 159752 | tf_op jit(solution)/shard_map/ppermute | solution.py:523
  42.0 3.7 %collective-permute-start.13 = (bf16[208,128]{1,0:T(8,128)(2,1)S(1)}, bf16[208,128]{1,0:T(8,128)(2,1)S(1)}, u32[]{:S(2)}, u32[]{:S(2)}) collective-permute-start(bf16[208,128]{1,0:T(8,128)(2,1)S(1)} %add_convert_fusion.refs_0_), channel_id=1, source_target_pairs={{0,1},{1,0},{2,3},{3,2},{4,5},{5,4},{6,7},{7,6},{8,9},{9,8},{10,11... | collective-permute-start | bytes 159752 | tf_op jit(solution)/shard_map/ppermute | solution.py:523

commit v6 on v5

--- a/solution.py
+++ b/solution.py
@@ -612,7 +612,7 @@
         row(in_bias),
         in_hbm=5,
     )
-    far, zn_own, pg_own = lax.optimization_barrier((far, zn_own, pg_own))
+    far, zn_own, pg_own, pgs[0] = lax.optimization_barrier((far, zn_own, pg_own, pgs[0]))
     across = swap(far, "dap", n_dap, 1)
     prod, left_sq, right_sq, zn_cols = call(
         product_kernel,
@@ -682,7 +682,7 @@
 
     chunks = grads.reshape(n_dap, -1, LANES)
     total = pick(chunks, me).astype(F32)
-    got = [swap(pick(chunks, me ^ s), "dap", n_dap, s) for s in range(1, n_dap)]
+    got = [swap(pick(chunks, me ^ s), "dap", n_dap, s) for s in range(n_dap - 1, 0, -1)]
     for c in got:
         total = total + c.astype(F32)
     total = total.astype(BF16)
@@ -696,7 +696,8 @@
         while len(terms) > 1:
             terms = [p + q for p, q in zip(terms[::2], terms[1::2])]
         total = terms[0].astype(BF16)
-    parts = [total] + [swap(total, "dap", n_dap, s) for s in range(1, n_dap)]
+    parts = {s: swap(total, "dap", n_dap, s) for s in range(n_dap - 1, 0, -1)}
+    parts = [total] + [parts[s] for s in range(1, n_dap)]
     edges, gate, outs, in_norm, out_norm = call(
         functools.partial(finish_kernel, n_dap),
         1,

time: 46.7 us -> 46.1 us (0.987)
  waiting for transfers between devices: 12.8 us -> 12.3 us
    ppermute x16, waiting for transfers between devices: 12.8 us -> 12.3 us  [swap(): return lax.ppermute(x, axis, [(i, i ^ bit) for i in range(n)])]
where the time goes in v6:
time: 46.1 us; the launch traced here: 45.9 us
  starting transfers between devices  15.8 us (34%)
  waiting for transfers between devices  12.3 us (27%)
  Pallas kernels  12.1 us (26%)
  local copies, waits for them, and re-layouts  4.83 us (10%)
  between operations  0.81 us (2%)
    ppermute x16, starting transfers between devices, swap(): return lax.ppermute(x, axis, [(i, i ^ bit) for i in range(n)])  15.8 us
    ppermute x16, waiting for transfers between devices, swap(): return lax.ppermute(x, axis, [(i, i ^ bit) for i in range(n)])  12.3 us
    pallas_call x5, Pallas kernels, call(): pl.pallas_call(kernel, out_shape=tuple(outs), in_specs=[pl.BlockSpec(memo...  12.1 us
    unnamed x20, local copies, waits for them, and re-layouts  3.85 us
    squeeze x1, local copies, waits for them, and re-layouts, per_device_fused(): lax.dynamic_index_in_dim(cut, me ^ s, 1, keepdims=False)  0.96 us
  transfers between devices with their start and end apart: 16, of which 9 were waited for; matrix products, arithmetic and copies ran while one was open for 2% of the time, Pallas kernels for 15%

profile of v6, /device:TPU:0, one launch (start us, length us, event | category | flops | bytes accessed | tf_op | source)
XLA Modules:
  0.0 45.9 jit_solution(621420816416028028)
XLA Ops:
  0.6 0.5 %collective-permute-start.1 = (bf16[16,64,128]{2,1,0:T(8,128)(2,1)}, bf16[16,64,128]{2,1,0:T(8,128)(2,1)S(1)}, u32[]{:S(2)}, u32[]{:S(2)}) collective-permute-start(bf16[16,64,128]{2,1,0:T(8,128)(2,1)} %bitcast.37), channel_id=1, source_target_pairs={{0,1},{1,0},{2,3},{3,2},{4,5},{5,4},{6,7},{7,6},{8,9},{9,8},{10,11... | collective-permute-start | bytes 786440 | tf_op jit(solution)/shard_map/ppermute | solution.py:523
  1.1 2.6 %collective-permute-start = (bf16[16,64,128]{2,1,0:T(8,128)(2,1)}, bf16[16,64,128]{2,1,0:T(8,128)(2,1)S(1)}, u32[]{:S(2)}, u32[]{:S(2)}) collective-permute-start(bf16[16,64,128]{2,1,0:T(8,128)(2,1)} %bitcast.38), channel_id=1, source_target_pairs={{0,2},{1,3},{2,0},{3,1},{4,6},{5,7},{6,4},{7,5},{8,10},{9,11},{10,... | collective-permute-start | bytes 786440 | tf_op jit(solution)/shard_map/ppermute | solution.py:523
  3.7 1.0 %dynamic-slice_bitcast_fusion = (bf16[16,16,128]{2,1,0:T(8,128)(2,1)S(1)}, bf16[16,16,128]{2,1,0:T(8,128)(2,1)S(1)}, bf16[16,16,128]{2,1,0:T(8,128)(2,1)S(1)}, bf16[16,16,128]{2,1,0:T(8,128)(2,1)S(1)}) fusion(bf16[16,4,16,128]{3,2,1,0:T(8,128)(2,1)} %bitcast.35, s32[]{:T(128)S(6)} %select_n.21, s32[]{:T(128)S(6)} %select_n.20, s32[]{:T(128)S(6)} %select_n.19, ...), kind=kLoop, calls=%fused_computation.6 | loop fusion | bytes 524304 | tf_op jit(solution)/shard_map/jit(dynamic_index_in_dim)/squeeze | solution.py:582
  4.7 0.2 collective-permute-start.2
  4.9 0.0 collective-permute-done.1.near_ref
  4.9 0.9 %copy-done.1 = bf16[128,512]{1,0:T(8,128)(2,1)S(1)} copy-done((bf16[128,512]{1,0:T(8,128)(2,1)S(1)}, bf16[128,512]{1,0:T(8,128)(2,1)}, u32[]{:S(2)}) %copy-start.1) | copy-done | bytes 131096
  5.8 0.9 %copy-done.2 = bf16[1,16,64,128]{3,2,1,0:T(8,128)(2,1)S(1)} copy-done((bf16[1,16,64,128]{3,2,1,0:T(8,128)(2,1)S(1)}, bf16[1,16,64,128]{3,2,1,0:T(8,128)(2,1)}, u32[]{:S(2)}) %copy-start.2) | copy-done | bytes 262168
  6.8 0.7 %copy-done.5 = s32[1,64]{1,0:T(1,128)S(1)} copy-done((s32[1,64]{1,0:T(1,128)S(1)}, s32[1,64]{1,0:T(1,128)}, u32[]{:S(2)}) %copy-start.5) | copy-done | bytes 280
  7.5 0.7 %copy-done.6 = f32[128]{0:T(128)S(1)} copy-done((f32[128]{0:T(128)S(1)}, f32[128]{0:T(128)}, u32[]{:S(2)}) %copy-start.6) | copy-done | bytes 536
  8.1 0.7 %copy-done.7 = f32[128]{0:T(128)S(1)} copy-done((f32[128]{0:T(128)S(1)}, f32[128]{0:T(128)}, u32[]{:S(2)}) %copy-start.7) | copy-done | bytes 536
  8.8 1.6 %shard_map.145 = (bf16[512,128]{1,0:T(8,128)(2,1)S(1)}, f32[2,1024,128]{2,1,0:T(8,128)S(1)}, f32[2,1024,128]{2,1,0:T(8,128)S(1)}, f32[8,512,128]{2,1,0:T(8,128)S...) custom-call(s32[1]{0:T(128)} %bitcast.me_ref, ...), custom_call_target="tpu_custom_call" | custom-call | bytes 14400000 | tf_op jit(solution)/shard_map/pallas_call | solution.py:565
  10.4 0.0 copy-start
  10.4 0.0 copy-start.3
  10.4 0.0 copy-start.4
  10.4 0.0 copy-start.8
  10.4 0.0 copy-start.9
  10.5 0.0 collective-permute-done.2.pg1
  10.5 0.4 collective-permute-done.pair2
  10.9 0.1 collective-permute-start.3
  10.9 1.8 %collective-permute-start.5 = (bf16[16,16,128]{2,1,0:T(8,128)(2,1)S(1)}, bf16[16,16,128]{2,1,0:T(8,128)(2,1)S(1)}, u32[]{:S(2)}, u32[]{:S(2)}) collective-permute-start(bf16[16,16,128]{2,1,0:T(8,128)(2,1)S(1)} %get-tuple-element.56), channel_id=1, source_target_pairs={{0,3},{1,2},{2,1},{3,0},{4,7},{5,6},{6,5},{7,4},{8,11},{9,10},{10,... | collective-permute-start | bytes 196616 | tf_op jit(solution)/shard_map/ppermute | solution.py:523
  12.7 0.3 collective-permute-start.4
  13.0 0.0 collective-permute-done.3.pair3
  13.0 4.3 %shard_map.146 = (f32[2,1024,128]{2,1,0:T(8,128)S(1)}, bf16[128,64,64]{2,1,0:T(8,128)(2,1)S(1)}, bf16[128,64,64]{2,1,0:T(8,128)(2,1)S(1)}, bf16[8,128,128]{2,1,0:T(8,128)(2,1)S(1)}) custom-call(s32[1]{0:T(128)} %bitcast.me_ref, bf16[16,64,128]{2,1,0:T(8,128)(2,1)S(1)} %collective-permute-done.pair2, bf16[16,64,128]{2,1,0:T(8,128)(2,1)S(1)} %collective-permute-done.3.pair3, ...), custom_call_target="tpu_custom_call" | custom-call | bytes 28800000 | tf_op jit(solution)/shard_map/pallas_call | solution.py:565
  17.3 0.0 collective-permute-done.5.pg3
  17.3 0.0 collective-permute-done.4.pg2
  17.4 4.4 %shard_map.147 = (f32[8,128,128]{2,1,0:T(8,128)S(1)}, bf16[832,128]{1,0:T(8,128)(2,1)S(1)}) custom-call(s32[1]{0:T(128)} %bitcast.me_ref, f32[2,1024,128]{2,1,0:T(8,128)S(1)} %get-tuple-element.39.prod, bf16[128,64,64]{2,1,0:T(8,128)(2,1)S(1)} %get-tuple-element.40.left_sq, bf16[128,64,64]{2,1,0:T(8,128)(2,1)S(1)} %get-tuple-element.41.right_sq, ...), custom_call_target="tpu_custom_call" | custom-call | bytes 28800000 | tf_op jit(solution)/shard_map/pallas_call | solution.py:565
  21.8 1.2 %collective-permute-start.6 = (bf16[208,128]{1,0:T(8,128)(2,1)S(1)}, bf16[208,128]{1,0:T(8,128)(2,1)S(1)}, u32[]{:S(2)}, u32[]{:S(2)}) collective-permute-start(bf16[208,128]{1,0:T(8,128)(2,1)S(1)} %get-tuple-element.60), channel_id=1, source_target_pairs={{0,3},{1,2},{2,1},{3,0},{4,7},{5,6},{6,5},{7,4},{8,11},{9,10},{10,... | collective-permute-start | bytes 159752 | tf_op jit(solution)/shard_map/ppermute | solution.py:523
  23.0 0.8 %collective-permute-start.8 = (bf16[208,128]{1,0:T(8,128)(2,1)S(1)}, bf16[208,128]{1,0:T(8,128)(2,1)S(1)}, u32[]{:S(2)}, u32[]{:S(2)}) collective-permute-start(bf16[208,128]{1,0:T(8,128)(2,1)S(1)} %get-tuple-element.61), channel_id=1, source_target_pairs={{0,1},{1,0},{2,3},{3,2},{4,5},{5,4},{6,7},{7,6},{8,9},{9,8},{10,11... | collective-permute-start | bytes 159752 | tf_op jit(solution)/shard_map/ppermute | solution.py:523
  23.8 0.2 collective-permute-start.7
  24.0 1.7 %collective-permute-done.6 = bf16[208,128]{1,0:T(8,128)(2,1)S(1)} collective-permute-done((bf16[208,128]{1,0:T(8,128)(2,1)S(1)}, bf16[208,128]{1,0:T(8,128)(2,1)S(1)}, u32[]{:S(2)}, u32[]{:S(2)}) %collective-permute-start.6) | collective-permute-done | bytes 53280 | tf_op jit(solution)/shard_map/ppermute | solution.py:523
  25.7 0.0 collective-permute-done.8
  25.7 2.3 %collective-permute-done.7 = bf16[208,128]{1,0:T(8,128)(2,1)S(1)} collective-permute-done((bf16[208,128]{1,0:T(8,128)(2,1)S(1)}, bf16[208,128]{1,0:T(8,128)(2,1)S(1)}, u32[]{:S(2)}, u32[]{:S(2)}) %collective-permute-start.7) | collective-permute-done | bytes 53280 | tf_op jit(solution)/shard_map/ppermute | solution.py:523
  28.0 2.6 %collective-permute-start.11 = (bf16[208,128]{1,0:T(8,128)(2,1)S(1)}, bf16[208,128]{1,0:T(8,128)(2,1)S(1)}, u32[]{:S(2)}, u32[]{:S(2)}) collective-permute-start(bf16[208,128]{1,0:T(8,128)(2,1)S(1)} %fusion.2), channel_id=1, source_target_pairs={{0,12},{4,8},{8,4},{12,0},{16,28},{20,24},{24,20},{28,16},{1,13},{... | collective-permute-start | bytes 159752 | tf_op jit(solution)/shard_map/ppermute | solution.py:523
  30.5 0.5 collective-permute-start.10
  31.0 0.5 %collective-permute-start.9 = (bf16[208,128]{1,0:T(8,128)(2,1)S(1)}, bf16[208,128]{1,0:T(8,128)(2,1)S(1)}, u32[]{:S(2)}, u32[]{:S(2)}) collective-permute-start(bf16[208,128]{1,0:T(8,128)(2,1)S(1)} %fusion.2), channel_id=1, source_target_pairs={{0,4},{4,0},{8,12},{12,8},{16,20},{20,16},{24,28},{28,24},{1,5},{5... | collective-permute-start | bytes 159752 | tf_op jit(solution)/shard_map/ppermute | solution.py:523
  31.5 1.5 %collective-permute-done.11 = bf16[208,128]{1,0:T(8,128)(2,1)S(1)} collective-permute-done((bf16[208,128]{1,0:T(8,128)(2,1)S(1)}, bf16[208,128]{1,0:T(8,128)(2,1)S(1)}, u32[]{:S(2)}, u32[]{:S(2)}) %collective-permute-start.11) | collective-permute-done | bytes 53280 | tf_op jit(solution)/shard_map/ppermute | solution.py:523
  33.1 1.6 %collective-permute-done.10 = bf16[208,128]{1,0:T(8,128)(2,1)S(1)} collective-permute-done((bf16[208,128]{1,0:T(8,128)(2,1)S(1)}, bf16[208,128]{1,0:T(8,128)(2,1)S(1)}, u32[]{:S(2)}, u32[]{:S(2)}) %collective-permute-start.10) | collective-permute-done | bytes 53280 | tf_op jit(solution)/shard_map/ppermute | solution.py:523
  34.7 0.5 collective-permute-done.9
  35.2 2.7 %collective-permute-start.12 = (bf16[208,128]{1,0:T(8,128)(2,1)S(1)}, bf16[208,128]{1,0:T(8,128)(2,1)S(1)}, u32[]{:S(2)}, u32[]{:S(2)}) collective-permute-start(bf16[208,128]{1,0:T(8,128)(2,1)S(1)} %add_convert_fusion.1), channel_id=1, source_target_pairs={{0,16},{4,20},{8,24},{12,28},{16,0},{20,4},{24,8},{28,12},{1,17},{... | collective-permute-start | bytes 159752 | tf_op jit(solution)/shard_map/ppermute | solution.py:523
  37.8 2.4 %collective-permute-done.12 = bf16[208,128]{1,0:T(8,128)(2,1)S(1)} collective-permute-done((bf16[208,128]{1,0:T(8,128)(2,1)S(1)}, bf16[208,128]{1,0:T(8,128)(2,1)S(1)}, u32[]{:S(2)}, u32[]{:S(2)}) %collective-permute-start.12) | collective-permute-done | bytes 53280 | tf_op jit(solution)/shard_map/ppermute | solution.py:523
  40.3 0.1 collective-permute-start.15
  40.4 1.0 %collective-permute-start.14 = (bf16[208,128]{1,0:T(8,128)(2,1)S(1)}, bf16[208,128]{1,0:T(8,128)(2,1)S(1)}, u32[]{:S(2)}, u32[]{:S(2)}) collective-permute-start(bf16[208,128]{1,0:T(8,128)(2,1)S(1)} %add_convert_fusion.refs_0_), channel_id=1, source_target_pairs={{0,2},{1,3},{2,0},{3,1},{4,6},{5,7},{6,4},{7,5},{8,10},{9,11},{10,... | collective-permute-start | bytes 159752 | tf_op jit(solution)/shard_map/ppermute | solution.py:523
  41.3 0.9 %collective-permute-start.13 = (bf16[208,128]{1,0:T(8,128)(2,1)S(1)}, bf16[208,128]{1,0:T(8,128)(2,1)S(1)}, u32[]{:S(2)}, u32[]{:S(2)}) collective-permute-start(bf16[208,128]{1,0:T(8,128)(2,1)S(1)} %add_convert_fusion.refs_0_), channel_id=1, source_target_pairs={{0,1},{1,0},{2,3},{3,2},{4,5},{5,4},{6,7},{7,6},{8,9},{9,8},{10,11... | collective-permute-start | bytes 159752 | tf_op jit(solution)/shard_map/ppermute | solution.py:523
  42.2 1.0 %shard_map.148 = bf16[16,64,128]{2,1,0:T(8,128)(2,1)} custom-call(s32[1]{0:T(128)} %bitcast.me_ref, f32[8,128,128]{2,1,0:T(8,128)S(1)} %get-tuple-element.48.dzn_ref, f32[8,128,128]{2,1,0:T(8,128)S(1)} %get-tuple-element.45.zhat_own, f32[8,1,128]{2,1,0:T(1,128)S(1)} %get-tuple-element.49.rstd_own, f32[2,128,128]{2,1,0:T(8,128)S(1)} %get-tuple-element.36.vec), custom_call_target="tpu_custom_call" | custom-call | bytes 3600000 | tf_op jit(solution)/shard_map/pallas_call | solution.py:565
  43.2 0.8 %collective-permute-done.15.refs_3_ = bf16[208,128]{1,0:T(8,128)(2,1)S(1)} collective-permute-done((bf16[208,128]{1,0:T(8,128)(2,1)S(1)}, bf16[208,128]{1,0:T(8,128)(2,1)S(1)}, u32[]{:S(2)}, u32[]{:S(2)}) %collective-permute-start.15) | collective-permute-done | bytes 53280 | tf_op jit(solution)/shard_map/ppermute | solution.py:523
  44.0 1.2 %collective-permute-done.14.refs_2_ = bf16[208,128]{1,0:T(8,128)(2,1)S(1)} collective-permute-done((bf16[208,128]{1,0:T(8,128)(2,1)S(1)}, bf16[208,128]{1,0:T(8,128)(2,1)S(1)}, u32[]{:S(2)}, u32[]{:S(2)}) %collective-permute-start.14) | collective-permute-done | bytes 53280 | tf_op jit(solution)/shard_map/ppermute | solution.py:523
  45.1 0.0 collective-permute-done.13.refs_1_
  45.1 0.8 %shard_map.149 = (f32[128,512]{1,0:T(8,128)}, f32[128,128]{1,0:T(8,128)}, f32[128,128]{1,0:T(8,128)}, f32[2,128]{1,0:T(2,128)}, f32[2,128]{1,0:T(2,128)}) custom-call(s32[1]{0:T(128)} %bitcast.me_ref, bf16[208,128]{1,0:T(8,128)(2,1)S(1)} %add_convert_fusion.refs_0_, bf16[208,128]{1,0:T(8,128)(2,1)S(1)} %collective-permute-done.13.refs_1_, ...), custom_call_target="tpu_custom_call" | custom-call | bytes 3600000 | tf_op jit(solution)/shard_map/pallas_call | solution.py:565
  (14 shorter events, 0.1 us)
Async XLA Ops:
  0.6 4.3 %collective-permute-start.1 = (bf16[16,64,128]{2,1,0:T(8,128)(2,1)}, bf16[16,64,128]{2,1,0:T(8,128)(2,1)S(1)}, u32[]{:S(2)}, u32[]{:S(2)}) collective-permute-start(bf16[16,64,128]{2,1,0:T(8,128)(2,1)} %bitcast.37), channel_id=1, source_target_pairs={{0,1},{1,0},{2,3},{3,2},{4,5},{5,4},{6,7},{7,6},{8,9},{9,8},{10,11... | collective-permute-start | bytes 786440 | tf_op jit(solution)/shard_map/ppermute | solution.py:523
  1.1 9.7 %collective-permute-start = (bf16[16,64,128]{2,1,0:T(8,128)(2,1)}, bf16[16,64,128]{2,1,0:T(8,128)(2,1)S(1)}, u32[]{:S(2)}, u32[]{:S(2)}) collective-permute-start(bf16[16,64,128]{2,1,0:T(8,128)(2,1)} %bitcast.38), channel_id=1, source_target_pairs={{0,2},{1,3},{2,0},{3,1},{4,6},{5,7},{6,4},{7,5},{8,10},{9,11},{10,... | collective-permute-start | bytes 786440 | tf_op jit(solution)/shard_map/ppermute | solution.py:523
  4.7 5.8 %collective-permute-start.2 = (bf16[16,16,128]{2,1,0:T(8,128)(2,1)S(1)}, bf16[16,16,128]{2,1,0:T(8,128)(2,1)S(1)}, u32[]{:S(2)}, u32[]{:S(2)}) collective-permute-start(bf16[16,16,128]{2,1,0:T(8,128)(2,1)S(1)} %get-tuple-element.58), channel_id=1, source_target_pairs={{0,1},{1,0},{2,3},{3,2},{4,5},{5,4},{6,7},{7,6},{8,9},{9,8},{10,11... | collective-permute-start | bytes 196616 | tf_op jit(solution)/shard_map/ppermute | solution.py:523
  4.9 0.9 %copy-start.1 = (bf16[128,512]{1,0:T(8,128)(2,1)S(1)}, bf16[128,512]{1,0:T(8,128)(2,1)}, u32[]{:S(2)}) copy-start(bf16[128,512]{1,0:T(8,128)(2,1)} %we_ref.1) | copy-start | bytes 393220
  5.8 0.9 %copy-start.2 = (bf16[1,16,64,128]{3,2,1,0:T(8,128)(2,1)S(1)}, bf16[1,16,64,128]{3,2,1,0:T(8,128)(2,1)}, u32[]{:S(2)}) copy-start(bf16[1,16,64,128]{3,2,1,0:T(8,128)(2,1)} %param.10) | copy-start | bytes 786436
  6.8 0.7 %copy-start.5 = (s32[1,64]{1,0:T(1,128)S(1)}, s32[1,64]{1,0:T(1,128)}, u32[]{:S(2)}) copy-start(s32[1,64]{1,0:T(1,128)} %mask_hbm.1) | copy-start | bytes 772
  7.5 0.7 %copy-start.6 = (f32[128]{0:T(128)S(1)}, f32[128]{0:T(128)}, u32[]{:S(2)}) copy-start(f32[128]{0:T(128)} %param.16) | copy-start | bytes 1540
  8.1 0.7 %copy-start.7 = (f32[128]{0:T(128)S(1)}, f32[128]{0:T(128)}, u32[]{:S(2)}) copy-start(f32[128]{0:T(128)} %param.17) | copy-start | bytes 1540
  10.4 6.9 %copy-start = (bf16[1,16,64,128]{3,2,1,0:T(8,128)(2,1)S(1)}, bf16[1,16,64,128]{3,2,1,0:T(8,128)(2,1)}, u32[]{:S(2)}) copy-start(bf16[1,16,64,128]{3,2,1,0:T(8,128)(2,1)} %param.11) | copy-start | bytes 786436
  10.4 6.9 %copy-start.3 = (bf16[128,128]{1,0:T(8,128)(2,1)S(1)}, bf16[128,128]{1,0:T(8,128)(2,1)}, u32[]{:S(2)}) copy-start(bf16[128,128]{1,0:T(8,128)(2,1)} %wg_ref.1) | copy-start | bytes 98308
  10.4 6.9 %copy-start.4 = (bf16[128,128]{1,0:T(8,128)(2,1)S(1)}, bf16[128,128]{1,0:T(8,128)(2,1)}, u32[]{:S(2)}) copy-start(bf16[128,128]{1,0:T(8,128)(2,1)} %wo_ref.1) | copy-start | bytes 98308
  10.4 6.9 %copy-start.8 = (f32[128]{0:T(128)S(1)}, f32[128]{0:T(128)}, u32[]{:S(2)}) copy-start(f32[128]{0:T(128)} %param.18) | copy-start | bytes 1540
  10.4 6.9 %copy-start.9 = (f32[128]{0:T(128)S(1)}, f32[128]{0:T(128)}, u32[]{:S(2)}) copy-start(f32[128]{0:T(128)} %param.19) | copy-start | bytes 1540
  10.9 2.1 %collective-permute-start.3 = (bf16[16,64,128]{2,1,0:T(8,128)(2,1)S(1)}, bf16[16,64,128]{2,1,0:T(8,128)(2,1)S(1)}, u32[]{:S(2)}, u32[]{:S(2)}) collective-permute-start(bf16[16,64,128]{2,1,0:T(8,128)(2,1)S(1)} %collective-permute-done.pair2), channel_id=1, source_target_pairs={{0,1},{1,0},{2,3},{3,2},{4,5},{5,4},{6,7},{7,6},{8,9},{9,8},{10,11... | collective-permute-start | bytes 786440 | tf_op jit(solution)/shard_map/ppermute | solution.py:523
  10.9 6.4 %collective-permute-start.5 = (bf16[16,16,128]{2,1,0:T(8,128)(2,1)S(1)}, bf16[16,16,128]{2,1,0:T(8,128)(2,1)S(1)}, u32[]{:S(2)}, u32[]{:S(2)}) collective-permute-start(bf16[16,16,128]{2,1,0:T(8,128)(2,1)S(1)} %get-tuple-element.56), channel_id=1, source_target_pairs={{0,3},{1,2},{2,1},{3,0},{4,7},{5,6},{6,5},{7,4},{8,11},{9,10},{10,... | collective-permute-start | bytes 196616 | tf_op jit(solution)/shard_map/ppermute | solution.py:523
  12.7 4.6 %collective-permute-start.4 = (bf16[16,16,128]{2,1,0:T(8,128)(2,1)S(1)}, bf16[16,16,128]{2,1,0:T(8,128)(2,1)S(1)}, u32[]{:S(2)}, u32[]{:S(2)}) collective-permute-start(bf16[16,16,128]{2,1,0:T(8,128)(2,1)S(1)} %get-tuple-element.57), channel_id=1, source_target_pairs={{0,2},{1,3},{2,0},{3,1},{4,6},{5,7},{6,4},{7,5},{8,10},{9,11},{10,... | collective-permute-start | bytes 196616 | tf_op jit(solution)/shard_map/ppermute | solution.py:523
  21.8 3.9 %collective-permute-start.6 = (bf16[208,128]{1,0:T(8,128)(2,1)S(1)}, bf16[208,128]{1,0:T(8,128)(2,1)S(1)}, u32[]{:S(2)}, u32[]{:S(2)}) collective-permute-start(bf16[208,128]{1,0:T(8,128)(2,1)S(1)} %get-tuple-element.60), channel_id=1, source_target_pairs={{0,3},{1,2},{2,1},{3,0},{4,7},{5,6},{6,5},{7,4},{8,11},{9,10},{10,... | collective-permute-start | bytes 159752 | tf_op jit(solution)/shard_map/ppermute | solution.py:523
  23.0 2.6 %collective-permute-start.8 = (bf16[208,128]{1,0:T(8,128)(2,1)S(1)}, bf16[208,128]{1,0:T(8,128)(2,1)S(1)}, u32[]{:S(2)}, u32[]{:S(2)}) collective-permute-start(bf16[208,128]{1,0:T(8,128)(2,1)S(1)} %get-tuple-element.61), channel_id=1, source_target_pairs={{0,1},{1,0},{2,3},{3,2},{4,5},{5,4},{6,7},{7,6},{8,9},{9,8},{10,11... | collective-permute-start | bytes 159752 | tf_op jit(solution)/shard_map/ppermute | solution.py:523
  23.8 4.1 %collective-permute-start.7 = (bf16[208,128]{1,0:T(8,128)(2,1)S(1)}, bf16[208,128]{1,0:T(8,128)(2,1)S(1)}, u32[]{:S(2)}, u32[]{:S(2)}) collective-permute-start(bf16[208,128]{1,0:T(8,128)(2,1)S(1)} %get-tuple-element.62), channel_id=1, source_target_pairs={{0,2},{1,3},{2,0},{3,1},{4,6},{5,7},{6,4},{7,5},{8,10},{9,11},{10,... | collective-permute-start | bytes 159752 | tf_op jit(solution)/shard_map/ppermute | solution.py:523
  28.0 5.1 %collective-permute-start.11 = (bf16[208,128]{1,0:T(8,128)(2,1)S(1)}, bf16[208,128]{1,0:T(8,128)(2,1)S(1)}, u32[]{:S(2)}, u32[]{:S(2)}) collective-permute-start(bf16[208,128]{1,0:T(8,128)(2,1)S(1)} %fusion.2), channel_id=1, source_target_pairs={{0,12},{4,8},{8,4},{12,0},{16,28},{20,24},{24,20},{28,16},{1,13},{... | collective-permute-start | bytes 159752 | tf_op jit(solution)/shard_map/ppermute | solution.py:523
  30.5 4.1 %collective-permute-start.10 = (bf16[208,128]{1,0:T(8,128)(2,1)S(1)}, bf16[208,128]{1,0:T(8,128)(2,1)S(1)}, u32[]{:S(2)}, u32[]{:S(2)}) collective-permute-start(bf16[208,128]{1,0:T(8,128)(2,1)S(1)} %fusion.2), channel_id=1, source_target_pairs={{0,8},{4,12},{8,0},{12,4},{16,24},{20,28},{24,16},{28,20},{1,9},{5... | collective-permute-start | bytes 159752 | tf_op jit(solution)/shard_map/ppermute | solution.py:523
  31.0 4.1 %collective-permute-start.9 = (bf16[208,128]{1,0:T(8,128)(2,1)S(1)}, bf16[208,128]{1,0:T(8,128)(2,1)S(1)}, u32[]{:S(2)}, u32[]{:S(2)}) collective-permute-start(bf16[208,128]{1,0:T(8,128)(2,1)S(1)} %fusion.2), channel_id=1, source_target_pairs={{0,4},{4,0},{8,12},{12,8},{16,20},{20,16},{24,28},{28,24},{1,5},{5... | collective-permute-start | bytes 159752 | tf_op jit(solution)/shard_map/ppermute | solution.py:523
  35.2 5.1 %collective-permute-start.12 = (bf16[208,128]{1,0:T(8,128)(2,1)S(1)}, bf16[208,128]{1,0:T(8,128)(2,1)S(1)}, u32[]{:S(2)}, u32[]{:S(2)}) collective-permute-start(bf16[208,128]{1,0:T(8,128)(2,1)S(1)} %add_convert_fusion.1), channel_id=1, source_target_pairs={{0,16},{4,20},{8,24},{12,28},{16,0},{20,4},{24,8},{28,12},{1,17},{... | collective-permute-start | bytes 159752 | tf_op jit(solution)/shard_map/ppermute | solution.py:523
  40.3 3.7 %collective-permute-start.15 = (bf16[208,128]{1,0:T(8,128)(2,1)S(1)}, bf16[208,128]{1,0:T(8,128)(2,1)S(1)}, u32[]{:S(2)}, u32[]{:S(2)}) collective-permute-start(bf16[208,128]{1,0:T(8,128)(2,1)S(1)} %add_convert_fusion.refs_0_), channel_id=1, source_target_pairs={{0,3},{1,2},{2,1},{3,0},{4,7},{5,6},{6,5},{7,4},{8,11},{9,10},{10,... | collective-permute-start | bytes 159752 | tf_op jit(solution)/shard_map/ppermute | solution.py:523
  40.4 4.8 %collective-permute-start.14 = (bf16[208,128]{1,0:T(8,128)(2,1)S(1)}, bf16[208,128]{1,0:T(8,128)(2,1)S(1)}, u32[]{:S(2)}, u32[]{:S(2)}) collective-permute-start(bf16[208,128]{1,0:T(8,128)(2,1)S(1)} %add_convert_fusion.refs_0_), channel_id=1, source_target_pairs={{0,2},{1,3},{2,0},{3,1},{4,6},{5,7},{6,4},{7,5},{8,10},{9,11},{10,... | collective-permute-start | bytes 159752 | tf_op jit(solution)/shard_map/ppermute | solution.py:523
  41.3 3.8 %collective-permute-start.13 = (bf16[208,128]{1,0:T(8,128)(2,1)S(1)}, bf16[208,128]{1,0:T(8,128)(2,1)S(1)}, u32[]{:S(2)}, u32[]{:S(2)}) collective-permute-start(bf16[208,128]{1,0:T(8,128)(2,1)S(1)} %add_convert_fusion.refs_0_), channel_id=1, source_target_pairs={{0,1},{1,0},{2,3},{3,2},{4,5},{5,4},{6,7},{7,6},{8,9},{9,8},{10,11... | collective-permute-start | bytes 159752 | tf_op jit(solution)/shard_map/ppermute | solution.py:523
